TPU v7x, 32 devices: a whole 2x2x4 slice. The times are simulated.
32 devices in a mesh: dp: 8 (over y, x, core), expert: 4 (over z).
Axes of the slice: x: 2, y: 2, z: 4, core: 2. Of those that a mesh axis runs over, the one named last changes fastest.
Arguments:
- tokens: bfloat16 [2048, 2048], P('expert', 'dp'), may hold values from -6 to 6
- routes: int32 [2048, 2], P('expert'), may hold values from 0 to 3, all different within a row; in each aligned block of 512 rows (0 to 511, 512 to 1023, ...) at most 384 rows name the same one
- scores: int32 [2048, 2], P('expert'), may hold values from 1 to 1023
- gate_weight: bfloat16 [4, 2048, 8192], P('expert', None, 'dp'), may hold values from -0.125 to 0.125
- up_weight: bfloat16 [4, 2048, 8192], P('expert', None, 'dp'), may hold values from -0.125 to 0.125
- down_weight: bfloat16 [4, 8192, 2048], P('expert', 'dp'), may hold values from -0.0625 to 0.0625
Outputs:
- layer_out: bfloat16 [2048, 2048], P('expert', 'dp')
Inputs may be any that keep to these rules, and one draw needn't show every extreme that they name: `routes`: each row names 2 different experts. Within each aligned block of 512 rows no expert is named by more than 384 rows, and in every draw some expert is named by exactly 384 rows of a block.
All inputs are finite; a program needn't handle non-finite values.
Results may differ from a plain program's by a relative error of at most 0.025.
Values may be sent and summed in bfloat16 or wider, within the bound.
No kernel may reach another device: no remote copies, remote signals or barrier semaphores. Data moves between devices by JAX's collectives and lax.ppermute only.
A program may use at most 64 MiB of HBM per device.

v0:
```python
import jax
import jax.numpy as jnp
from jax import lax
from jax.sharding import PartitionSpec as P


def shards(tokens, routes, scores, gate_weight, up_weight, down_weight):
    expert_count = lax.axis_size("expert")
    row_count = tokens.shape[0]
    local_cols = tokens.shape[1]
    capacity = 3 * row_count // expert_count
    slot_count = expert_count * capacity
    expert_ids = jnp.arange(expert_count, dtype=jnp.int32)
    onehot = (routes[:, :, None] == expert_ids[None, None, :]).astype(jnp.int32)
    named = jnp.sum(onehot, axis=1)
    earlier = jnp.cumsum(named, axis=0) - named
    slot_rank = jnp.sum(onehot * earlier[:, None, :], axis=2)
    target = routes * capacity + slot_rank
    slot_ids = jnp.arange(slot_count, dtype=jnp.int32)
    placement = jnp.any(target[None, :, :] == slot_ids[:, None, None], axis=2).astype(jnp.bfloat16)
    weight = scores.astype(jnp.float32)
    weight = weight / jnp.sum(weight, axis=1, keepdims=True)
    gate_mat = gate_weight[0]
    up_mat = up_weight[0]
    down_mat = down_weight[0]
    outgoing = jnp.dot(placement, tokens, preferred_element_type=jnp.float32).astype(jnp.bfloat16)
    arrived = lax.all_to_all(
        outgoing.reshape(expert_count, capacity, local_cols),
        "expert",
        split_axis=0,
        concat_axis=0,
        tiled=True,
    )
    arrived = arrived.reshape(slot_count, local_cols)
    piece = lax.all_gather(arrived, "dp", axis=1, tiled=True)
    gate = jnp.dot(piece, gate_mat, preferred_element_type=jnp.float32)
    upval = jnp.dot(piece, up_mat, preferred_element_type=jnp.float32)
    hidden = (jax.nn.silu(gate) * upval).astype(jnp.bfloat16)
    summed = lax.psum_scatter(
        lax.dot_general(
            down_mat, hidden, (((0,), (1,)), ((), ())), preferred_element_type=jnp.float32
        ).astype(jnp.bfloat16),
        "dp",
        scatter_dimension=0,
        tiled=True,
    ).astype(jnp.float32)
    returned = lax.all_to_all(
        summed.reshape(local_cols, expert_count, capacity).astype(jnp.bfloat16),
        "expert",
        split_axis=1,
        concat_axis=1,
        tiled=True,
    ).astype(jnp.float32)
    returned = returned.reshape(local_cols, slot_count)
    first_part = jnp.take(returned, target[:, 0], axis=1)
    second_part = jnp.take(returned, target[:, 1], axis=1)
    combined = (first_part * weight[:, 0][None, :] + second_part * weight[:, 1][None, :]).T
    return combined.astype(jnp.bfloat16)


def solution(mesh):
    return jax.shard_map(
        shards,
        mesh=mesh,
        in_specs=(
            P("expert", "dp"),
            P("expert", None),
            P("expert", None),
            P("expert", None, "dp"),
            P("expert", None, "dp"),
            P("expert", "dp", None),
        ),
        out_specs=P("expert", "dp"),
        check_vma=False,
    )
```

profile of v0, /device:TPU:0, one launch (start us, length us, event | category | flops | bytes accessed | tf_op | source)
XLA Modules:
  0.0 215.4 jit_solution(12873606224567190590)
XLA Ops:
  6.5 0.7 convert_reduce_fusion
  7.3 1.2 reduce-window.6
  8.5 0.2 slice_reduce_fusion
  8.7 0.2 reduce-window.9
  8.9 0.1 add_bitcast_fusion
  9.0 0.7 select_reduce_fusion
  9.7 0.7 multiply_add_fusion
  10.4 2.0 fusion.1
  12.4 0.6 convolution_convert_fusion.1
  13.0 26.3 %all_to_all.10 = bf16[4,384,256]{2,1,0:T(8,128)(2,1)} all-to-all(bf16[4,384,256]{2,1,0:T(8,128)(2,1)S(1)} %bitcast.57), channel_id=1, replica_groups=mesh['dp'=8,'expert'=4] {'expert'}, dimensions={0} | all-to-all | bytes 1572864 | tf_op jit(solution)/shard_map/all_to_all | solution.py:27
  39.3 0.0 all-gather.2.cloned.1.call-update
  39.4 0.0 reduce-scatter.2.cloned.1.call-start
  39.4 45.9 %all-gather.2.cloned.1.call-done = bf16[1536,2048]{1,0:T(8,128)(2,1)} async-done(((bf16[1536,256]{1,0:T(8,128)(2,1)}), bf16[1536,2048]{1,0:T(8,128)(2,1)}) %all-gather.2.cloned.1.call-update) | async-done | bytes 6291472 | tf_op jit(solution)/shard_map/all_gather | solution.py:35
  85.3 11.6 %fusion.6 = f32[1536,1024]{1,0:T(8,128)} fusion(bf16[1536,2048]{1,0:T(8,128)(2,1)} %all-gather.2.cloned.1.call-done, bf16[1,2048,1024]{2,1,0:T(8,128)(2,1)} %param.11), kind=kOutput, calls=%fused_computation.9 | convolution fusion | flops 6442450944 | bytes 16777216 | tf_op jit(solution)/shard_map/dot_general | solution.py:36
  96.9 20.5 %fusion = bf16[2048,1536]{0,1:T(8,128)(2,1)} fusion(bf16[1,1024,2048]{2,1,0:T(8,128)(2,1)} %param.13, f32[1536,1024]{1,0:T(8,128)} %fusion.6, bf16[1536,2048]{1,0:T(8,128)(2,1)} %all-gather.2.cloned.1.call-done, bf16[1,2048,1024]{2,1,0:T(8,128)(2,1)} %param.12), kind=kOutput, calls=%fused_computation.3 | convolution fusion | flops 12897484800 | bytes 27262976 | tf_op jit(solution)/shard_map/dot_general | solution.py:40
  117.5 0.0 reduce-scatter.2.cloned.1.call-update
  117.5 61.9 %reduce-scatter.2.cloned.1.call-done = bf16[256,1536]{0,1:T(8,128)(2,1)} async-done(((bf16[2048,1536]{0,1:T(8,128)(2,1)}), bf16[256,1536]{0,1:T(8,128)(2,1)}) %reduce-scatter.2.cloned.1.call-update) | async-done | bytes 786448 | tf_op jit(solution)/shard_map/reduce_scatter | solution.py:39
  179.4 4.6 %all-to-all-start.1 = ((bf16[256,4,384]{0,2,1:T(8,128)(2,1)}), bf16[256,4,384]{0,2,1:T(8,128)(2,1)S(1)}, u32[]{:S(2)}, u32[]{:S(2)}) async-start(bf16[256,4,384]{0,2,1:T(8,128)(2,1)} %bitcast.56), calls=%async_computation.2 | async-start | bytes 1572864 | tf_op jit(solution)/shard_map/all_to_all | solution.py:47
  184.0 0.0 copy-done.1
  184.1 20.0 %all-to-all-done.1 = bf16[256,4,384]{0,2,1:T(8,128)(2,1)S(1)} async-done(((bf16[256,4,384]{0,2,1:T(8,128)(2,1)}), bf16[256,4,384]{0,2,1:T(8,128)(2,1)S(1)}, u32[]{:S(2)}, u32[]{:S(2)}) %all-to-all-start.1) | async-done | bytes 786464 | tf_op jit(solution)/shard_map/all_to_all | solution.py:47
  204.1 0.2 bitcast_convert_fusion
  204.3 1.6 gather_fusion
  205.9 1.6 gather_fusion.1
  207.5 1.1 fusion.11
  (15 shorter events, 0.1 us)
Async XLA Ops:
  6.5 5.9 %copy-start = (bf16[512,256]{1,0:T(8,128)(2,1)S(1)}, bf16[512,256]{1,0:T(8,128)(2,1)}, u32[]{:S(2)}) copy-start(bf16[512,256]{1,0:T(8,128)(2,1)} %param.8) | copy-start | bytes 786436
  6.5 78.8 %all-gather.2.cloned.1.call-start = ((), (), s32[]{:S(2)}) async-start(), calls=%async_computation.3 | async-start | bytes 7077888 | tf_op jit(solution)/shard_map/all_gather | solution.py:35
  39.4 140.0 %reduce-scatter.2.cloned.1.call-start = ((), (), s32[]{:S(2)}) async-start(), calls=%async_computation.4 | async-start | bytes 7077888 | tf_op jit(solution)/shard_map/reduce_scatter | solution.py:39
  117.5 66.6 %copy-start.1 = (s32[512,2]{0,1:T(2,128)S(1)}, s32[512,2]{0,1:T(2,128)}, u32[]{:S(2)}) copy-start(s32[512,2]{0,1:T(2,128)} %param.10) | copy-start | bytes 12292
  179.4 24.7 %all-to-all-start.1 = ((bf16[256,4,384]{0,2,1:T(8,128)(2,1)}), bf16[256,4,384]{0,2,1:T(8,128)(2,1)S(1)}, u32[]{:S(2)}, u32[]{:S(2)}) async-start(bf16[256,4,384]{0,2,1:T(8,128)(2,1)} %bitcast.56), calls=%async_computation.2 | async-start | bytes 1572864 | tf_op jit(solution)/shard_map/all_to_all | solution.py:47
Sparse Core Ops, SparseCore 0:
  39.5 45.7 all-gather.1
  117.6 61.7 reduce-scatter.1
where the time goes:
time: 216 us; the launch traced here: 215 us
  waiting for transfers between devices  128 us (59%)
  matrix products  32.8 us (15%)
  blocking collectives  26.3 us (12%)
  between operations  13.5 us (6%)
  other arithmetic  6.91 us (3%)
  starting transfers between devices  4.64 us (2%)
  local copies, waits for them, and re-layouts  3.4 us (2%)
    reduce_scatter x1, waiting for transfers between devices, shards(): lax.psum_scatter(lax.dot_general(down_mat, hidden, (((0,), (1,)), ((), ()...  61.9 us
    all_gather x1, waiting for transfers between devices, shards(): piece = lax.all_gather(arrived, 'dp', axis=1, tiled=True)  45.9 us
    all_to_all x1, blocking collectives, shards(): lax.all_to_all(outgoing.reshape(expert_count, capacity, local_cols), 'exp...  26.3 us
    dot_general x1, matrix products, shards(): lax.dot_general(down_mat, hidden, (((0,), (1,)), ((), ())), preferred_ele...  20.5 us
    all_to_all x1, waiting for transfers between devices, shards(): lax.all_to_all(summed.reshape(local_cols, expert_count, capacity).astype(...  20 us
    dot_general x1, matrix products, shards(): gate = jnp.dot(piece, gate_mat, preferred_element_type=jnp.float32)  11.6 us
    all_to_all x1, starting transfers between devices, shards(): lax.all_to_all(summed.reshape(local_cols, expert_count, capacity).astype(...  4.59 us
  transfers between devices with their start and end apart: 3, of which 3 were waited for; matrix products, arithmetic and copies ran while one was open for 0% of the time, Pallas kernels for 0%

commit v1 on v0

v1 whole, which is shorter than its diff:
```python
import functools

import jax
import jax.numpy as jnp
from jax import lax
from jax.experimental import pallas as pl
from jax.experimental.pallas import tpu as pltpu
from jax.sharding import PartitionSpec as P

F32 = jnp.float32
BF16 = jnp.bfloat16
ANY = pl.BlockSpec(memory_space=pl.ANY)
VMEM = pl.BlockSpec(memory_space=pltpu.VMEM)
SMEM = pl.BlockSpec(memory_space=pltpu.SMEM)
ORDER = (0, 1, 2, 3)
CORE = 1


def first_link(core):
    return 2 + 2 * core


def second_link(core):
    return 4 - 2 * core


def over_core(value):
    return lax.ppermute(value, "dp", [(i, i ^ CORE) for i in range(lax.axis_size("dp"))])


def over_first(value):
    return lax.ppermute(value, "dp", [(i, i ^ first_link(i & 1)) for i in range(lax.axis_size("dp"))])


def over_second(value):
    return lax.ppermute(value, "dp", [(i, i ^ second_link(i & 1)) for i in range(lax.axis_size("dp"))])


def over_expert(value, mask):
    return lax.ppermute(value, "expert", [(i, i ^ mask) for i in range(lax.axis_size("expert"))])


def ordered(body, operand_count, dep_count):
    def kernel(*refs):
        body(*refs[:operand_count], *refs[operand_count + dep_count :])

    return kernel


def call(body, name, shapes, operands, deps=(), specs=None, scratch=(), vmem=16):
    return pl.pallas_call(
        ordered(body, len(operands), len(deps)),
        out_shape=[jax.ShapeDtypeStruct(s, BF16) for s in shapes],
        in_specs=(specs or [VMEM] * len(operands)) + [ANY] * len(deps),
        out_specs=[VMEM] * len(shapes),
        scratch_shapes=list(scratch),
        compiler_params=pltpu.CompilerParams(vmem_limit_bytes=vmem << 20),
        cost_estimate=pl.CostEstimate(flops=0, bytes_accessed=0, transcendentals=0),
        name=name,
    )(*operands, *deps)


def slots_of(routes_ref, expert_count):
    row_count = routes_ref.shape[1]
    first, second = routes_ref[0:1, :], routes_ref[1:2, :]
    ids = lax.broadcasted_iota(jnp.int32, (8 * pl.cdiv(expert_count, 8), row_count), 0)
    named = (first == ids) | (second == ids)
    above = lax.broadcasted_iota(jnp.int32, (row_count, row_count), 0)
    below = lax.broadcasted_iota(jnp.int32, (row_count, row_count), 1)
    strict = (above < below).astype(F32).astype(BF16)
    earlier = jnp.dot(named.astype(F32).astype(BF16), strict, preferred_element_type=F32)
    return jnp.where(named, earlier.astype(jnp.int32), -1), ids


def dispatch_kernel(me_ref, routes_ref, tokens_ref, *out_refs):
    capacity = out_refs[0].shape[0]
    slots, ids = slots_of(routes_ref, len(out_refs))
    tokens = tokens_ref[...]
    slot_ids = lax.broadcasted_iota(jnp.int32, (capacity, tokens.shape[0]), 0)
    for j in range(len(out_refs)):
        mine = jnp.max(jnp.where(ids == me_ref[0] ^ j, slots, -1), axis=0, keepdims=True)
        placement = (slot_ids == mine).astype(F32).astype(BF16)
        out_refs[j][...] = jnp.dot(placement, tokens, preferred_element_type=F32).astype(BF16)


def mixing_kernel(me_ref, routes_ref, scores_ref, *out_refs):
    row_count, capacity = out_refs[0].shape
    slots, ids = slots_of(routes_ref, len(out_refs))
    scores = scores_ref[...].astype(F32)
    weights = scores / jnp.sum(scores, axis=0, keepdims=True)
    slot_ids = lax.broadcasted_iota(jnp.int32, (capacity, row_count), 0)
    for j in range(len(out_refs)):
        expert = me_ref[0] ^ j
        mine = jnp.max(jnp.where(ids == expert, slots, -1), axis=0, keepdims=True)
        weight = jnp.where(routes_ref[0:1, :] == expert, weights[0:1, :], weights[1:2, :])
        out_refs[j][...] = jnp.where(slot_ids == mine, weight, 0.0).T.astype(BF16)


def mixing(me, routes, scores, expert_count, capacity, deps=()):
    return call(
        mixing_kernel,
        "mixing",
        [(routes.shape[0], capacity)] * expert_count,
        [me, routes.T, scores.T],
        deps,
        specs=[SMEM, VMEM, VMEM],
    )


def combine_kernel(*refs):
    count = (len(refs) - 1) // 2
    total = None
    for mix_ref, rows_ref in zip(refs[:count], refs[count : 2 * count]):
        part = jnp.dot(mix_ref[...], rows_ref[...], preferred_element_type=F32)
        total = part if total is None else total + part
    refs[-1][...] = total.astype(BF16)


def stack_kernel(low_ref, high_ref, out_ref):
    out_ref[0] = low_ref[...]
    out_ref[1] = high_ref[...]


def pick_kernel(pair_ref, out_ref):
    out_ref[...] = pair_ref[0]


def expert_kernel(
    me_ref, pair_ref, near_ref, far_ref, diag_ref, other_diag_ref, gate_ref, up_ref, down_ref,
    own_ref, keep_ref, give_ref, hidden,
):
    me = me_ref[1]
    core = me & 1
    mine, theirs = first_link(core), second_link(core)
    width = pair_ref.shape[2]
    units = hidden.shape[1]
    tile = 256
    pieces = (
        (pair_ref.at[0], me),
        (pair_ref.at[1], me ^ 1),
        (near_ref.at[0], me ^ mine),
        (near_ref.at[1], me ^ mine ^ 1),
        (far_ref.at[1], me ^ theirs),
        (far_ref.at[0], me ^ theirs ^ 1),
        (diag_ref, me ^ 6),
        (other_diag_ref, me ^ 7),
    )
    for start in range(0, units, tile):
        gate = up = None
        for ref, source in pieces:
            rows = pl.ds(pl.multiple_of(source * width, width), width)
            x = ref[...]
            g = jnp.dot(x, gate_ref[rows, start : start + tile], preferred_element_type=F32)
            u = jnp.dot(x, up_ref[rows, start : start + tile], preferred_element_type=F32)
            gate = g if gate is None else gate + g
            up = u if up is None else up + u
        hidden[:, start : start + tile] = (gate / (1.0 + jnp.exp(-gate)) * up).astype(BF16)
    results = (
        (keep_ref.at[2], me ^ 6),
        (give_ref.at[2], me ^ 7),
        (give_ref.at[1], me ^ theirs),
        (give_ref.at[0], me ^ theirs ^ 1),
        (keep_ref.at[0], me ^ mine),
        (keep_ref.at[1], me ^ mine ^ 1),
        (own_ref.at[0], me),
        (own_ref.at[1], me ^ 1),
    )
    for ref, target in results:
        columns = pl.ds(pl.multiple_of(target * width, width), width)
        ref[...] = jnp.dot(hidden[...], down_ref[:, columns], preferred_element_type=F32).astype(BF16)


def diag_sum_kernel(keep_ref, got_ref, out_ref):
    out_ref[...] = (keep_ref[2].astype(F32) + got_ref[2].astype(F32)).astype(BF16)


def near_sum_kernel(keep_ref, got_ref, relayed_ref, out_ref):
    out_ref[0] = (keep_ref[0].astype(F32) + got_ref[0].astype(F32) + relayed_ref[...].astype(F32)).astype(BF16)
    out_ref[1] = (keep_ref[1].astype(F32) + got_ref[1].astype(F32)).astype(BF16)


def other_sum_kernel(own_ref, near_ref, out_ref):
    out_ref[...] = (own_ref[1].astype(F32) + near_ref[1].astype(F32)).astype(BF16)


def last_sum_kernel(own_ref, near_ref, other_ref, out_ref):
    out_ref[...] = (own_ref[0].astype(F32) + near_ref[0].astype(F32) + other_ref[...].astype(F32)).astype(BF16)


def copy_kernel(in_ref, out_ref):
    out_ref[...] = in_ref[...]


def load_kernel(gate_ref, up_ref, down_ref, new_gate_ref, new_up_ref, new_down_ref, sems):
    pairs = ((gate_ref, new_gate_ref), (up_ref, new_up_ref), (down_ref, new_down_ref))
    copies = [pltpu.make_async_copy(old, new, sems.at[i]) for i, (old, new) in enumerate(pairs)]
    for copy in copies:
        copy.start()
    for copy in copies:
        copy.wait()


def experts_by_chips(outgoing, weights, expert_count, capacity, me, routes, scores):
    width = outgoing[0].shape[1]
    units = weights[0].shape[1]
    one, two, three = (capacity, width), (2, capacity, width), (3, capacity, width)
    n = expert_count
    pieces = [outgoing[0]] + [over_expert(outgoing[j], j) for j in range(1, n)]
    near, far, diag, picked, pair = {}, {}, {}, {}, {}
    own, keep, got, relayed, total, back = {}, {}, {}, {}, {}, {}
    summed, nearby = {}, {}

    def gather_start(j, *deps):
        piece = pieces[j]
        if j:
            piece = call(copy_kernel, "arrived", [one], [piece], deps)[0]
        pair[j] = call(stack_kernel, "pair", [two], [piece, over_core(piece)], deps)[0]
        near[j] = over_first(pair[j])

    def gather_relay(j, *deps):
        picked[j] = call(pick_kernel, "pick", [one], [near[j]], deps)[0]
        far[j] = over_core(near[j])
        diag[j] = over_second(picked[j])

    def compute(j, deps, late_deps):
        diag[j] = call(copy_kernel, "relayed", [one], [diag[j]], deps)[0]
        own[j], keep[j], give = call(
            expert_kernel,
            "expert",
            [two, three, three],
            [me, pair[j], near[j], far[j], diag[j], over_core(diag[j]), gate_mat, up_mat, down_mat],
            late_deps,
            specs=[SMEM] + [VMEM] * 8,
            scratch=[pltpu.VMEM((capacity, units), BF16)],
            vmem=16,
        )
        got[j] = over_core(give)

    def scatter_relay(j, *deps):
        summed[j] = call(diag_sum_kernel, "diag_sum", [one], [keep[j], got[j]], deps)[0]
        relayed[j] = over_second(summed[j])

    def scatter_near(j, *deps):
        nearby[j] = call(near_sum_kernel, "near_sum", [two], [keep[j], got[j], relayed[j]], deps)[0]
        total[j] = over_first(nearby[j])

    def scatter_end(j, *deps):
        other = over_core(call(other_sum_kernel, "other_sum", [one], [own[j], total[j]], deps)[0])
        result = call(last_sum_kernel, "last_sum", [one], [own[j], total[j], other])[0]
        back[j] = over_expert(result, j) if j else result

    c0, c1, c2, c3 = ORDER
    gather_start(c0)
    mix = mixing(me, routes, scores, n, capacity, (pair[c0],))
    gather_relay(c0, mix[0])
    gather_start(c1, picked[c0])
    gate_mat, up_mat, down_mat = call(
        load_kernel,
        "load",
        [w.shape for w in weights],
        [pltpu.with_memory_space_constraint(w, pltpu.HBM) for w in weights],
        (pair[c1],),
        specs=[ANY] * 3,
        scratch=[pltpu.SemaphoreType.DMA((3,))],
    )
    gather_relay(c1, gate_mat)
    gather_start(c2, picked[c1])
    compute(c0, (pair[c2],), ())
    gather_start(c3, own[c0])
    gather_relay(c2, pair[c3])
    compute(c1, (picked[c2],), ())
    gather_relay(c3, own[c1])
    scatter_relay(c0, picked[c3])
    compute(c2, (summed[c0],), ())
    scatter_near(c0, own[c2])
    scatter_relay(c1, nearby[c0])
    compute(c3, (summed[c1],), ())
    scatter_near(c1, own[c3])
    scatter_relay(c2, nearby[c1])
    scatter_end(c0, summed[c2])
    scatter_relay(c3, summed[c2])
    scatter_near(c2, summed[c3])
    scatter_end(c1, nearby[c2])
    scatter_near(c3, nearby[c2])
    scatter_end(c2, nearby[c3])
    scatter_end(c3, nearby[c3])
    return mix, [back[j] for j in range(n)]


def experts_by_axes(outgoing, weights):
    expert_count = lax.axis_size("expert")
    capacity, width = outgoing[0].shape
    me = lax.axis_index("expert")
    order = jnp.arange(expert_count) ^ me
    rows = jnp.stack(outgoing)[order]
    rows = lax.all_to_all(rows, "expert", split_axis=0, concat_axis=0, tiled=True)
    rows = lax.all_gather(rows.reshape(-1, width), "dp", axis=1, tiled=True)
    gate = jnp.dot(rows, weights[0], preferred_element_type=F32)
    up = jnp.dot(rows, weights[1], preferred_element_type=F32)
    hidden = (jax.nn.silu(gate) * up).astype(BF16)
    part = jnp.dot(hidden, weights[2], preferred_element_type=F32).astype(BF16)
    total = lax.psum_scatter(part, "dp", scatter_dimension=1, tiled=True)
    back = lax.all_to_all(
        total.reshape(expert_count, capacity, width), "expert", split_axis=0, concat_axis=0, tiled=True
    )[order]
    return [back[j] for j in range(expert_count)]


def shards(tokens, routes, scores, gate_weight, up_weight, down_weight):
    expert_count = lax.axis_size("expert")
    row_count = tokens.shape[0]
    capacity = 3 * row_count // expert_count
    me = jnp.stack([lax.axis_index("expert"), lax.axis_index("dp")]).astype(jnp.int32)
    weights = gate_weight[0], up_weight[0], down_weight[0]

    shape = (capacity, tokens.shape[1])
    outgoing = call(
        dispatch_kernel,
        "dispatch",
        [shape] * expert_count,
        [me, routes.T, tokens],
        specs=[SMEM, VMEM, VMEM],
    )
    if expert_count == 4 and lax.axis_size("dp") == 8:
        mix, results = experts_by_chips(outgoing, weights, expert_count, capacity, me, routes, scores)
    else:
        mix = mixing(me, routes, scores, expert_count, capacity)
        results = experts_by_axes(outgoing, weights)
    return call(combine_kernel, "combine", [tokens.shape], [*mix, *results])[0]


def solution(mesh):
    return jax.shard_map(
        shards,
        mesh=mesh,
        in_specs=(
            P("expert", "dp"),
            P("expert", None),
            P("expert", None),
            P("expert", None, "dp"),
            P("expert", None, "dp"),
            P("expert", "dp", None),
        ),
        out_specs=P("expert", "dp"),
        check_vma=False,
    )
```

time: 216 us -> 133 us (0.62)
  waiting for transfers between devices: 128 us -> 59.5 us
  Pallas kernels: 0 us -> 33 us
  matrix products: 32.8 us -> 0 us
  starting transfers between devices: 4.64 us -> 35.8 us
  blocking collectives: 26.3 us -> 0 us
  between operations: 13.5 us -> 0.35 us
  other arithmetic: 6.91 us -> 0.07 us
    reduce_scatter x1 -> x0, waiting for transfers between devices: 61.9 us -> none  [shards(): lax.psum_scatter(lax.dot_general(down_mat, hidden, (((0,), (1,)), ((), ()...]
    ppermute x0 -> x42, waiting for transfers between devices: none -> 59.5 us  [the longest x8 26 us: over_second(): lax.ppermute(value, 'dp', [(i, i ^ second_link(i & 1)) for i in range(lax...]
    all_gather x1 -> x0, waiting for transfers between devices: 45.9 us -> none  [shards(): piece = lax.all_gather(arrived, 'dp', axis=1, tiled=True)]
    ppermute x0 -> x42, starting transfers between devices: none -> 35.8 us  [the longest x6 12.7 us: over_expert(): lax.ppermute(value, 'expert', [(i, i ^ mask) for i in range(lax.axis_size...]
    pallas_call x0 -> x39, Pallas kernels: none -> 33 us  [call(): pl.pallas_call(ordered(body, len(operands), len(deps)), out_shape=[jax.Sh...]
    dot_general x3 -> x0, matrix products: 32.8 us -> none  [the longest x1 20.5 us: shards(): lax.dot_general(down_mat, hidden, (((0,), (1,)), ((), ())), preferred_ele...]
    all_to_all x1 -> x0, blocking collectives: 26.3 us -> none  [shards(): lax.all_to_all(outgoing.reshape(expert_count, capacity, local_cols), 'exp...]
    all_to_all x1 -> x0, waiting for transfers between devices: 20 us -> none  [shards(): lax.all_to_all(summed.reshape(local_cols, expert_count, capacity).astype(...]
  transfers between devices with their start and end apart: 3 -> 42, of which waited for: 3 -> 18; matrix products, arithmetic and copies ran while one was open for 0% -> 0% of each run, Pallas kernels for 0% -> 23%
where the time goes in v1:
time: 133 us; the launch traced here: 132 us
  waiting for transfers between devices  59.5 us (45%)
  starting transfers between devices  35.8 us (27%)
  Pallas kernels  33 us (25%)
  local copies, waits for them, and re-layouts  3.01 us (2%)
    pallas_call x39, Pallas kernels, call(): pl.pallas_call(ordered(body, len(operands), len(deps)), out_shape=[jax.Sh...  33 us
    ppermute x8, waiting for transfers between devices, over_second(): lax.ppermute(value, 'dp', [(i, i ^ second_link(i & 1)) for i in range(lax...  26 us
    ppermute x6, waiting for transfers between devices, over_expert(): lax.ppermute(value, 'expert', [(i, i ^ mask) for i in range(lax.axis_size...  19.2 us
    ppermute x6, starting transfers between devices, over_expert(): lax.ppermute(value, 'expert', [(i, i ^ mask) for i in range(lax.axis_size...  12.7 us
    ppermute x8, waiting for transfers between devices, over_first(): lax.ppermute(value, 'dp', [(i, i ^ first_link(i & 1)) for i in range(lax....  10.1 us
    ppermute x8, starting transfers between devices, over_first(): lax.ppermute(value, 'dp', [(i, i ^ first_link(i & 1)) for i in range(lax....  9.88 us
    ppermute x8, starting transfers between devices, over_second(): lax.ppermute(value, 'dp', [(i, i ^ second_link(i & 1)) for i in range(lax...  7.91 us
    ppermute x20, starting transfers between devices, over_core(): lax.ppermute(value, 'dp', [(i, i ^ CORE) for i in range(lax.axis_size('dp...  5.29 us
  transfers between devices with their start and end apart: 42, of which 18 were waited for; matrix products, arithmetic and copies ran while one was open for 0% of the time, Pallas kernels for 23%

profile of v1, /device:TPU:0, one launch (start us, length us, event | category | flops | bytes accessed | tf_op | source)
XLA Modules:
  0.0 131.6 jit_solution(12593945015771336002)
XLA Ops:
  4.6 2.9 %collective-permute-start.1 = (bf16[2,384,256]{2,1,0:T(8,128)(2,1)S(1)}, bf16[2,384,256]{2,1,0:T(8,128)(2,1)S(1)}, u32[]{:S(2)}, u32[]{:S(2)}) collective-permute-start(bf16[2,384,256]{2,1,0:T(8,128)(2,1)S(1)} %pair.4.refs_3_.refs_1_), channel_id=1, source_target_pairs={{0,8},{4,20},{8,0},{12,28},{16,24},{20,4},{24,16},{28,12},{1,9},{5... | collective-permute-start | bytes 1179656 | tf_op jit(solution)/shard_map/ppermute | solution.py:32
  7.5 1.6 %collective-permute-start.5 = (bf16[384,256]{1,0:T(8,128)(2,1)S(1)}, bf16[384,256]{1,0:T(8,128)(2,1)S(1)}, u32[]{:S(2)}, u32[]{:S(2)}) collective-permute-start(bf16[384,256]{1,0:T(8,128)(2,1)S(1)} %get-tuple-element.34), channel_id=1, source_target_pairs={{0,1},{1,0},{2,3},{3,2},{4,5},{5,4},{6,7},{7,6},{8,9},{9,8},{10,11... | collective-permute-start | bytes 589832 | tf_op jit(solution)/shard_map/ppermute | solution.py:40
  11.8 1.5 %collective-permute-done.1.refs_0_.refs_2_ = bf16[2,384,256]{2,1,0:T(8,128)(2,1)S(1)} collective-permute-done((bf16[2,384,256]{2,1,0:T(8,128)(2,1)S(1)}, bf16[2,384,256]{2,1,0:T(8,128)(2,1)S(1)}, u32[]{:S(2)}, u32[]{:S(2)}) %collective-permute-start.1) | collective-permute-done | bytes 393248 | tf_op jit(solution)/shard_map/ppermute | solution.py:32
  17.0 3.0 %collective-permute-start.4 = (bf16[384,256]{1,0:T(8,128)(2,1)S(1)}, bf16[384,256]{1,0:T(8,128)(2,1)S(1)}, u32[]{:S(2)}, u32[]{:S(2)}) collective-permute-start(bf16[384,256]{1,0:T(8,128)(2,1)S(1)} %get-tuple-element.33), channel_id=1, source_target_pairs={{0,2},{1,3},{2,0},{3,1},{4,6},{5,7},{6,4},{7,5},{8,10},{9,11},{10,... | collective-permute-start | bytes 589832 | tf_op jit(solution)/shard_map/ppermute | solution.py:40
  19.9 4.7 %load.1 = (bf16[2048,1024]{1,0:T(8,128)(2,1)S(1)}, bf16[2048,1024]{1,0:T(8,128)(2,1)S(1)}, bf16[1024,2048]{1,0:T(8,128)(2,1)S(1)}) custom-call(bf16[2048,1024]{1,0:T(8,128)(2,1)} %bitcast.10, bf16[2048,1024]{1,0:T(8,128)(2,1)} %bitcast.11, bf16[1024,2048]{1,0:T(8,128)(2,1)} %bitcast.12, bf16[2,384,256]{2,1,0:T(8,128)(2,1)S(1)} %pair.5.refs_3_.refs_1_), custom_call_target="tpu_custom_call" | custom-call | tf_op jit(solution)/shard_map/load/pallas_call | solution.py:51
  24.6 4.1 %collective-permute-done.4.refs_0_ = bf16[384,256]{1,0:T(8,128)(2,1)S(1)} collective-permute-done((bf16[384,256]{1,0:T(8,128)(2,1)S(1)}, bf16[384,256]{1,0:T(8,128)(2,1)S(1)}, u32[]{:S(2)}, u32[]{:S(2)}) %collective-permute-start.4) | collective-permute-done | bytes 196640 | tf_op jit(solution)/shard_map/ppermute | solution.py:40
  30.6 4.0 %collective-permute-done.3.refs_0_ = bf16[384,256]{1,0:T(8,128)(2,1)S(1)} collective-permute-done((bf16[384,256]{1,0:T(8,128)(2,1)S(1)}, bf16[384,256]{1,0:T(8,128)(2,1)S(1)}, u32[]{:S(2)}, u32[]{:S(2)}) %collective-permute-start.3) | collective-permute-done | bytes 196640 | tf_op jit(solution)/shard_map/ppermute | solution.py:36
  34.7 3.6 %collective-permute-start.11 = (bf16[384,256]{1,0:T(8,128)(2,1)S(1)}, bf16[384,256]{1,0:T(8,128)(2,1)S(1)}, u32[]{:S(2)}, u32[]{:S(2)}) collective-permute-start(bf16[384,256]{1,0:T(8,128)(2,1)S(1)} %get-tuple-element.41), channel_id=1, source_target_pairs={{0,3},{1,2},{2,1},{3,0},{4,7},{5,6},{6,5},{7,4},{8,11},{9,10},{10,... | collective-permute-start | bytes 589832 | tf_op jit(solution)/shard_map/ppermute | solution.py:40
  38.2 1.5 %collective-permute-start.16 = (bf16[2,384,256]{2,1,0:T(8,128)(2,1)S(1)}, bf16[2,384,256]{2,1,0:T(8,128)(2,1)S(1)}, u32[]{:S(2)}, u32[]{:S(2)}) collective-permute-start(bf16[2,384,256]{2,1,0:T(8,128)(2,1)S(1)} %pair.6.refs_1_), channel_id=1, source_target_pairs={{0,8},{4,20},{8,0},{12,28},{16,24},{20,4},{24,16},{28,12},{1,9},{5... | collective-permute-start | bytes 1179656 | tf_op jit(solution)/shard_map/ppermute | solution.py:32
  39.7 5.7 %expert.4 = (bf16[2,384,256]{2,1,0:T(8,128)(2,1)S(1)}, bf16[3,384,256]{2,1,0:T(8,128)(2,1)S(1)}, bf16[3,384,256]{2,1,0:T(8,128)(2,1)S(1)}) custom-call(s32[2]{0:T(128)S(1)} %pad_add_fusion.refs_0_, bf16[2,384,256]{2,1,0:T(8,128)(2,1)S(1)} %pair.4.refs_3_.refs_1_, bf16[2,384,256]{2,1,0:T(8,128)(2,1)S(1)} %collective-permute-done.1.refs_0_.refs_2_, ...), custom_call_target="tpu_custom_call" | custom-call | tf_op jit(solution)/shard_map/expert/pallas_call | solution.py:51
  47.1 4.2 %collective-permute-done.15.refs_0_ = bf16[384,256]{1,0:T(8,128)(2,1)S(1)} collective-permute-done((bf16[384,256]{1,0:T(8,128)(2,1)S(1)}, bf16[384,256]{1,0:T(8,128)(2,1)S(1)}, u32[]{:S(2)}, u32[]{:S(2)}) %collective-permute-start.15) | collective-permute-done | bytes 196640 | tf_op jit(solution)/shard_map/ppermute | solution.py:36
  52.8 5.7 %expert.5 = (bf16[2,384,256]{2,1,0:T(8,128)(2,1)S(1)}, bf16[3,384,256]{2,1,0:T(8,128)(2,1)S(1)}, bf16[3,384,256]{2,1,0:T(8,128)(2,1)S(1)}) custom-call(s32[2]{0:T(128)S(1)} %pad_add_fusion.refs_0_, bf16[2,384,256]{2,1,0:T(8,128)(2,1)S(1)} %pair.5.refs_3_.refs_1_, bf16[2,384,256]{2,1,0:T(8,128)(2,1)S(1)} %collective-permute-done.7.refs_0_.refs_2_, ...), custom_call_target="tpu_custom_call" | custom-call | tf_op jit(solution)/shard_map/expert/pallas_call | solution.py:51
  60.0 4.7 %collective-permute-done.20.refs_0_ = bf16[384,256]{1,0:T(8,128)(2,1)S(1)} collective-permute-done((bf16[384,256]{1,0:T(8,128)(2,1)S(1)}, bf16[384,256]{1,0:T(8,128)(2,1)S(1)}, u32[]{:S(2)}, u32[]{:S(2)}) %collective-permute-start.20) | collective-permute-done | bytes 196640 | tf_op jit(solution)/shard_map/ppermute | solution.py:36
  66.9 5.9 %expert.6 = (bf16[2,384,256]{2,1,0:T(8,128)(2,1)S(1)}, bf16[3,384,256]{2,1,0:T(8,128)(2,1)S(1)}, bf16[3,384,256]{2,1,0:T(8,128)(2,1)S(1)}) custom-call(s32[2]{0:T(128)S(1)} %pad_add_fusion.refs_0_, bf16[2,384,256]{2,1,0:T(8,128)(2,1)S(1)} %pair.6.refs_1_, bf16[2,384,256]{2,1,0:T(8,128)(2,1)S(1)} %collective-permute-done.16.refs_0_.refs_2_, ...), custom_call_target="tpu_custom_call" | custom-call | tf_op jit(solution)/shard_map/expert/pallas_call | solution.py:51
  74.7 5.7 %expert.7 = (bf16[2,384,256]{2,1,0:T(8,128)(2,1)S(1)}, bf16[3,384,256]{2,1,0:T(8,128)(2,1)S(1)}, bf16[3,384,256]{2,1,0:T(8,128)(2,1)S(1)}) custom-call(s32[2]{0:T(128)S(1)} %pad_add_fusion.refs_0_, bf16[2,384,256]{2,1,0:T(8,128)(2,1)S(1)} %pair.7.refs_1_, bf16[2,384,256]{2,1,0:T(8,128)(2,1)S(1)} %collective-permute-done.13.refs_0_.refs_2_, ...), custom_call_target="tpu_custom_call" | custom-call | tf_op jit(solution)/shard_map/expert/pallas_call | solution.py:51
  81.7 4.8 %collective-permute-done.25.refs_2_ = bf16[384,256]{1,0:T(8,128)(2,1)S(1)} collective-permute-done((bf16[384,256]{1,0:T(8,128)(2,1)S(1)}, bf16[384,256]{1,0:T(8,128)(2,1)S(1)}, u32[]{:S(2)}, u32[]{:S(2)}) %collective-permute-start.25) | collective-permute-done | bytes 196640 | tf_op jit(solution)/shard_map/ppermute | solution.py:36
  89.6 4.9 %collective-permute-done.31.refs_2_ = bf16[384,256]{1,0:T(8,128)(2,1)S(1)} collective-permute-done((bf16[384,256]{1,0:T(8,128)(2,1)S(1)}, bf16[384,256]{1,0:T(8,128)(2,1)S(1)}, u32[]{:S(2)}, u32[]{:S(2)}) %collective-permute-start.31) | collective-permute-done | bytes 196640 | tf_op jit(solution)/shard_map/ppermute | solution.py:36
  95.4 3.3 %collective-permute-done.36.refs_2_ = bf16[384,256]{1,0:T(8,128)(2,1)S(1)} collective-permute-done((bf16[384,256]{1,0:T(8,128)(2,1)S(1)}, bf16[384,256]{1,0:T(8,128)(2,1)S(1)}, u32[]{:S(2)}, u32[]{:S(2)}) %collective-permute-start.36) | collective-permute-done | bytes 196640 | tf_op jit(solution)/shard_map/ppermute | solution.py:36
  103.1 3.6 %collective-permute-done.39.refs_1_ = bf16[2,384,256]{2,1,0:T(8,128)(2,1)S(1)} collective-permute-done((bf16[2,384,256]{2,1,0:T(8,128)(2,1)S(1)}, bf16[2,384,256]{2,1,0:T(8,128)(2,1)S(1)}, u32[]{:S(2)}, u32[]{:S(2)}) %collective-permute-start.39) | collective-permute-done | bytes 393248 | tf_op jit(solution)/shard_map/ppermute | solution.py:32
  107.3 3.6 %collective-permute-done.22.refs_1_ = bf16[2,384,256]{2,1,0:T(8,128)(2,1)S(1)} collective-permute-done((bf16[2,384,256]{2,1,0:T(8,128)(2,1)S(1)}, bf16[2,384,256]{2,1,0:T(8,128)(2,1)S(1)}, u32[]{:S(2)}, u32[]{:S(2)}) %collective-permute-start.22) | collective-permute-done | bytes 393248 | tf_op jit(solution)/shard_map/ppermute | solution.py:32
  111.3 1.7 %collective-permute-start.34 = (bf16[384,256]{1,0:T(8,128)(2,1)S(1)}, bf16[384,256]{1,0:T(8,128)(2,1)S(1)}, u32[]{:S(2)}, u32[]{:S(2)}) collective-permute-start(bf16[384,256]{1,0:T(8,128)(2,1)S(1)} %last_sum.5), channel_id=1, source_target_pairs={{0,1},{1,0},{2,3},{3,2},{4,5},{5,4},{6,7},{7,6},{8,9},{9,8},{10,11... | collective-permute-start | bytes 589832 | tf_op jit(solution)/shard_map/ppermute | solution.py:40
  114.2 1.8 %collective-permute-start.41 = (bf16[384,256]{1,0:T(8,128)(2,1)S(1)}, bf16[384,256]{1,0:T(8,128)(2,1)S(1)}, u32[]{:S(2)}, u32[]{:S(2)}) collective-permute-start(bf16[384,256]{1,0:T(8,128)(2,1)S(1)} %last_sum.7), channel_id=1, source_target_pairs={{0,3},{1,2},{2,1},{3,0},{4,7},{5,6},{6,5},{7,4},{8,11},{9,10},{10,... | collective-permute-start | bytes 589832 | tf_op jit(solution)/shard_map/ppermute | solution.py:40
  116.1 5.0 %collective-permute-done.34.refs_5_ = bf16[384,256]{1,0:T(8,128)(2,1)S(1)} collective-permute-done((bf16[384,256]{1,0:T(8,128)(2,1)S(1)}, bf16[384,256]{1,0:T(8,128)(2,1)S(1)}, u32[]{:S(2)}, u32[]{:S(2)}) %collective-permute-start.34) | collective-permute-done | bytes 196640 | tf_op jit(solution)/shard_map/ppermute | solution.py:40
  121.1 9.1 %collective-permute-done.38.refs_6_ = bf16[384,256]{1,0:T(8,128)(2,1)S(1)} collective-permute-done((bf16[384,256]{1,0:T(8,128)(2,1)S(1)}, bf16[384,256]{1,0:T(8,128)(2,1)S(1)}, u32[]{:S(2)}, u32[]{:S(2)}) %collective-permute-start.38) | collective-permute-done | bytes 196640 | tf_op jit(solution)/shard_map/ppermute | solution.py:40
  (108 shorter events, 34.8 us)
Async XLA Ops:
  4.6 8.7 %collective-permute-start.1 = (bf16[2,384,256]{2,1,0:T(8,128)(2,1)S(1)}, bf16[2,384,256]{2,1,0:T(8,128)(2,1)S(1)}, u32[]{:S(2)}, u32[]{:S(2)}) collective-permute-start(bf16[2,384,256]{2,1,0:T(8,128)(2,1)S(1)} %pair.4.refs_3_.refs_1_), channel_id=1, source_target_pairs={{0,8},{4,20},{8,0},{12,28},{16,24},{20,4},{24,16},{28,12},{1,9},{5... | collective-permute-start | bytes 1179656 | tf_op jit(solution)/shard_map/ppermute | solution.py:32
  15.8 8.8 %collective-permute-start.7 = (bf16[2,384,256]{2,1,0:T(8,128)(2,1)S(1)}, bf16[2,384,256]{2,1,0:T(8,128)(2,1)S(1)}, u32[]{:S(2)}, u32[]{:S(2)}) collective-permute-start(bf16[2,384,256]{2,1,0:T(8,128)(2,1)S(1)} %pair.5.refs_3_.refs_1_), channel_id=1, source_target_pairs={{0,8},{4,20},{8,0},{12,28},{16,24},{20,4},{24,16},{28,12},{1,9},{5... | collective-permute-start | bytes 1179656 | tf_op jit(solution)/shard_map/ppermute | solution.py:32
  17.0 11.8 %collective-permute-start.4 = (bf16[384,256]{1,0:T(8,128)(2,1)S(1)}, bf16[384,256]{1,0:T(8,128)(2,1)S(1)}, u32[]{:S(2)}, u32[]{:S(2)}) collective-permute-start(bf16[384,256]{1,0:T(8,128)(2,1)S(1)} %get-tuple-element.33), channel_id=1, source_target_pairs={{0,2},{1,3},{2,0},{3,1},{4,6},{5,7},{6,4},{7,5},{8,10},{9,11},{10,... | collective-permute-start | bytes 589832 | tf_op jit(solution)/shard_map/ppermute | solution.py:40
  29.8 9.9 %collective-permute-start.2 = (bf16[2,384,256]{2,1,0:T(8,128)(2,1)S(1)}, bf16[2,384,256]{2,1,0:T(8,128)(2,1)S(1)}, u32[]{:S(2)}, u32[]{:S(2)}) collective-permute-start(bf16[2,384,256]{2,1,0:T(8,128)(2,1)S(1)} %collective-permute-done.1.refs_0_.refs_2_), channel_id=1, source_target_pairs={{0,4},{4,0},{8,12},{12,8},{16,20},{20,16},{24,28},{28,24},{1,5},{5... | collective-permute-start | bytes 1179656 | tf_op jit(solution)/shard_map/ppermute | solution.py:28
  34.7 10.7 %collective-permute-start.11 = (bf16[384,256]{1,0:T(8,128)(2,1)S(1)}, bf16[384,256]{1,0:T(8,128)(2,1)S(1)}, u32[]{:S(2)}, u32[]{:S(2)}) collective-permute-start(bf16[384,256]{1,0:T(8,128)(2,1)S(1)} %get-tuple-element.41), channel_id=1, source_target_pairs={{0,3},{1,2},{2,1},{3,0},{4,7},{5,6},{6,5},{7,4},{8,11},{9,10},{10,... | collective-permute-start | bytes 589832 | tf_op jit(solution)/shard_map/ppermute | solution.py:40
  38.2 8.8 %collective-permute-start.16 = (bf16[2,384,256]{2,1,0:T(8,128)(2,1)S(1)}, bf16[2,384,256]{2,1,0:T(8,128)(2,1)S(1)}, u32[]{:S(2)}, u32[]{:S(2)}) collective-permute-start(bf16[2,384,256]{2,1,0:T(8,128)(2,1)S(1)} %pair.6.refs_1_), channel_id=1, source_target_pairs={{0,8},{4,20},{8,0},{12,28},{16,24},{20,4},{24,16},{28,12},{1,9},{5... | collective-permute-start | bytes 1179656 | tf_op jit(solution)/shard_map/ppermute | solution.py:32
  46.5 13.5 %collective-permute-start.10 = (bf16[3,384,256]{2,1,0:T(8,128)(2,1)S(1)}, bf16[3,384,256]{2,1,0:T(8,128)(2,1)S(1)}, u32[]{:S(2)}, u32[]{:S(2)}) collective-permute-start(bf16[3,384,256]{2,1,0:T(8,128)(2,1)S(1)} %get-tuple-element.40), channel_id=1, source_target_pairs={{0,4},{4,0},{8,12},{12,8},{16,20},{20,16},{24,28},{28,24},{1,5},{5... | collective-permute-start | bytes 1769480 | tf_op jit(solution)/shard_map/ppermute | solution.py:28
  51.4 8.6 %collective-permute-start.13 = (bf16[2,384,256]{2,1,0:T(8,128)(2,1)S(1)}, bf16[2,384,256]{2,1,0:T(8,128)(2,1)S(1)}, u32[]{:S(2)}, u32[]{:S(2)}) collective-permute-start(bf16[2,384,256]{2,1,0:T(8,128)(2,1)S(1)} %pair.7.refs_1_), channel_id=1, source_target_pairs={{0,8},{4,20},{8,0},{12,28},{16,24},{20,4},{24,16},{28,12},{1,9},{5... | collective-permute-start | bytes 1179656 | tf_op jit(solution)/shard_map/ppermute | solution.py:32
  58.5 14.4 %collective-permute-start.24 = (bf16[3,384,256]{2,1,0:T(8,128)(2,1)S(1)}, bf16[3,384,256]{2,1,0:T(8,128)(2,1)S(1)}, u32[]{:S(2)}, u32[]{:S(2)}) collective-permute-start(bf16[3,384,256]{2,1,0:T(8,128)(2,1)S(1)} %get-tuple-element.47), channel_id=1, source_target_pairs={{0,4},{4,0},{8,12},{12,8},{16,20},{20,16},{24,28},{28,24},{1,5},{5... | collective-permute-start | bytes 1769480 | tf_op jit(solution)/shard_map/ppermute | solution.py:28
  58.7 8.2 %collective-permute-start.19 = (bf16[2,384,256]{2,1,0:T(8,128)(2,1)S(1)}, bf16[2,384,256]{2,1,0:T(8,128)(2,1)S(1)}, u32[]{:S(2)}, u32[]{:S(2)}) collective-permute-start(bf16[2,384,256]{2,1,0:T(8,128)(2,1)S(1)} %collective-permute-done.16.refs_0_.refs_2_), channel_id=1, source_target_pairs={{0,4},{4,0},{8,12},{12,8},{16,20},{20,16},{24,28},{28,24},{1,5},{5... | collective-permute-start | bytes 1179656 | tf_op jit(solution)/shard_map/ppermute | solution.py:28
  64.8 8.0 %collective-permute-start.18 = (bf16[384,256]{1,0:T(8,128)(2,1)S(1)}, bf16[384,256]{1,0:T(8,128)(2,1)S(1)}, u32[]{:S(2)}, u32[]{:S(2)}) collective-permute-start(bf16[384,256]{1,0:T(8,128)(2,1)S(1)} %diag_sum.4.refs_1_), channel_id=1, source_target_pairs={{0,16},{4,12},{8,24},{12,4},{16,0},{20,28},{24,8},{28,20},{1,17},{... | collective-permute-start | bytes 589832 | tf_op jit(solution)/shard_map/ppermute | solution.py:36
  73.6 13.0 %collective-permute-start.23 = (bf16[3,384,256]{2,1,0:T(8,128)(2,1)S(1)}, bf16[3,384,256]{2,1,0:T(8,128)(2,1)S(1)}, u32[]{:S(2)}, u32[]{:S(2)}) collective-permute-start(bf16[3,384,256]{2,1,0:T(8,128)(2,1)S(1)} %get-tuple-element.45), channel_id=1, source_target_pairs={{0,4},{4,0},{8,12},{12,8},{16,20},{20,16},{24,28},{28,24},{1,5},{5... | collective-permute-start | bytes 1769480 | tf_op jit(solution)/shard_map/ppermute | solution.py:28
  86.7 7.8 %collective-permute-start.31 = (bf16[384,256]{1,0:T(8,128)(2,1)S(1)}, bf16[384,256]{1,0:T(8,128)(2,1)S(1)}, u32[]{:S(2)}, u32[]{:S(2)}) collective-permute-start(bf16[384,256]{1,0:T(8,128)(2,1)S(1)} %diag_sum.6.refs_2_), channel_id=1, source_target_pairs={{0,16},{4,12},{8,24},{12,4},{16,0},{20,28},{24,8},{28,20},{1,17},{... | collective-permute-start | bytes 589832 | tf_op jit(solution)/shard_map/ppermute | solution.py:36
  87.7 11.0 %collective-permute-start.36 = (bf16[384,256]{1,0:T(8,128)(2,1)S(1)}, bf16[384,256]{1,0:T(8,128)(2,1)S(1)}, u32[]{:S(2)}, u32[]{:S(2)}) collective-permute-start(bf16[384,256]{1,0:T(8,128)(2,1)S(1)} %diag_sum.7.refs_3_), channel_id=1, source_target_pairs={{0,16},{4,12},{8,24},{12,4},{16,0},{20,28},{24,8},{28,20},{1,17},{... | collective-permute-start | bytes 589832 | tf_op jit(solution)/shard_map/ppermute | solution.py:36
  88.9 12.1 %collective-permute-start.30 = (bf16[2,384,256]{2,1,0:T(8,128)(2,1)S(1)}, bf16[2,384,256]{2,1,0:T(8,128)(2,1)S(1)}, u32[]{:S(2)}, u32[]{:S(2)}) collective-permute-start(bf16[2,384,256]{2,1,0:T(8,128)(2,1)S(1)} %near_sum.5.refs_2_), channel_id=1, source_target_pairs={{0,8},{4,20},{8,0},{12,28},{16,24},{20,4},{24,16},{28,12},{1,9},{5... | collective-permute-start | bytes 1179656 | tf_op jit(solution)/shard_map/ppermute | solution.py:32
  94.6 7.8 %collective-permute-start.35 = (bf16[2,384,256]{2,1,0:T(8,128)(2,1)S(1)}, bf16[2,384,256]{2,1,0:T(8,128)(2,1)S(1)}, u32[]{:S(2)}, u32[]{:S(2)}) collective-permute-start(bf16[2,384,256]{2,1,0:T(8,128)(2,1)S(1)} %near_sum.6.refs_2_.refs_3_), channel_id=1, source_target_pairs={{0,8},{4,20},{8,0},{12,28},{16,24},{20,4},{24,16},{28,12},{1,9},{5... | collective-permute-start | bytes 1179656 | tf_op jit(solution)/shard_map/ppermute | solution.py:32
  98.8 7.8 %collective-permute-start.39 = (bf16[2,384,256]{2,1,0:T(8,128)(2,1)S(1)}, bf16[2,384,256]{2,1,0:T(8,128)(2,1)S(1)}, u32[]{:S(2)}, u32[]{:S(2)}) collective-permute-start(bf16[2,384,256]{2,1,0:T(8,128)(2,1)S(1)} %near_sum.7.refs_2_), channel_id=1, source_target_pairs={{0,8},{4,20},{8,0},{12,28},{16,24},{20,4},{24,16},{28,12},{1,9},{5... | collective-permute-start | bytes 1179656 | tf_op jit(solution)/shard_map/ppermute | solution.py:32
  99.6 11.3 %collective-permute-start.22 = (bf16[2,384,256]{2,1,0:T(8,128)(2,1)S(1)}, bf16[2,384,256]{2,1,0:T(8,128)(2,1)S(1)}, u32[]{:S(2)}, u32[]{:S(2)}) collective-permute-start(bf16[2,384,256]{2,1,0:T(8,128)(2,1)S(1)} %near_sum.4.refs_2_), channel_id=1, source_target_pairs={{0,8},{4,20},{8,0},{12,28},{16,24},{20,4},{24,16},{28,12},{1,9},{5... | collective-permute-start | bytes 1179656 | tf_op jit(solution)/shard_map/ppermute | solution.py:32
  101.0 10.2 %collective-permute-start.33 = (bf16[384,256]{1,0:T(8,128)(2,1)S(1)}, bf16[384,256]{1,0:T(8,128)(2,1)S(1)}, u32[]{:S(2)}, u32[]{:S(2)}) collective-permute-start(bf16[384,256]{1,0:T(8,128)(2,1)S(1)} %other_sum.5), channel_id=1, source_target_pairs={{0,4},{4,0},{8,12},{12,8},{16,20},{20,16},{24,28},{28,24},{1,5},{5... | collective-permute-start | bytes 589832 | tf_op jit(solution)/shard_map/ppermute | solution.py:28
  102.5 10.4 %collective-permute-start.37 = (bf16[384,256]{1,0:T(8,128)(2,1)S(1)}, bf16[384,256]{1,0:T(8,128)(2,1)S(1)}, u32[]{:S(2)}, u32[]{:S(2)}) collective-permute-start(bf16[384,256]{1,0:T(8,128)(2,1)S(1)} %other_sum.6), channel_id=1, source_target_pairs={{0,4},{4,0},{8,12},{12,8},{16,20},{20,16},{24,28},{28,24},{1,5},{5... | collective-permute-start | bytes 589832 | tf_op jit(solution)/shard_map/ppermute | solution.py:28
  106.7 7.4 %collective-permute-start.40 = (bf16[384,256]{1,0:T(8,128)(2,1)S(1)}, bf16[384,256]{1,0:T(8,128)(2,1)S(1)}, u32[]{:S(2)}, u32[]{:S(2)}) collective-permute-start(bf16[384,256]{1,0:T(8,128)(2,1)S(1)} %other_sum.7), channel_id=1, source_target_pairs={{0,4},{4,0},{8,12},{12,8},{16,20},{20,16},{24,28},{28,24},{1,5},{5... | collective-permute-start | bytes 589832 | tf_op jit(solution)/shard_map/ppermute | solution.py:28
  111.3 9.8 %collective-permute-start.34 = (bf16[384,256]{1,0:T(8,128)(2,1)S(1)}, bf16[384,256]{1,0:T(8,128)(2,1)S(1)}, u32[]{:S(2)}, u32[]{:S(2)}) collective-permute-start(bf16[384,256]{1,0:T(8,128)(2,1)S(1)} %last_sum.5), channel_id=1, source_target_pairs={{0,1},{1,0},{2,3},{3,2},{4,5},{5,4},{6,7},{7,6},{8,9},{9,8},{10,11... | collective-permute-start | bytes 589832 | tf_op jit(solution)/shard_map/ppermute | solution.py:40
  113.0 17.2 %collective-permute-start.38 = (bf16[384,256]{1,0:T(8,128)(2,1)S(1)}, bf16[384,256]{1,0:T(8,128)(2,1)S(1)}, u32[]{:S(2)}, u32[]{:S(2)}) collective-permute-start(bf16[384,256]{1,0:T(8,128)(2,1)S(1)} %last_sum.6), channel_id=1, source_target_pairs={{0,2},{1,3},{2,0},{3,1},{4,6},{5,7},{6,4},{7,5},{8,10},{9,11},{10,... | collective-permute-start | bytes 589832 | tf_op jit(solution)/shard_map/ppermute | solution.py:40
  114.2 16.0 %collective-permute-start.41 = (bf16[384,256]{1,0:T(8,128)(2,1)S(1)}, bf16[384,256]{1,0:T(8,128)(2,1)S(1)}, u32[]{:S(2)}, u32[]{:S(2)}) collective-permute-start(bf16[384,256]{1,0:T(8,128)(2,1)S(1)} %last_sum.7), channel_id=1, source_target_pairs={{0,3},{1,2},{2,1},{3,0},{4,7},{5,6},{6,5},{7,4},{8,11},{9,10},{10,... | collective-permute-start | bytes 589832 | tf_op jit(solution)/shard_map/ppermute | solution.py:40
  (22 other events, 81.3 us)

commit v2 on v1

v2 whole, which is shorter than its diff:
```python
import functools

import jax
import jax.numpy as jnp
from jax import lax
from jax.experimental import pallas as pl
from jax.experimental.pallas import tpu as pltpu
from jax.sharding import PartitionSpec as P

F32 = jnp.float32
BF16 = jnp.bfloat16
ANY = pl.BlockSpec(memory_space=pl.ANY)
VMEM = pl.BlockSpec(memory_space=pltpu.VMEM)
SMEM = pl.BlockSpec(memory_space=pltpu.SMEM)
CORE, X, Y, DIAGONAL = 1, 2, 4, 6
ORDER = (0, 2, 3, 1)


def over_dp(value, mask):
    return lax.ppermute(value, "dp", [(i, i ^ mask) for i in range(lax.axis_size("dp"))])


def over_expert(value, mask):
    return lax.ppermute(value, "expert", [(i, i ^ mask) for i in range(lax.axis_size("expert"))])


def ordered(body, operand_count, dep_count):
    def kernel(*refs):
        body(*refs[:operand_count], *refs[operand_count + dep_count :])

    return kernel


def call(body, name, shapes, operands, deps=(), specs=None, scratch=(), vmem=16, dtype=BF16):
    return pl.pallas_call(
        ordered(body, len(operands), len(deps)),
        out_shape=[jax.ShapeDtypeStruct(s, dtype) for s in shapes],
        in_specs=(specs or [VMEM] * len(operands)) + [ANY] * len(deps),
        out_specs=[VMEM] * len(shapes),
        scratch_shapes=list(scratch),
        compiler_params=pltpu.CompilerParams(vmem_limit_bytes=vmem << 20),
        cost_estimate=pl.CostEstimate(flops=0, bytes_accessed=0, transcendentals=0),
        name=name,
    )(*operands, *deps)


def slots_of(routes_ref, expert_count):
    row_count = routes_ref.shape[1]
    first, second = routes_ref[0:1, :], routes_ref[1:2, :]
    ids = lax.broadcasted_iota(jnp.int32, (8 * pl.cdiv(expert_count, 8), row_count), 0)
    named = (first == ids) | (second == ids)
    above = lax.broadcasted_iota(jnp.int32, (row_count, row_count), 0)
    below = lax.broadcasted_iota(jnp.int32, (row_count, row_count), 1)
    strict = (above < below).astype(F32).astype(BF16)
    earlier = jnp.dot(named.astype(F32).astype(BF16), strict, preferred_element_type=F32)
    return jnp.where(named, earlier.astype(jnp.int32), -1), ids


def dispatch_kernel(me_ref, routes_ref, tokens_ref, *out_refs):
    capacity = out_refs[0].shape[0]
    slots, ids = slots_of(routes_ref, len(out_refs))
    tokens = tokens_ref[...]
    slot_ids = lax.broadcasted_iota(jnp.int32, (capacity, tokens.shape[0]), 0)
    for j in range(len(out_refs)):
        mine = jnp.max(jnp.where(ids == me_ref[0] ^ j, slots, -1), axis=0, keepdims=True)
        placement = (slot_ids == mine).astype(F32).astype(BF16)
        out_refs[j][...] = jnp.dot(placement, tokens, preferred_element_type=F32).astype(BF16)


def mixing_kernel(me_ref, routes_ref, scores_ref, *out_refs):
    row_count, capacity = out_refs[0].shape
    slots, ids = slots_of(routes_ref, len(out_refs))
    scores = scores_ref[...].astype(F32)
    weights = scores / jnp.sum(scores, axis=0, keepdims=True)
    slot_ids = lax.broadcasted_iota(jnp.int32, (capacity, row_count), 0)
    for j in range(len(out_refs)):
        expert = me_ref[0] ^ j
        mine = jnp.max(jnp.where(ids == expert, slots, -1), axis=0, keepdims=True)
        weight = jnp.where(routes_ref[0:1, :] == expert, weights[0:1, :], weights[1:2, :])
        out_refs[j][...] = jnp.where(slot_ids == mine, weight, 0.0).T.astype(BF16)


def mixing(me, routes, scores, expert_count, capacity, deps=()):
    return call(
        mixing_kernel,
        "mixing",
        [(routes.shape[0], capacity)] * expert_count,
        [me, routes.T, scores.T],
        deps,
        specs=[SMEM, VMEM, VMEM],
    )


def combine_kernel(*refs):
    ins, out_ref = refs[:-1], refs[-1]
    total = ins[-1][...] if len(ins) % 2 else None
    for mix_ref, rows_ref in zip(ins[0:-1:2], ins[1::2]):
        part = jnp.dot(mix_ref[...], rows_ref[...], preferred_element_type=F32)
        total = part if total is None else total + part
    out_ref[...] = total.astype(out_ref.dtype)


def expert_kernel(me_ref, mine_ref, theirs_ref, gate_ref, up_ref, down_ref, keep_ref, *rest):
    me = me_ref[1]
    give_refs, hidden = rest[:-1], rest[-1]
    chips, _, width = mine_ref.shape
    units = hidden.shape[1]
    slots = [(ref, j, me ^ (2 * j + core)) for core, ref in enumerate((mine_ref, theirs_ref)) for j in range(chips)]
    for start in range(0, units, width):
        columns = slice(start, start + width)
        gate = up = None
        for ref, j, source in slots:
            rows = pl.ds(pl.multiple_of(source * width, width), width)
            x = ref[j]
            g = jnp.dot(x, gate_ref[rows, columns], preferred_element_type=F32)
            u = jnp.dot(x, up_ref[rows, columns], preferred_element_type=F32)
            gate = g if gate is None else gate + g
            up = u if up is None else up + u
        hidden[:, columns] = (gate / (1.0 + jnp.exp(-gate)) * up).astype(BF16)
    slots = [(ref, me ^ (2 * j + 1)) for j, ref in enumerate(give_refs)]
    slots += [(keep_ref.at[j], me ^ (2 * j)) for j in range(chips)]
    for ref, target in slots:
        columns = pl.ds(pl.multiple_of(target * width, width), width)
        ref[...] = jnp.dot(hidden[...], down_ref[:, columns], preferred_element_type=F32).astype(BF16)


def hub(name, outputs, deps=()):
    arrays = []
    for _, entries in outputs:
        for _, terms in entries:
            arrays += [array for array, _ in terms if not any(array is seen for seen in arrays)]
    position = {id(array): i for i, array in enumerate(arrays)}

    def body(*refs):
        for out_ref, (_, entries) in zip(refs[len(arrays) :], outputs):
            for place, terms in entries:
                values = [refs[position[id(array)]][at] for array, at in terms]
                if len(values) == 1:
                    out_ref[place] = values[0]
                else:
                    out_ref[place] = sum(v.astype(F32) for v in values).astype(BF16)

    return call(body, name, [shape for shape, _ in outputs], arrays, deps)


def load_kernel(gate_ref, up_ref, down_ref, new_gate_ref, new_up_ref, new_down_ref, sems):
    pairs = ((gate_ref, new_gate_ref), (up_ref, new_up_ref), (down_ref, new_down_ref))
    copies = [pltpu.make_async_copy(old, new, sems.at[i]) for i, (old, new) in enumerate(pairs)]
    for copy in copies:
        copy.start()
    for copy in copies:
        copy.wait()


def experts_by_chips(outgoing, weights, me, routes, scores):
    capacity, width = outgoing[0].shape
    units = weights[0].shape[1]
    half = capacity // 2
    top, bot = slice(0, half), slice(half, capacity)
    pieces = [outgoing[j] if j == 0 else over_expert(outgoing[j], j) for j in ORDER]
    count = len(pieces)
    from_x, from_y, relay_x, relay_y, sums_x, sums_y, last_x, last_y = ({} for _ in range(8))
    keep, got, mix, back = {}, {}, None, {}

    def both(c, j, rows, extra=()):
        return [(keep[c], (j, rows)), (got[c][j], rows), *extra]

    def send(steps):
        to_x, to_y, lands = [], [], []
        for kind, c in steps:
            at = len(to_x), len(to_y)
            if kind == "piece":
                to_x += [[(pieces[c], top)], [(pieces[c], bot)]]
                to_y += [[(pieces[c], top)], [(pieces[c], bot)]]
            elif kind == "relay":
                to_x += [[from_y[c][0]]]
                to_y += [[from_x[c][1]]]
            elif kind == "diagonal":
                to_x += [both(c, 3, top)]
                to_y += [both(c, 3, bot)]
            else:
                to_x += [both(c, 1, top), both(c, 1, bot, sums_y[c])]
                to_y += [both(c, 2, top, sums_x[c]), both(c, 2, bot)]
            lands.append((kind, c, *at, len(to_x)))
        return to_x, to_y, lands

    def land(lands, got_x, got_y):
        kinds = {
            "piece": (from_x, from_y),
            "relay": (relay_x, relay_y),
            "diagonal": (sums_x, sums_y),
            "near": (last_x, last_y),
        }
        for kind, c, at_x, at_y, end in lands:
            for store, array, at in zip(kinds[kind], (got_x, got_y), (at_x, at_y)):
                store[c] = [(array, i) for i in range(at, at + end - at_x)]

    def phase(name, steps, ready=None, results=(), deps=()):
        to_x, to_y, lands = send(steps)
        outputs = [((len(p), half, width), [(i, terms) for i, terms in enumerate(p)]) for p in (to_x, to_y) if p]
        if ready is not None:
            c = ready
            terms = [(0, top), (0, bot), (1, top), (1, bot), (2, top), (2, bot), (3, top), (3, bot)]
            views = [(pieces[c], top), (pieces[c], bot), *from_x[c], *from_y[c], *relay_x[c], *relay_y[c]]
            outputs.append(((4, capacity, width), [(place, [view]) for place, view in zip(terms, views)]))
        for c in results:
            rows = [
                (place, [*both(c, 0, place), last_x[c][i], last_y[c][i]]) for i, place in enumerate((top, bot))
            ]
            outputs.append(((capacity, width), rows))
        made = hub(name, outputs, deps)
        rest = made
        if to_x:
            land(lands, over_dp(made[0], X), over_dp(made[1], Y))
            rest = made[2:]
        if ready is not None:
            give_to = over_dp(rest[0], CORE)
            keep[ready], *give = call(
                expert_kernel,
                "expert",
                [(4, capacity, width)] + [(capacity, width)] * 4,
                [me, rest[0], give_to, *matrices],
                specs=[SMEM] + [VMEM] * 5,
                scratch=[pltpu.VMEM((capacity, units), BF16)],
            )
            got[ready] = [over_dp(array, CORE) for array in give]
            rest = rest[1:]
        for c, result in zip(results, rest):
            back[c] = over_expert(result, ORDER[c]) if ORDER[c] else result
        return made[0]

    land([("piece", 0, 0, 0, 2)], over_dp(pieces[0].reshape(2, half, width), X), over_dp(pieces[0].reshape(2, half, width), Y))
    matrices = call(
        load_kernel,
        "load",
        [w.shape for w in weights],
        [pltpu.with_memory_space_constraint(w, pltpu.HBM) for w in weights],
        (outgoing[0],),
        specs=[ANY] * 3,
        scratch=[pltpu.SemaphoreType.DMA((3,))],
    )
    made = phase("hub_b", [("relay", 0), ("piece", 1)], deps=(matrices[0],))
    mix = [mixing(me, routes, scores, count, capacity, (made,))[j] for j in ORDER]
    phase("hub_c", [("relay", 1), ("piece", 2)], ready=0, deps=(mix[0],))
    phase("hub_d", [("relay", 2), ("piece", 3)], ready=1, deps=(keep[0],))
    phase("hub_e", [("relay", 3), ("diagonal", 1)], ready=2)
    phase("hub_f", [("diagonal", 2), ("near", 1)], ready=3)
    phase("hub_g", [("diagonal", 3), ("diagonal", 0), ("near", 2)], results=(1,))
    acc = call(combine_kernel, "combine", [routes.shape[:1] + (width,)], [mix[1], back[1]], dtype=F32)[0]
    phase("hub_h", [("near", 3), ("near", 0)], results=(2,), deps=(acc,))
    acc = call(combine_kernel, "combine", [acc.shape], [mix[2], back[2], acc], dtype=F32)[0]
    phase("hub_i", [], results=(3, 0), deps=(acc,))
    acc = call(combine_kernel, "combine", [acc.shape], [mix[0], back[0], acc], dtype=F32)[0]
    return call(combine_kernel, "combine", [acc.shape], [mix[3], back[3], acc])[0]


def experts_by_axes(outgoing, weights):
    expert_count = lax.axis_size("expert")
    capacity, width = outgoing[0].shape
    me = lax.axis_index("expert")
    order = jnp.arange(expert_count) ^ me
    rows = jnp.stack(outgoing)[order]
    rows = lax.all_to_all(rows, "expert", split_axis=0, concat_axis=0, tiled=True)
    rows = lax.all_gather(rows.reshape(-1, width), "dp", axis=1, tiled=True)
    gate = jnp.dot(rows, weights[0], preferred_element_type=F32)
    up = jnp.dot(rows, weights[1], preferred_element_type=F32)
    hidden = (jax.nn.silu(gate) * up).astype(BF16)
    part = jnp.dot(hidden, weights[2], preferred_element_type=F32).astype(BF16)
    total = lax.psum_scatter(part, "dp", scatter_dimension=1, tiled=True)
    back = lax.all_to_all(
        total.reshape(expert_count, capacity, width), "expert", split_axis=0, concat_axis=0, tiled=True
    )[order]
    return [back[j] for j in range(expert_count)]


def shards(tokens, routes, scores, gate_weight, up_weight, down_weight):
    expert_count = lax.axis_size("expert")
    row_count = tokens.shape[0]
    capacity = 3 * row_count // expert_count
    me = jnp.stack([lax.axis_index("expert"), lax.axis_index("dp")]).astype(jnp.int32)
    weights = gate_weight[0], up_weight[0], down_weight[0]

    shape = (capacity, tokens.shape[1])
    outgoing = call(
        dispatch_kernel,
        "dispatch",
        [shape] * expert_count,
        [me, routes.T, tokens],
        specs=[SMEM, VMEM, VMEM],
    )
    if expert_count == 4 and lax.axis_size("dp") == 8:
        return experts_by_chips(outgoing, weights, me, routes, scores)
    mix = mixing(me, routes, scores, expert_count, capacity)
    results = experts_by_axes(outgoing, weights)
    pairs = [array for pair in zip(mix, results) for array in pair]
    return call(combine_kernel, "combine", [tokens.shape], pairs)[0]


def solution(mesh):
    return jax.shard_map(
        shards,
        mesh=mesh,
        in_specs=(
            P("expert", "dp"),
            P("expert", None),
            P("expert", None),
            P("expert", None, "dp"),
            P("expert", None, "dp"),
            P("expert", "dp", None),
        ),
        out_specs=P("expert", "dp"),
        check_vma=False,
    )
```

time: 133 us -> 103 us (0.77)
  waiting for transfers between devices: 59.5 us -> 28.7 us
  starting transfers between devices: 35.8 us -> 38.8 us
  local copies, waits for them, and re-layouts: 3.01 us -> 1.64 us
    ppermute x36, waiting for transfers between devices: 40.3 us -> 7.82 us  [over_dp(): lax.ppermute(value, 'dp', [(i, i ^ mask) for i in range(lax.axis_size('dp...]
    ppermute x6, starting transfers between devices: 12.7 us -> 16.6 us  [over_expert(): lax.ppermute(value, 'expert', [(i, i ^ mask) for i in range(lax.axis_size...]
    ppermute x6, waiting for transfers between devices: 19.2 us -> 20.9 us  [over_expert(): lax.ppermute(value, 'expert', [(i, i ^ mask) for i in range(lax.axis_size...]
    unnamed x8 -> x6, local copies, waits for them, and re-layouts: 3.01 us -> 1.64 us
    pallas_call x39 -> x19, Pallas kernels: 33 us -> 33.4 us  [call(): pl.pallas_call(ordered(body, len(operands), len(deps)), out_shape=[jax.Sh...]
  transfers between devices with their start and end apart: 42 -> 42, of which waited for: 18 -> 14; matrix products, arithmetic and copies ran while one was open for 0% -> 0% of each run, Pallas kernels for 23% -> 29%
where the time goes in v2:
time: 103 us
  starting transfers between devices  38.8 us (38%)
  Pallas kernels  33.4 us (32%)
  waiting for transfers between devices  28.7 us (28%)
  local copies, waits for them, and re-layouts  1.64 us (2%)
    pallas_call x19, Pallas kernels, call(): pl.pallas_call(ordered(body, len(operands), len(deps)), out_shape=[jax.Sh...  33.4 us
    ppermute x36, starting transfers between devices, over_dp(): lax.ppermute(value, 'dp', [(i, i ^ mask) for i in range(lax.axis_size('dp...  22.2 us
    ppermute x6, waiting for transfers between devices, over_expert(): lax.ppermute(value, 'expert', [(i, i ^ mask) for i in range(lax.axis_size...  20.9 us
    ppermute x6, starting transfers between devices, over_expert(): lax.ppermute(value, 'expert', [(i, i ^ mask) for i in range(lax.axis_size...  16.6 us
    ppermute x36, waiting for transfers between devices, over_dp(): lax.ppermute(value, 'dp', [(i, i ^ mask) for i in range(lax.axis_size('dp...  7.82 us
  transfers between devices with their start and end apart: 42, of which 14 were waited for; matrix products, arithmetic and copies ran while one was open for 0% of the time, Pallas kernels for 29%

profile of v2, /device:TPU:0, one launch (start us, length us, event | category | flops | bytes accessed | tf_op | source)
XLA Modules:
  0.0 102.9 jit_solution(7811605563412436045)
XLA Ops:
  3.0 4.1 %collective-permute-start.1 = (bf16[384,256]{1,0:T(8,128)(2,1)S(1)}, bf16[384,256]{1,0:T(8,128)(2,1)S(1)}, u32[]{:S(2)}, u32[]{:S(2)}) collective-permute-start(bf16[384,256]{1,0:T(8,128)(2,1)S(1)} %get-tuple-element.59), channel_id=1, source_target_pairs={{0,2},{1,3},{2,0},{3,1},{4,6},{5,7},{6,4},{7,5},{8,10},{9,11},{10,... | collective-permute-start | bytes 589832 | tf_op jit(solution)/shard_map/ppermute | solution.py:24
  7.1 1.5 %collective-permute-start.2 = (bf16[2,192,256]{2,1,0:T(8,128)(2,1)S(1)}, bf16[2,192,256]{2,1,0:T(8,128)(2,1)S(1)}, u32[]{:S(2)}, u32[]{:S(2)}) collective-permute-start(bf16[2,192,256]{2,1,0:T(8,128)(2,1)S(1)} %bitcast.8), channel_id=1, source_target_pairs={{0,8},{4,12},{8,0},{12,4},{16,24},{20,28},{24,16},{28,20},{1,9},{5... | collective-permute-start | bytes 589832 | tf_op jit(solution)/shard_map/ppermute | solution.py:20
  8.6 1.5 %collective-permute-start = (bf16[2,192,256]{2,1,0:T(8,128)(2,1)S(1)}, bf16[2,192,256]{2,1,0:T(8,128)(2,1)S(1)}, u32[]{:S(2)}, u32[]{:S(2)}) collective-permute-start(bf16[2,192,256]{2,1,0:T(8,128)(2,1)S(1)} %bitcast.9), channel_id=1, source_target_pairs={{0,16},{4,20},{8,24},{12,28},{16,0},{20,4},{24,8},{28,12},{1,17},{... | collective-permute-start | bytes 589832 | tf_op jit(solution)/shard_map/ppermute | solution.py:20
  10.1 4.7 %load.1 = (bf16[2048,1024]{1,0:T(8,128)(2,1)S(1)}, bf16[2048,1024]{1,0:T(8,128)(2,1)S(1)}, bf16[1024,2048]{1,0:T(8,128)(2,1)S(1)}) custom-call(bf16[2048,1024]{1,0:T(8,128)(2,1)} %bitcast.13, bf16[2048,1024]{1,0:T(8,128)(2,1)} %bitcast.14, bf16[1024,2048]{1,0:T(8,128)(2,1)} %bitcast.15, bf16[384,256]{1,0:T(8,128)(2,1)S(1)} %get-tuple-element.58.refs_3_), custom_call_target="tpu_custom_call" | custom-call | tf_op jit(solution)/shard_map/load/pallas_call | solution.py:35
  14.8 1.4 %collective-permute-done.1.refs_1_.refs_3_ = bf16[384,256]{1,0:T(8,128)(2,1)S(1)} collective-permute-done((bf16[384,256]{1,0:T(8,128)(2,1)S(1)}, bf16[384,256]{1,0:T(8,128)(2,1)S(1)}, u32[]{:S(2)}, u32[]{:S(2)}) %collective-permute-start.1) | collective-permute-done | bytes 196640 | tf_op jit(solution)/shard_map/ppermute | solution.py:24
  16.3 1.6 %collective-permute-start.3 = (bf16[3,192,256]{2,1,0:T(8,128)(2,1)S(1)}, bf16[3,192,256]{2,1,0:T(8,128)(2,1)S(1)}, u32[]{:S(2)}, u32[]{:S(2)}) collective-permute-start(bf16[3,192,256]{2,1,0:T(8,128)(2,1)S(1)} %get-tuple-element.63), channel_id=1, source_target_pairs={{0,16},{4,20},{8,24},{12,28},{16,0},{20,4},{24,8},{28,12},{1,17},{... | collective-permute-start | bytes 884744 | tf_op jit(solution)/shard_map/ppermute | solution.py:20
  17.9 1.5 %collective-permute-start.5 = (bf16[3,192,256]{2,1,0:T(8,128)(2,1)S(1)}, bf16[3,192,256]{2,1,0:T(8,128)(2,1)S(1)}, u32[]{:S(2)}, u32[]{:S(2)}) collective-permute-start(bf16[3,192,256]{2,1,0:T(8,128)(2,1)S(1)} %get-tuple-element.61.refs_3_), channel_id=1, source_target_pairs={{0,8},{4,12},{8,0},{12,4},{16,24},{20,28},{24,16},{28,20},{1,9},{5... | collective-permute-start | bytes 884744 | tf_op jit(solution)/shard_map/ppermute | solution.py:20
  19.4 3.5 %collective-permute-start.4 = (bf16[384,256]{1,0:T(8,128)(2,1)S(1)}, bf16[384,256]{1,0:T(8,128)(2,1)S(1)}, u32[]{:S(2)}, u32[]{:S(2)}) collective-permute-start(bf16[384,256]{1,0:T(8,128)(2,1)S(1)} %get-tuple-element.64), channel_id=1, source_target_pairs={{0,3},{1,2},{2,1},{3,0},{4,7},{5,6},{6,5},{7,4},{8,11},{9,10},{10,... | collective-permute-start | bytes 589832 | tf_op jit(solution)/shard_map/ppermute | solution.py:24
  24.2 3.3 %collective-permute-done.4.refs_1_.refs_4_ = bf16[384,256]{1,0:T(8,128)(2,1)S(1)} collective-permute-done((bf16[384,256]{1,0:T(8,128)(2,1)S(1)}, bf16[384,256]{1,0:T(8,128)(2,1)S(1)}, u32[]{:S(2)}, u32[]{:S(2)}) %collective-permute-start.4) | collective-permute-done | bytes 196640 | tf_op jit(solution)/shard_map/ppermute | solution.py:24
  28.8 3.0 %collective-permute-start.7 = (bf16[384,256]{1,0:T(8,128)(2,1)S(1)}, bf16[384,256]{1,0:T(8,128)(2,1)S(1)}, u32[]{:S(2)}, u32[]{:S(2)}) collective-permute-start(bf16[384,256]{1,0:T(8,128)(2,1)S(1)} %get-tuple-element.67), channel_id=1, source_target_pairs={{0,1},{1,0},{2,3},{3,2},{4,5},{5,4},{6,7},{7,6},{8,9},{9,8},{10,11... | collective-permute-start | bytes 589832 | tf_op jit(solution)/shard_map/ppermute | solution.py:24
  31.8 5.7 %expert.4 = (bf16[4,384,256]{2,1,0:T(8,128)(2,1)S(1)}, bf16[384,256]{1,0:T(8,128)(2,1)S(1)}, bf16[384,256]{1,0:T(8,128)(2,1)S(1)}, bf16[384,256]{1,0:T(8,128)(2,1)S(1)}, bf16[384,256]{1,0:T(8,128)(2,1)S(1)}) custom-call(s32[2]{0:T(128)S(1)} %pad_add_fusion.refs_0_, bf16[4,384,256]{2,1,0:T(8,128)(2,1)S(1)} %get-tuple-element.69.refs_1_, ...), custom_call_target="tpu_custom_call" | custom-call | tf_op jit(solution)/shard_map/expert/pallas_call | solution.py:35
  37.7 1.6 %collective-permute-start.10 = (bf16[3,192,256]{2,1,0:T(8,128)(2,1)S(1)}, bf16[3,192,256]{2,1,0:T(8,128)(2,1)S(1)}, u32[]{:S(2)}, u32[]{:S(2)}) collective-permute-start(bf16[3,192,256]{2,1,0:T(8,128)(2,1)S(1)} %get-tuple-element.73), channel_id=1, source_target_pairs={{0,16},{4,20},{8,24},{12,28},{16,0},{20,4},{24,8},{28,12},{1,17},{... | collective-permute-start | bytes 884744 | tf_op jit(solution)/shard_map/ppermute | solution.py:20
  39.3 1.5 %collective-permute-start.13 = (bf16[3,192,256]{2,1,0:T(8,128)(2,1)S(1)}, bf16[3,192,256]{2,1,0:T(8,128)(2,1)S(1)}, u32[]{:S(2)}, u32[]{:S(2)}) collective-permute-start(bf16[3,192,256]{2,1,0:T(8,128)(2,1)S(1)} %get-tuple-element.77), channel_id=1, source_target_pairs={{0,8},{4,12},{8,0},{12,4},{16,24},{20,28},{24,16},{28,20},{1,9},{5... | collective-permute-start | bytes 884744 | tf_op jit(solution)/shard_map/ppermute | solution.py:20
  40.8 5.7 %expert.5 = (bf16[4,384,256]{2,1,0:T(8,128)(2,1)S(1)}, bf16[384,256]{1,0:T(8,128)(2,1)S(1)}, bf16[384,256]{1,0:T(8,128)(2,1)S(1)}, bf16[384,256]{1,0:T(8,128)(2,1)S(1)}, bf16[384,256]{1,0:T(8,128)(2,1)S(1)}) custom-call(s32[2]{0:T(128)S(1)} %pad_add_fusion.refs_0_, bf16[4,384,256]{2,1,0:T(8,128)(2,1)S(1)} %get-tuple-element.74.refs_1_, ...), custom_call_target="tpu_custom_call" | custom-call | tf_op jit(solution)/shard_map/expert/pallas_call | solution.py:35
  49.7 1.5 %collective-permute-start.19 = (bf16[2,192,256]{2,1,0:T(8,128)(2,1)S(1)}, bf16[2,192,256]{2,1,0:T(8,128)(2,1)S(1)}, u32[]{:S(2)}, u32[]{:S(2)}) collective-permute-start(bf16[2,192,256]{2,1,0:T(8,128)(2,1)S(1)} %get-tuple-element.84), channel_id=1, source_target_pairs={{0,8},{4,12},{8,0},{12,4},{16,24},{20,28},{24,16},{28,20},{1,9},{5... | collective-permute-start | bytes 589832 | tf_op jit(solution)/shard_map/ppermute | solution.py:20
  51.2 5.9 %expert.6 = (bf16[4,384,256]{2,1,0:T(8,128)(2,1)S(1)}, bf16[384,256]{1,0:T(8,128)(2,1)S(1)}, bf16[384,256]{1,0:T(8,128)(2,1)S(1)}, bf16[384,256]{1,0:T(8,128)(2,1)S(1)}, bf16[384,256]{1,0:T(8,128)(2,1)S(1)}) custom-call(s32[2]{0:T(128)S(1)} %pad_add_fusion.refs_0_, bf16[4,384,256]{2,1,0:T(8,128)(2,1)S(1)} %get-tuple-element.78.refs_1_, ...), custom_call_target="tpu_custom_call" | custom-call | tf_op jit(solution)/shard_map/expert/pallas_call | solution.py:35
  59.5 1.5 %collective-permute-start.26 = (bf16[3,192,256]{2,1,0:T(8,128)(2,1)S(1)}, bf16[3,192,256]{2,1,0:T(8,128)(2,1)S(1)}, u32[]{:S(2)}, u32[]{:S(2)}) collective-permute-start(bf16[3,192,256]{2,1,0:T(8,128)(2,1)S(1)} %get-tuple-element.92), channel_id=1, source_target_pairs={{0,16},{4,20},{8,24},{12,28},{16,0},{20,4},{24,8},{28,12},{1,17},{... | collective-permute-start | bytes 884744 | tf_op jit(solution)/shard_map/ppermute | solution.py:20
  62.0 5.7 %expert.7 = (bf16[4,384,256]{2,1,0:T(8,128)(2,1)S(1)}, bf16[384,256]{1,0:T(8,128)(2,1)S(1)}, bf16[384,256]{1,0:T(8,128)(2,1)S(1)}, bf16[384,256]{1,0:T(8,128)(2,1)S(1)}, bf16[384,256]{1,0:T(8,128)(2,1)S(1)}) custom-call(s32[2]{0:T(128)S(1)} %pad_add_fusion.refs_0_, bf16[4,384,256]{2,1,0:T(8,128)(2,1)S(1)} %get-tuple-element.85.refs_1_, ...), custom_call_target="tpu_custom_call" | custom-call | tf_op jit(solution)/shard_map/expert/pallas_call | solution.py:35
  70.3 1.9 %collective-permute-start.36 = (bf16[384,256]{1,0:T(8,128)(2,1)S(1)}, bf16[384,256]{1,0:T(8,128)(2,1)S(1)}, u32[]{:S(2)}, u32[]{:S(2)}) collective-permute-start(bf16[384,256]{1,0:T(8,128)(2,1)S(1)} %get-tuple-element.103), channel_id=1, source_target_pairs={{0,2},{1,3},{2,0},{3,1},{4,6},{5,7},{6,4},{7,5},{8,10},{9,11},{10,... | collective-permute-start | bytes 589832 | tf_op jit(solution)/shard_map/ppermute | solution.py:24
  74.6 7.1 %collective-permute-done.36.refs_1_ = bf16[384,256]{1,0:T(8,128)(2,1)S(1)} collective-permute-done((bf16[384,256]{1,0:T(8,128)(2,1)S(1)}, bf16[384,256]{1,0:T(8,128)(2,1)S(1)}, u32[]{:S(2)}, u32[]{:S(2)}) %collective-permute-start.36) | collective-permute-done | bytes 196640 | tf_op jit(solution)/shard_map/ppermute | solution.py:24
  83.6 1.5 %collective-permute-start.37 = (bf16[4,192,256]{2,1,0:T(8,128)(2,1)S(1)}, bf16[4,192,256]{2,1,0:T(8,128)(2,1)S(1)}, u32[]{:S(2)}, u32[]{:S(2)}) collective-permute-start(bf16[4,192,256]{2,1,0:T(8,128)(2,1)S(1)} %get-tuple-element.104), channel_id=1, source_target_pairs={{0,8},{4,12},{8,0},{12,4},{16,24},{20,28},{24,16},{28,20},{1,9},{5... | collective-permute-start | bytes 1179656 | tf_op jit(solution)/shard_map/ppermute | solution.py:20
  85.7 3.0 %collective-permute-start.40 = (bf16[384,256]{1,0:T(8,128)(2,1)S(1)}, bf16[384,256]{1,0:T(8,128)(2,1)S(1)}, u32[]{:S(2)}, u32[]{:S(2)}) collective-permute-start(bf16[384,256]{1,0:T(8,128)(2,1)S(1)} %get-tuple-element.108), channel_id=1, source_target_pairs={{0,3},{1,2},{2,1},{3,0},{4,7},{5,6},{6,5},{7,4},{8,11},{9,10},{10,... | collective-permute-start | bytes 589832 | tf_op jit(solution)/shard_map/ppermute | solution.py:24
  89.3 4.6 %collective-permute-done.40.refs_1_ = bf16[384,256]{1,0:T(8,128)(2,1)S(1)} collective-permute-done((bf16[384,256]{1,0:T(8,128)(2,1)S(1)}, bf16[384,256]{1,0:T(8,128)(2,1)S(1)}, u32[]{:S(2)}, u32[]{:S(2)}) %collective-permute-start.40) | collective-permute-done | bytes 196640 | tf_op jit(solution)/shard_map/ppermute | solution.py:24
  97.4 4.5 %collective-permute-done.41.refs_1_ = bf16[384,256]{1,0:T(8,128)(2,1)S(1)} collective-permute-done((bf16[384,256]{1,0:T(8,128)(2,1)S(1)}, bf16[384,256]{1,0:T(8,128)(2,1)S(1)}, u32[]{:S(2)}, u32[]{:S(2)}) %collective-permute-start.41) | collective-permute-done | bytes 196640 | tf_op jit(solution)/shard_map/ppermute | solution.py:24
  (86 shorter events, 24.9 us)
Async XLA Ops:
  3.0 13.2 %collective-permute-start.1 = (bf16[384,256]{1,0:T(8,128)(2,1)S(1)}, bf16[384,256]{1,0:T(8,128)(2,1)S(1)}, u32[]{:S(2)}, u32[]{:S(2)}) collective-permute-start(bf16[384,256]{1,0:T(8,128)(2,1)S(1)} %get-tuple-element.59), channel_id=1, source_target_pairs={{0,2},{1,3},{2,0},{3,1},{4,6},{5,7},{6,4},{7,5},{8,10},{9,11},{10,... | collective-permute-start | bytes 589832 | tf_op jit(solution)/shard_map/ppermute | solution.py:24
  7.1 9.1 %collective-permute-start.2 = (bf16[2,192,256]{2,1,0:T(8,128)(2,1)S(1)}, bf16[2,192,256]{2,1,0:T(8,128)(2,1)S(1)}, u32[]{:S(2)}, u32[]{:S(2)}) collective-permute-start(bf16[2,192,256]{2,1,0:T(8,128)(2,1)S(1)} %bitcast.8), channel_id=1, source_target_pairs={{0,8},{4,12},{8,0},{12,4},{16,24},{20,28},{24,16},{28,20},{1,9},{5... | collective-permute-start | bytes 589832 | tf_op jit(solution)/shard_map/ppermute | solution.py:20
  16.3 11.2 %collective-permute-start.3 = (bf16[3,192,256]{2,1,0:T(8,128)(2,1)S(1)}, bf16[3,192,256]{2,1,0:T(8,128)(2,1)S(1)}, u32[]{:S(2)}, u32[]{:S(2)}) collective-permute-start(bf16[3,192,256]{2,1,0:T(8,128)(2,1)S(1)} %get-tuple-element.63), channel_id=1, source_target_pairs={{0,16},{4,20},{8,24},{12,28},{16,0},{20,4},{24,8},{28,12},{1,17},{... | collective-permute-start | bytes 884744 | tf_op jit(solution)/shard_map/ppermute | solution.py:20
  17.9 9.6 %collective-permute-start.5 = (bf16[3,192,256]{2,1,0:T(8,128)(2,1)S(1)}, bf16[3,192,256]{2,1,0:T(8,128)(2,1)S(1)}, u32[]{:S(2)}, u32[]{:S(2)}) collective-permute-start(bf16[3,192,256]{2,1,0:T(8,128)(2,1)S(1)} %get-tuple-element.61.refs_3_), channel_id=1, source_target_pairs={{0,8},{4,12},{8,0},{12,4},{16,24},{20,28},{24,16},{28,20},{1,9},{5... | collective-permute-start | bytes 884744 | tf_op jit(solution)/shard_map/ppermute | solution.py:20
  19.4 8.1 %collective-permute-start.4 = (bf16[384,256]{1,0:T(8,128)(2,1)S(1)}, bf16[384,256]{1,0:T(8,128)(2,1)S(1)}, u32[]{:S(2)}, u32[]{:S(2)}) collective-permute-start(bf16[384,256]{1,0:T(8,128)(2,1)S(1)} %get-tuple-element.64), channel_id=1, source_target_pairs={{0,3},{1,2},{2,1},{3,0},{4,7},{5,6},{6,5},{7,4},{8,11},{9,10},{10,... | collective-permute-start | bytes 589832 | tf_op jit(solution)/shard_map/ppermute | solution.py:24
  27.7 9.9 %collective-permute-start.6 = (bf16[3,192,256]{2,1,0:T(8,128)(2,1)S(1)}, bf16[3,192,256]{2,1,0:T(8,128)(2,1)S(1)}, u32[]{:S(2)}, u32[]{:S(2)}) collective-permute-start(bf16[3,192,256]{2,1,0:T(8,128)(2,1)S(1)} %get-tuple-element.66), channel_id=1, source_target_pairs={{0,16},{4,20},{8,24},{12,28},{16,0},{20,4},{24,8},{28,12},{1,17},{... | collective-permute-start | bytes 884744 | tf_op jit(solution)/shard_map/ppermute | solution.py:20
  28.2 9.3 %collective-permute-start.8 = (bf16[3,192,256]{2,1,0:T(8,128)(2,1)S(1)}, bf16[3,192,256]{2,1,0:T(8,128)(2,1)S(1)}, u32[]{:S(2)}, u32[]{:S(2)}) collective-permute-start(bf16[3,192,256]{2,1,0:T(8,128)(2,1)S(1)} %get-tuple-element.68), channel_id=1, source_target_pairs={{0,8},{4,12},{8,0},{12,4},{16,24},{20,28},{24,16},{28,20},{1,9},{5... | collective-permute-start | bytes 884744 | tf_op jit(solution)/shard_map/ppermute | solution.py:20
  28.8 8.7 %collective-permute-start.7 = (bf16[384,256]{1,0:T(8,128)(2,1)S(1)}, bf16[384,256]{1,0:T(8,128)(2,1)S(1)}, u32[]{:S(2)}, u32[]{:S(2)}) collective-permute-start(bf16[384,256]{1,0:T(8,128)(2,1)S(1)} %get-tuple-element.67), channel_id=1, source_target_pairs={{0,1},{1,0},{2,3},{3,2},{4,5},{5,4},{6,7},{7,6},{8,9},{9,8},{10,11... | collective-permute-start | bytes 589832 | tf_op jit(solution)/shard_map/ppermute | solution.py:24
  37.7 9.4 %collective-permute-start.10 = (bf16[3,192,256]{2,1,0:T(8,128)(2,1)S(1)}, bf16[3,192,256]{2,1,0:T(8,128)(2,1)S(1)}, u32[]{:S(2)}, u32[]{:S(2)}) collective-permute-start(bf16[3,192,256]{2,1,0:T(8,128)(2,1)S(1)} %get-tuple-element.73), channel_id=1, source_target_pairs={{0,16},{4,20},{8,24},{12,28},{16,0},{20,4},{24,8},{28,12},{1,17},{... | collective-permute-start | bytes 884744 | tf_op jit(solution)/shard_map/ppermute | solution.py:20
  39.3 9.1 %collective-permute-start.13 = (bf16[3,192,256]{2,1,0:T(8,128)(2,1)S(1)}, bf16[3,192,256]{2,1,0:T(8,128)(2,1)S(1)}, u32[]{:S(2)}, u32[]{:S(2)}) collective-permute-start(bf16[3,192,256]{2,1,0:T(8,128)(2,1)S(1)} %get-tuple-element.77), channel_id=1, source_target_pairs={{0,8},{4,12},{8,0},{12,4},{16,24},{20,28},{24,16},{28,20},{1,9},{5... | collective-permute-start | bytes 884744 | tf_op jit(solution)/shard_map/ppermute | solution.py:20
  48.6 8.5 %collective-permute-start.16 = (bf16[384,256]{1,0:T(8,128)(2,1)S(1)}, bf16[384,256]{1,0:T(8,128)(2,1)S(1)}, u32[]{:S(2)}, u32[]{:S(2)}) collective-permute-start(bf16[384,256]{1,0:T(8,128)(2,1)S(1)} %get-tuple-element.81), channel_id=1, source_target_pairs={{0,4},{4,0},{8,12},{12,8},{16,20},{20,16},{24,28},{28,24},{1,5},{5... | collective-permute-start | bytes 589832 | tf_op jit(solution)/shard_map/ppermute | solution.py:20
  49.1 8.1 %collective-permute-start.18 = (bf16[384,256]{1,0:T(8,128)(2,1)S(1)}, bf16[384,256]{1,0:T(8,128)(2,1)S(1)}, u32[]{:S(2)}, u32[]{:S(2)}) collective-permute-start(bf16[384,256]{1,0:T(8,128)(2,1)S(1)} %get-tuple-element.83), channel_id=1, source_target_pairs={{0,4},{4,0},{8,12},{12,8},{16,20},{20,16},{24,28},{28,24},{1,5},{5... | collective-permute-start | bytes 589832 | tf_op jit(solution)/shard_map/ppermute | solution.py:20
  49.2 8.0 %collective-permute-start.17 = (bf16[2,192,256]{2,1,0:T(8,128)(2,1)S(1)}, bf16[2,192,256]{2,1,0:T(8,128)(2,1)S(1)}, u32[]{:S(2)}, u32[]{:S(2)}) collective-permute-start(bf16[2,192,256]{2,1,0:T(8,128)(2,1)S(1)} %get-tuple-element.82), channel_id=1, source_target_pairs={{0,16},{4,20},{8,24},{12,28},{16,0},{20,4},{24,8},{28,12},{1,17},{... | collective-permute-start | bytes 589832 | tf_op jit(solution)/shard_map/ppermute | solution.py:20
  59.3 8.4 %collective-permute-start.29 = (bf16[384,256]{1,0:T(8,128)(2,1)S(1)}, bf16[384,256]{1,0:T(8,128)(2,1)S(1)}, u32[]{:S(2)}, u32[]{:S(2)}) collective-permute-start(bf16[384,256]{1,0:T(8,128)(2,1)S(1)} %get-tuple-element.95), channel_id=1, source_target_pairs={{0,4},{4,0},{8,12},{12,8},{16,20},{20,16},{24,28},{28,24},{1,5},{5... | collective-permute-start | bytes 589832 | tf_op jit(solution)/shard_map/ppermute | solution.py:20
  59.5 9.3 %collective-permute-start.26 = (bf16[3,192,256]{2,1,0:T(8,128)(2,1)S(1)}, bf16[3,192,256]{2,1,0:T(8,128)(2,1)S(1)}, u32[]{:S(2)}, u32[]{:S(2)}) collective-permute-start(bf16[3,192,256]{2,1,0:T(8,128)(2,1)S(1)} %get-tuple-element.92), channel_id=1, source_target_pairs={{0,16},{4,20},{8,24},{12,28},{16,0},{20,4},{24,8},{28,12},{1,17},{... | collective-permute-start | bytes 884744 | tf_op jit(solution)/shard_map/ppermute | solution.py:20
  61.0 9.0 %collective-permute-start.28 = (bf16[3,192,256]{2,1,0:T(8,128)(2,1)S(1)}, bf16[3,192,256]{2,1,0:T(8,128)(2,1)S(1)}, u32[]{:S(2)}, u32[]{:S(2)}) collective-permute-start(bf16[3,192,256]{2,1,0:T(8,128)(2,1)S(1)} %get-tuple-element.94), channel_id=1, source_target_pairs={{0,8},{4,12},{8,0},{12,4},{16,24},{20,28},{24,16},{28,20},{1,9},{5... | collective-permute-start | bytes 884744 | tf_op jit(solution)/shard_map/ppermute | solution.py:20
  70.3 11.4 %collective-permute-start.36 = (bf16[384,256]{1,0:T(8,128)(2,1)S(1)}, bf16[384,256]{1,0:T(8,128)(2,1)S(1)}, u32[]{:S(2)}, u32[]{:S(2)}) collective-permute-start(bf16[384,256]{1,0:T(8,128)(2,1)S(1)} %get-tuple-element.103), channel_id=1, source_target_pairs={{0,2},{1,3},{2,0},{3,1},{4,6},{5,7},{6,4},{7,5},{8,10},{9,11},{10,... | collective-permute-start | bytes 589832 | tf_op jit(solution)/shard_map/ppermute | solution.py:24
  72.2 11.0 %collective-permute-start.30 = (bf16[4,192,256]{2,1,0:T(8,128)(2,1)S(1)}, bf16[4,192,256]{2,1,0:T(8,128)(2,1)S(1)}, u32[]{:S(2)}, u32[]{:S(2)}) collective-permute-start(bf16[4,192,256]{2,1,0:T(8,128)(2,1)S(1)} %get-tuple-element.96), channel_id=1, source_target_pairs={{0,16},{4,20},{8,24},{12,28},{16,0},{20,4},{24,8},{28,12},{1,17},{... | collective-permute-start | bytes 1179656 | tf_op jit(solution)/shard_map/ppermute | solution.py:20
  73.1 10.2 %collective-permute-start.33 = (bf16[4,192,256]{2,1,0:T(8,128)(2,1)S(1)}, bf16[4,192,256]{2,1,0:T(8,128)(2,1)S(1)}, u32[]{:S(2)}, u32[]{:S(2)}) collective-permute-start(bf16[4,192,256]{2,1,0:T(8,128)(2,1)S(1)} %get-tuple-element.99), channel_id=1, source_target_pairs={{0,8},{4,12},{8,0},{12,4},{16,24},{20,28},{24,16},{28,20},{1,9},{5... | collective-permute-start | bytes 1179656 | tf_op jit(solution)/shard_map/ppermute | solution.py:20
  74.1 7.9 %collective-permute-start.35 = (bf16[384,256]{1,0:T(8,128)(2,1)S(1)}, bf16[384,256]{1,0:T(8,128)(2,1)S(1)}, u32[]{:S(2)}, u32[]{:S(2)}) collective-permute-start(bf16[384,256]{1,0:T(8,128)(2,1)S(1)} %get-tuple-element.101), channel_id=1, source_target_pairs={{0,4},{4,0},{8,12},{12,8},{16,20},{20,16},{24,28},{28,24},{1,5},{5... | collective-permute-start | bytes 589832 | tf_op jit(solution)/shard_map/ppermute | solution.py:20
  74.1 7.9 %collective-permute-start.22 = (bf16[384,256]{1,0:T(8,128)(2,1)S(1)}, bf16[384,256]{1,0:T(8,128)(2,1)S(1)}, u32[]{:S(2)}, u32[]{:S(2)}) collective-permute-start(bf16[384,256]{1,0:T(8,128)(2,1)S(1)} %get-tuple-element.88), channel_id=1, source_target_pairs={{0,4},{4,0},{8,12},{12,8},{16,20},{20,16},{24,28},{28,24},{1,5},{5... | collective-permute-start | bytes 589832 | tf_op jit(solution)/shard_map/ppermute | solution.py:20
  83.6 11.1 %collective-permute-start.37 = (bf16[4,192,256]{2,1,0:T(8,128)(2,1)S(1)}, bf16[4,192,256]{2,1,0:T(8,128)(2,1)S(1)}, u32[]{:S(2)}, u32[]{:S(2)}) collective-permute-start(bf16[4,192,256]{2,1,0:T(8,128)(2,1)S(1)} %get-tuple-element.104), channel_id=1, source_target_pairs={{0,8},{4,12},{8,0},{12,4},{16,24},{20,28},{24,16},{28,20},{1,9},{5... | collective-permute-start | bytes 1179656 | tf_op jit(solution)/shard_map/ppermute | solution.py:20
  85.1 10.9 %collective-permute-start.38 = (bf16[4,192,256]{2,1,0:T(8,128)(2,1)S(1)}, bf16[4,192,256]{2,1,0:T(8,128)(2,1)S(1)}, u32[]{:S(2)}, u32[]{:S(2)}) collective-permute-start(bf16[4,192,256]{2,1,0:T(8,128)(2,1)S(1)} %get-tuple-element.105), channel_id=1, source_target_pairs={{0,16},{4,20},{8,24},{12,28},{16,0},{20,4},{24,8},{28,12},{1,17},{... | collective-permute-start | bytes 1179656 | tf_op jit(solution)/shard_map/ppermute | solution.py:20
  85.7 8.1 %collective-permute-start.40 = (bf16[384,256]{1,0:T(8,128)(2,1)S(1)}, bf16[384,256]{1,0:T(8,128)(2,1)S(1)}, u32[]{:S(2)}, u32[]{:S(2)}) collective-permute-start(bf16[384,256]{1,0:T(8,128)(2,1)S(1)} %get-tuple-element.108), channel_id=1, source_target_pairs={{0,3},{1,2},{2,1},{3,0},{4,7},{5,6},{6,5},{7,4},{8,11},{9,10},{10,... | collective-permute-start | bytes 589832 | tf_op jit(solution)/shard_map/ppermute | solution.py:24
  (21 other events, 89.0 us)

commit v3 on v2

--- a/solution.py
+++ b/solution.py
@@ -11,13 +11,17 @@
 BF16 = jnp.bfloat16
 ANY = pl.BlockSpec(memory_space=pl.ANY)
 VMEM = pl.BlockSpec(memory_space=pltpu.VMEM)
-SMEM = pl.BlockSpec(memory_space=pltpu.SMEM)
 CORE, X, Y, DIAGONAL = 1, 2, 4, 6
+PAD = 16
 ORDER = (0, 2, 3, 1)
 
 
-def over_dp(value, mask):
-    return lax.ppermute(value, "dp", [(i, i ^ mask) for i in range(lax.axis_size("dp"))])
+def over_core(value):
+    return lax.ppermute(value, "dp", [(i, i ^ CORE) for i in range(lax.axis_size("dp"))])
+
+
+def over_links(value, even, odd):
+    return lax.ppermute(value, "dp", [(i, i ^ (odd if i & 1 else even)) for i in range(lax.axis_size("dp"))])
 
 
 def over_expert(value, mask):
@@ -56,38 +60,48 @@
     return jnp.where(named, earlier.astype(jnp.int32), -1), ids
 
 
-def dispatch_kernel(me_ref, routes_ref, tokens_ref, *out_refs):
+def dispatch_kernel(routes_hbm, tokens_hbm, *refs):
+    *out_refs, routes_ref, tokens_ref, sems = refs
+    loads = [
+        pltpu.make_async_copy(routes_hbm, routes_ref, sems.at[0]),
+        pltpu.make_async_copy(tokens_hbm, tokens_ref, sems.at[1]),
+    ]
+    for load in loads:
+        load.start()
     capacity = out_refs[0].shape[0]
+    me = lax.axis_index("expert")
+    loads[0].wait()
     slots, ids = slots_of(routes_ref, len(out_refs))
+    slot_ids = lax.broadcasted_iota(jnp.int32, (capacity, tokens_ref.shape[0]), 0)
+    loads[1].wait()
     tokens = tokens_ref[...]
-    slot_ids = lax.broadcasted_iota(jnp.int32, (capacity, tokens.shape[0]), 0)
     for j in range(len(out_refs)):
-        mine = jnp.max(jnp.where(ids == me_ref[0] ^ j, slots, -1), axis=0, keepdims=True)
+        mine = jnp.max(jnp.where(ids == me ^ j, slots, -1), axis=0, keepdims=True)
         placement = (slot_ids == mine).astype(F32).astype(BF16)
         out_refs[j][...] = jnp.dot(placement, tokens, preferred_element_type=F32).astype(BF16)
 
 
-def mixing_kernel(me_ref, routes_ref, scores_ref, *out_refs):
+def mixing_kernel(routes_ref, scores_ref, *out_refs):
+    me = lax.axis_index("expert")
     row_count, capacity = out_refs[0].shape
     slots, ids = slots_of(routes_ref, len(out_refs))
     scores = scores_ref[...].astype(F32)
     weights = scores / jnp.sum(scores, axis=0, keepdims=True)
     slot_ids = lax.broadcasted_iota(jnp.int32, (capacity, row_count), 0)
     for j in range(len(out_refs)):
-        expert = me_ref[0] ^ j
+        expert = me ^ j
         mine = jnp.max(jnp.where(ids == expert, slots, -1), axis=0, keepdims=True)
         weight = jnp.where(routes_ref[0:1, :] == expert, weights[0:1, :], weights[1:2, :])
         out_refs[j][...] = jnp.where(slot_ids == mine, weight, 0.0).T.astype(BF16)
 
 
-def mixing(me, routes, scores, expert_count, capacity, deps=()):
+def mixing(routes, scores, expert_count, capacity, deps=()):
     return call(
         mixing_kernel,
         "mixing",
         [(routes.shape[0], capacity)] * expert_count,
-        [me, routes.T, scores.T],
+        [routes.T, scores.T],
         deps,
-        specs=[SMEM, VMEM, VMEM],
     )
 
 
@@ -95,13 +109,13 @@
     ins, out_ref = refs[:-1], refs[-1]
     total = ins[-1][...] if len(ins) % 2 else None
     for mix_ref, rows_ref in zip(ins[0:-1:2], ins[1::2]):
-        part = jnp.dot(mix_ref[...], rows_ref[...], preferred_element_type=F32)
+        part = jnp.dot(mix_ref[...], rows_ref[: mix_ref.shape[1]], preferred_element_type=F32)
         total = part if total is None else total + part
     out_ref[...] = total.astype(out_ref.dtype)
 
 
-def expert_kernel(me_ref, mine_ref, theirs_ref, gate_ref, up_ref, down_ref, keep_ref, *rest):
-    me = me_ref[1]
+def expert_kernel(mine_ref, theirs_ref, gate_ref, up_ref, down_ref, keep_ref, *rest):
+    me = lax.axis_index("dp")
     give_refs, hidden = rest[:-1], rest[-1]
     chips, _, width = mine_ref.shape
     units = hidden.shape[1]
@@ -124,23 +138,43 @@
         ref[...] = jnp.dot(hidden[...], down_ref[:, columns], preferred_element_type=F32).astype(BF16)
 
 
+class Crossed:
+    def __init__(self, first, second, axis):
+        self.by_core = (first, second) if axis == X else (second, first)
+
+
 def hub(name, outputs, deps=()):
     arrays = []
-    for _, entries in outputs:
-        for _, terms in entries:
-            arrays += [array for array, _ in terms if not any(array is seen for seen in arrays)]
-    position = {id(array): i for i, array in enumerate(arrays)}
+
+    def position(array):
+        for i, seen in enumerate(arrays):
+            if seen is array:
+                return i
+        arrays.append(array)
+        return len(arrays) - 1
+
+    plans = []
+    for core in (0, 1):
+        plan = []
+        for number, (_, *entries) in enumerate(outputs):
+            for place, terms in entries[core % len(entries)]:
+                terms = [(a.by_core[core] if isinstance(a, Crossed) else a, at) for a, at in terms]
+                plan.append((number, place, [(position(a), at) for a, at in terms]))
+        plans.append(plan)
 
     def body(*refs):
-        for out_ref, (_, entries) in zip(refs[len(arrays) :], outputs):
-            for place, terms in entries:
-                values = [refs[position[id(array)]][at] for array, at in terms]
-                if len(values) == 1:
-                    out_ref[place] = values[0]
-                else:
-                    out_ref[place] = sum(v.astype(F32) for v in values).astype(BF16)
-
-    return call(body, name, [shape for shape, _ in outputs], arrays, deps)
+        def run(plan):
+            for number, place, terms in plan:
+                values = [refs[i][at] for i, at in terms]
+                value = values[0] if len(values) == 1 else sum(v.astype(F32) for v in values).astype(BF16)
+                refs[len(arrays) + number][place] = value
+
+        core = lax.axis_index("dp") & 1
+        for parity in (0, 1):
+            pl.when(core == parity)(functools.partial(run, plans[parity]))
+
+    shapes = [shape for shape, *_ in outputs]
+    return call(body, name, shapes, arrays, deps)
 
 
 def load_kernel(gate_ref, up_ref, down_ref, new_gate_ref, new_up_ref, new_down_ref, sems):
@@ -152,11 +186,12 @@
         copy.wait()
 
 
-def experts_by_chips(outgoing, weights, me, routes, scores):
+def experts_by_chips(outgoing, weights, routes, scores):
     capacity, width = outgoing[0].shape
     units = weights[0].shape[1]
     half = capacity // 2
     top, bot = slice(0, half), slice(half, capacity)
+    rows_at = top
     pieces = [outgoing[j] if j == 0 else over_expert(outgoing[j], j) for j in ORDER]
     count = len(pieces)
     from_x, from_y, relay_x, relay_y, sums_x, sums_y, last_x, last_y = ({} for _ in range(8))
@@ -184,7 +219,7 @@
             lands.append((kind, c, *at, len(to_x)))
         return to_x, to_y, lands
 
-    def land(lands, got_x, got_y):
+    def land(lands, first, second):
         kinds = {
             "piece": (from_x, from_y),
             "relay": (relay_x, relay_y),
@@ -192,12 +227,22 @@
             "near": (last_x, last_y),
         }
         for kind, c, at_x, at_y, end in lands:
-            for store, array, at in zip(kinds[kind], (got_x, got_y), (at_x, at_y)):
-                store[c] = [(array, i) for i in range(at, at + end - at_x)]
-
-    def phase(name, steps, ready=None, results=(), deps=()):
-        to_x, to_y, lands = send(steps)
-        outputs = [((len(p), half, width), [(i, terms) for i, terms in enumerate(p)]) for p in (to_x, to_y) if p]
+            for store, axis, at in zip(kinds[kind], (X, Y), (at_x, at_y)):
+                store[c] = [(Crossed(first, second, axis), (i, rows_at)) for i in range(at, at + end - at_x)]
+
+    def phase(name, *groups, ready=None, results=(), deps=(), pads=()):
+        outputs, landings = [], []
+        for number, steps in enumerate(groups):
+            to_x, to_y, lands = send(steps)
+            pad = pads[number] if number < len(pads) else 0
+            to_x, to_y = (
+                [((i, rows_at), terms) for i, terms in enumerate(p)]
+                + [((i, slice(half, half + pad)), [(terms[0][0], (*terms[0][1][:-1], slice(0, pad)))]) for i, terms in enumerate(p) if pad]
+                for p in (to_x, to_y)
+            )
+            shape = (len(lands) and lands[-1][-1], half + pad, width)
+            outputs += [(shape, to_x, to_y), (shape, to_y, to_x)]
+            landings.append(lands)
         if ready is not None:
             c = ready
             terms = [(0, top), (0, bot), (1, top), (1, bot), (2, top), (2, bot), (3, top), (3, bot)]
@@ -207,29 +252,32 @@
             rows = [
                 (place, [*both(c, 0, place), last_x[c][i], last_y[c][i]]) for i, place in enumerate((top, bot))
             ]
-            outputs.append(((capacity, width), rows))
+            pad = PAD if c in (1, 2) else 0
+            if pad:
+                rows.append((slice(capacity, capacity + pad), [(keep[c], (0, slice(0, pad)))]))
+            outputs.append(((capacity + pad, width), rows))
         made = hub(name, outputs, deps)
-        rest = made
-        if to_x:
-            land(lands, over_dp(made[0], X), over_dp(made[1], Y))
-            rest = made[2:]
+        rest, came = made, []
+        for lands in landings:
+            came += [over_links(rest[0], X, Y), over_links(rest[1], Y, X)]
+            land(lands, *came[-2:])
+            rest = rest[2:]
         if ready is not None:
-            give_to = over_dp(rest[0], CORE)
             keep[ready], *give = call(
                 expert_kernel,
                 "expert",
                 [(4, capacity, width)] + [(capacity, width)] * 4,
-                [me, rest[0], give_to, *matrices],
-                specs=[SMEM] + [VMEM] * 5,
+                [rest[0], over_core(rest[0]), *matrices],
                 scratch=[pltpu.VMEM((capacity, units), BF16)],
             )
-            got[ready] = [over_dp(array, CORE) for array in give]
+            got[ready] = [over_core(array) for array in give]
             rest = rest[1:]
         for c, result in zip(results, rest):
             back[c] = over_expert(result, ORDER[c]) if ORDER[c] else result
-        return made[0]
-
-    land([("piece", 0, 0, 0, 2)], over_dp(pieces[0].reshape(2, half, width), X), over_dp(pieces[0].reshape(2, half, width), Y))
+        return made[0], came
+
+    own = pieces[0].reshape(2, half, width)
+    land([("piece", 0, 0, 0, 2)], over_links(own, X, Y), over_links(own, Y, X))
     matrices = call(
         load_kernel,
         "load",
@@ -239,19 +287,19 @@
         specs=[ANY] * 3,
         scratch=[pltpu.SemaphoreType.DMA((3,))],
     )
-    made = phase("hub_b", [("relay", 0), ("piece", 1)], deps=(matrices[0],))
-    mix = [mixing(me, routes, scores, count, capacity, (made,))[j] for j in ORDER]
+    made, _ = phase("hub_b", [("relay", 0), ("piece", 1)], deps=(matrices[0],))
+    mix = [mixing(routes, scores, count, capacity, (made,))[j] for j in ORDER]
     phase("hub_c", [("relay", 1), ("piece", 2)], ready=0, deps=(mix[0],))
     phase("hub_d", [("relay", 2), ("piece", 3)], ready=1, deps=(keep[0],))
-    phase("hub_e", [("relay", 3), ("diagonal", 1)], ready=2)
+    phase("hub_e", [("relay", 3), ("diagonal", 1), ("diagonal", 0)], ready=2)
     phase("hub_f", [("diagonal", 2), ("near", 1)], ready=3)
-    phase("hub_g", [("diagonal", 3), ("diagonal", 0), ("near", 2)], results=(1,))
-    acc = call(combine_kernel, "combine", [routes.shape[:1] + (width,)], [mix[1], back[1]], dtype=F32)[0]
-    phase("hub_h", [("near", 3), ("near", 0)], results=(2,), deps=(acc,))
-    acc = call(combine_kernel, "combine", [acc.shape], [mix[2], back[2], acc], dtype=F32)[0]
-    phase("hub_i", [], results=(3, 0), deps=(acc,))
-    acc = call(combine_kernel, "combine", [acc.shape], [mix[0], back[0], acc], dtype=F32)[0]
-    return call(combine_kernel, "combine", [acc.shape], [mix[3], back[3], acc])[0]
+    phase("hub_g", [("diagonal", 3)], [("near", 2)], results=(1,))
+    made, _ = phase("hub_h", [("near", 3)])
+    phase("hub_i", [("near", 0)], results=(2,), deps=(made,))
+    phase("hub_j", results=(3,), deps=(back[1],))
+    phase("hub_k", results=(0,))
+    pairs = [array for c in range(count) for array in (mix[c], back[c])]
+    return call(combine_kernel, "combine", [(routes.shape[0], width)], pairs)[0]
 
 
 def experts_by_axes(outgoing, weights):
@@ -277,20 +325,20 @@
     expert_count = lax.axis_size("expert")
     row_count = tokens.shape[0]
     capacity = 3 * row_count // expert_count
-    me = jnp.stack([lax.axis_index("expert"), lax.axis_index("dp")]).astype(jnp.int32)
     weights = gate_weight[0], up_weight[0], down_weight[0]
 
-    shape = (capacity, tokens.shape[1])
+    by_chips = expert_count == 4 and lax.axis_size("dp") == 8
     outgoing = call(
         dispatch_kernel,
         "dispatch",
-        [shape] * expert_count,
-        [me, routes.T, tokens],
-        specs=[SMEM, VMEM, VMEM],
+        [(capacity, tokens.shape[1])] * expert_count,
+        [pltpu.with_memory_space_constraint(a, pltpu.HBM) for a in (routes.T, tokens)],
+        specs=[ANY, ANY],
+        scratch=[pltpu.VMEM(routes.shape[::-1], routes.dtype), pltpu.VMEM(tokens.shape, BF16), pltpu.SemaphoreType.DMA((2,))],
     )
-    if expert_count == 4 and lax.axis_size("dp") == 8:
-        return experts_by_chips(outgoing, weights, me, routes, scores)
-    mix = mixing(me, routes, scores, expert_count, capacity)
+    if by_chips:
+        return experts_by_chips(outgoing, weights, routes, scores)
+    mix = mixing(routes, scores, expert_count, capacity)
     results = experts_by_axes(outgoing, weights)
     pairs = [array for pair in zip(mix, results) for array in pair]
     return call(combine_kernel, "combine", [tokens.shape], pairs)[0]

time: 103 us -> 93.8 us (0.911)
  waiting for transfers between devices: 28.7 us -> 21 us
  starting transfers between devices: 38.8 us -> 42.1 us
  Pallas kernels: 33.4 us -> 30.2 us
  local copies, waits for them, and re-layouts: 1.64 us -> 0.01 us
    ppermute x6, waiting for transfers between devices: 20.9 us -> 8.78 us  [over_expert(): lax.ppermute(value, 'expert', [(i, i ^ mask) for i in range(lax.axis_size...]
    ppermute x36 -> x40, waiting for transfers between devices: 7.82 us -> 12.2 us  [the longest x20 12.1 us: over_links(): lax.ppermute(value, 'dp', [(i, i ^ (odd if i & 1 else even)) for i in ran...]
    pallas_call x19 -> x18, Pallas kernels: 33.4 us -> 30.2 us  [call(): pl.pallas_call(ordered(body, len(operands), len(deps)), out_shape=[jax.Sh...]
    ppermute x36 -> x40, starting transfers between devices: 22.2 us -> 25.3 us  [the longest x20 21.4 us: over_links(): lax.ppermute(value, 'dp', [(i, i ^ (odd if i & 1 else even)) for i in ran...]
    unnamed x6 -> x4, local copies, waits for them, and re-layouts: 1.64 us -> 0.01 us
  transfers between devices with their start and end apart: 42 -> 46, of which waited for: 14 -> 12; matrix products, arithmetic and copies ran while one was open for 0% -> 0% of each run, Pallas kernels for 29% -> 28%
where the time goes in v3:
time: 93.8 us; the launch traced here: 93.7 us
  starting transfers between devices  42.1 us (45%)
  Pallas kernels  30.2 us (32%)
  waiting for transfers between devices  21 us (22%)
    pallas_call x18, Pallas kernels, call(): pl.pallas_call(ordered(body, len(operands), len(deps)), out_shape=[jax.Sh...  30.2 us
    ppermute x20, starting transfers between devices, over_links(): lax.ppermute(value, 'dp', [(i, i ^ (odd if i & 1 else even)) for i in ran...  21.4 us
    ppermute x6, starting transfers between devices, over_expert(): lax.ppermute(value, 'expert', [(i, i ^ mask) for i in range(lax.axis_size...  16.8 us
    ppermute x20, waiting for transfers between devices, over_links(): lax.ppermute(value, 'dp', [(i, i ^ (odd if i & 1 else even)) for i in ran...  12.1 us
    ppermute x6, waiting for transfers between devices, over_expert(): lax.ppermute(value, 'expert', [(i, i ^ mask) for i in range(lax.axis_size...  8.78 us
    ppermute x20, starting transfers between devices, over_core(): lax.ppermute(value, 'dp', [(i, i ^ CORE) for i in range(lax.axis_size('dp...  3.87 us
  transfers between devices with their start and end apart: 46, of which 12 were waited for; matrix products, arithmetic and copies ran while one was open for 0% of the time, Pallas kernels for 28%

profile of v3, /device:TPU:0, one launch (start us, length us, event | category | flops | bytes accessed | tf_op | source)
XLA Modules:
  0.0 93.7 jit_solution(10244211817600369712)
XLA Ops:
  0.0 1.6 %dispatch.1 = (bf16[384,256]{1,0:T(8,128)(2,1)S(1)}, bf16[384,256]{1,0:T(8,128)(2,1)S(1)}, bf16[384,256]{1,0:T(8,128)(2,1)S(1)}, bf16[384,256]{1,0:T(8,128)(2,1)S(1)}) custom-call(s32[2,512]{1,0:T(2,128)} %bitcast.8, bf16[512,256]{1,0:T(8,128)(2,1)} %refs_1_.1), custom_call_target="tpu_custom_call" | custom-call | tf_op jit(solution)/shard_map/dispatch/pallas_call | solution.py:39
  1.6 4.1 %collective-permute-start.1 = (bf16[384,256]{1,0:T(8,128)(2,1)S(1)}, bf16[384,256]{1,0:T(8,128)(2,1)S(1)}, u32[]{:S(2)}, u32[]{:S(2)}) collective-permute-start(bf16[384,256]{1,0:T(8,128)(2,1)S(1)} %get-tuple-element.61), channel_id=1, source_target_pairs={{0,2},{1,3},{2,0},{3,1},{4,6},{5,7},{6,4},{7,5},{8,10},{9,11},{10,... | collective-permute-start | bytes 589832 | tf_op jit(solution)/shard_map/ppermute | solution.py:28
  5.7 1.5 %collective-permute-start.2 = (bf16[2,192,256]{2,1,0:T(8,128)(2,1)S(1)}, bf16[2,192,256]{2,1,0:T(8,128)(2,1)S(1)}, u32[]{:S(2)}, u32[]{:S(2)}) collective-permute-start(bf16[2,192,256]{2,1,0:T(8,128)(2,1)S(1)} %bitcast.6), channel_id=1, source_target_pairs={{0,8},{4,20},{8,0},{12,28},{16,24},{20,4},{24,16},{28,12},{1,9},{5... | collective-permute-start | bytes 589832 | tf_op jit(solution)/shard_map/ppermute | solution.py:24
  7.2 1.5 %collective-permute-start = (bf16[2,192,256]{2,1,0:T(8,128)(2,1)S(1)}, bf16[2,192,256]{2,1,0:T(8,128)(2,1)S(1)}, u32[]{:S(2)}, u32[]{:S(2)}) collective-permute-start(bf16[2,192,256]{2,1,0:T(8,128)(2,1)S(1)} %bitcast.7), channel_id=1, source_target_pairs={{0,16},{4,12},{8,24},{12,4},{16,0},{20,28},{24,8},{28,20},{1,17},{... | collective-permute-start | bytes 589832 | tf_op jit(solution)/shard_map/ppermute | solution.py:24
  8.7 4.7 %load.1 = (bf16[2048,1024]{1,0:T(8,128)(2,1)S(1)}, bf16[2048,1024]{1,0:T(8,128)(2,1)S(1)}, bf16[1024,2048]{1,0:T(8,128)(2,1)S(1)}) custom-call(bf16[2048,1024]{1,0:T(8,128)(2,1)} %bitcast.11, bf16[2048,1024]{1,0:T(8,128)(2,1)} %bitcast.12, bf16[1024,2048]{1,0:T(8,128)(2,1)} %bitcast.13, bf16[384,256]{1,0:T(8,128)(2,1)S(1)} %get-tuple-element.60.refs_3_), custom_call_target="tpu_custom_call" | custom-call | tf_op jit(solution)/shard_map/load/pallas_call | solution.py:39
  14.9 1.6 %collective-permute-start.3 = (bf16[3,192,256]{2,1,0:T(8,128)(2,1)S(1)}, bf16[3,192,256]{2,1,0:T(8,128)(2,1)S(1)}, u32[]{:S(2)}, u32[]{:S(2)}) collective-permute-start(bf16[3,192,256]{2,1,0:T(8,128)(2,1)S(1)} %get-tuple-element.65), channel_id=1, source_target_pairs={{0,16},{4,12},{8,24},{12,4},{16,0},{20,28},{24,8},{28,20},{1,17},{... | collective-permute-start | bytes 884744 | tf_op jit(solution)/shard_map/ppermute | solution.py:24
  16.5 1.5 %collective-permute-start.5 = (bf16[3,192,256]{2,1,0:T(8,128)(2,1)S(1)}, bf16[3,192,256]{2,1,0:T(8,128)(2,1)S(1)}, u32[]{:S(2)}, u32[]{:S(2)}) collective-permute-start(bf16[3,192,256]{2,1,0:T(8,128)(2,1)S(1)} %get-tuple-element.63.refs_2_), channel_id=1, source_target_pairs={{0,8},{4,20},{8,0},{12,28},{16,24},{20,4},{24,16},{28,12},{1,9},{5... | collective-permute-start | bytes 884744 | tf_op jit(solution)/shard_map/ppermute | solution.py:24
  18.0 3.5 %collective-permute-start.4 = (bf16[384,256]{1,0:T(8,128)(2,1)S(1)}, bf16[384,256]{1,0:T(8,128)(2,1)S(1)}, u32[]{:S(2)}, u32[]{:S(2)}) collective-permute-start(bf16[384,256]{1,0:T(8,128)(2,1)S(1)} %get-tuple-element.66), channel_id=1, source_target_pairs={{0,3},{1,2},{2,1},{3,0},{4,7},{5,6},{6,5},{7,4},{8,11},{9,10},{10,... | collective-permute-start | bytes 589832 | tf_op jit(solution)/shard_map/ppermute | solution.py:28
  22.2 3.9 %collective-permute-done.4.refs_1_.refs_6_ = bf16[384,256]{1,0:T(8,128)(2,1)S(1)} collective-permute-done((bf16[384,256]{1,0:T(8,128)(2,1)S(1)}, bf16[384,256]{1,0:T(8,128)(2,1)S(1)}, u32[]{:S(2)}, u32[]{:S(2)}) %collective-permute-start.4) | collective-permute-done | bytes 196640 | tf_op jit(solution)/shard_map/ppermute | solution.py:28
  27.4 3.0 %collective-permute-start.10 = (bf16[384,256]{1,0:T(8,128)(2,1)S(1)}, bf16[384,256]{1,0:T(8,128)(2,1)S(1)}, u32[]{:S(2)}, u32[]{:S(2)}) collective-permute-start(bf16[384,256]{1,0:T(8,128)(2,1)S(1)} %get-tuple-element.74), channel_id=1, source_target_pairs={{0,1},{1,0},{2,3},{3,2},{4,5},{5,4},{6,7},{7,6},{8,9},{9,8},{10,11... | collective-permute-start | bytes 589832 | tf_op jit(solution)/shard_map/ppermute | solution.py:28
  30.4 5.1 %expert.4 = (bf16[4,384,256]{2,1,0:T(8,128)(2,1)S(1)}, bf16[384,256]{1,0:T(8,128)(2,1)S(1)}, bf16[384,256]{1,0:T(8,128)(2,1)S(1)}, bf16[384,256]{1,0:T(8,128)(2,1)S(1)}, bf16[384,256]{1,0:T(8,128)(2,1)S(1)}) custom-call(bf16[4,384,256]{2,1,0:T(8,128)(2,1)S(1)} %get-tuple-element.67.refs_0_, bf16[4,384,256]{2,1,0:T(8,128)(2,1)S(1)} %collective-permute-done.6.refs_1_, ...), custom_call_target="tpu_custom_call" | custom-call | tf_op jit(solution)/shard_map/expert/pallas_call | solution.py:39
  38.8 5.1 %expert.5 = (bf16[4,384,256]{2,1,0:T(8,128)(2,1)S(1)}, bf16[384,256]{1,0:T(8,128)(2,1)S(1)}, bf16[384,256]{1,0:T(8,128)(2,1)S(1)}, bf16[384,256]{1,0:T(8,128)(2,1)S(1)}, bf16[384,256]{1,0:T(8,128)(2,1)S(1)}) custom-call(bf16[4,384,256]{2,1,0:T(8,128)(2,1)S(1)} %get-tuple-element.77.refs_0_, bf16[4,384,256]{2,1,0:T(8,128)(2,1)S(1)} %collective-permute-done.13.refs_1_, ...), custom_call_target="tpu_custom_call" | custom-call | tf_op jit(solution)/shard_map/expert/pallas_call | solution.py:39
  47.4 1.5 %collective-permute-start.19 = (bf16[3,192,256]{2,1,0:T(8,128)(2,1)S(1)}, bf16[3,192,256]{2,1,0:T(8,128)(2,1)S(1)}, u32[]{:S(2)}, u32[]{:S(2)}) collective-permute-start(bf16[3,192,256]{2,1,0:T(8,128)(2,1)S(1)} %get-tuple-element.84), channel_id=1, source_target_pairs={{0,8},{4,20},{8,0},{12,28},{16,24},{20,4},{24,16},{28,12},{1,9},{5... | collective-permute-start | bytes 884744 | tf_op jit(solution)/shard_map/ppermute | solution.py:24
  49.4 5.1 %expert.6 = (bf16[4,384,256]{2,1,0:T(8,128)(2,1)S(1)}, bf16[384,256]{1,0:T(8,128)(2,1)S(1)}, bf16[384,256]{1,0:T(8,128)(2,1)S(1)}, bf16[384,256]{1,0:T(8,128)(2,1)S(1)}, bf16[384,256]{1,0:T(8,128)(2,1)S(1)}) custom-call(bf16[4,384,256]{2,1,0:T(8,128)(2,1)S(1)} %get-tuple-element.85.refs_0_, bf16[4,384,256]{2,1,0:T(8,128)(2,1)S(1)} %collective-permute-done.20.refs_1_, ...), custom_call_target="tpu_custom_call" | custom-call | tf_op jit(solution)/shard_map/expert/pallas_call | solution.py:39
  59.1 5.1 %expert.7 = (bf16[4,384,256]{2,1,0:T(8,128)(2,1)S(1)}, bf16[384,256]{1,0:T(8,128)(2,1)S(1)}, bf16[384,256]{1,0:T(8,128)(2,1)S(1)}, bf16[384,256]{1,0:T(8,128)(2,1)S(1)}, bf16[384,256]{1,0:T(8,128)(2,1)S(1)}) custom-call(bf16[4,384,256]{2,1,0:T(8,128)(2,1)S(1)} %get-tuple-element.91.refs_0_, bf16[4,384,256]{2,1,0:T(8,128)(2,1)S(1)} %collective-permute-done.25.refs_1_, ...), custom_call_target="tpu_custom_call" | custom-call | tf_op jit(solution)/shard_map/expert/pallas_call | solution.py:39
  66.5 1.8 %collective-permute-start.32 = (bf16[2,192,256]{2,1,0:T(8,128)(2,1)S(1)}, bf16[2,192,256]{2,1,0:T(8,128)(2,1)S(1)}, u32[]{:S(2)}, u32[]{:S(2)}) collective-permute-start(bf16[2,192,256]{2,1,0:T(8,128)(2,1)S(1)} %get-tuple-element.99), channel_id=1, source_target_pairs={{0,8},{4,20},{8,0},{12,28},{16,24},{20,4},{24,16},{28,12},{1,9},{5... | collective-permute-start | bytes 589832 | tf_op jit(solution)/shard_map/ppermute | solution.py:24
  69.8 2.1 %collective-permute-start.40 = (bf16[400,256]{1,0:T(8,128)(2,1)S(1)}, bf16[400,256]{1,0:T(8,128)(2,1)S(1)}, u32[]{:S(2)}, u32[]{:S(2)}) collective-permute-start(bf16[400,256]{1,0:T(8,128)(2,1)S(1)} %get-tuple-element.109), channel_id=1, source_target_pairs={{0,2},{1,3},{2,0},{3,1},{4,6},{5,7},{6,4},{7,5},{8,10},{9,11},{10,... | collective-permute-start | bytes 614408 | tf_op jit(solution)/shard_map/ppermute | solution.py:28
  71.9 1.9 %collective-permute-done.35.refs_2_ = bf16[1,192,256]{2,1,0:T(8,128)(2,1)S(1)} collective-permute-done((bf16[1,192,256]{2,1,0:T(8,128)(2,1)S(1)}, bf16[1,192,256]{2,1,0:T(8,128)(2,1)S(1)}, u32[]{:S(2)}, u32[]{:S(2)}) %collective-permute-start.35) | collective-permute-done | bytes 98336 | tf_op jit(solution)/shard_map/ppermute | solution.py:24
  76.8 3.3 %collective-permute-done.33.refs_8_ = bf16[2,192,256]{2,1,0:T(8,128)(2,1)S(1)} collective-permute-done((bf16[2,192,256]{2,1,0:T(8,128)(2,1)S(1)}, bf16[2,192,256]{2,1,0:T(8,128)(2,1)S(1)}, u32[]{:S(2)}, u32[]{:S(2)}) %collective-permute-start.33) | collective-permute-done | bytes 196640 | tf_op jit(solution)/shard_map/ppermute | solution.py:24
  80.3 2.3 %collective-permute-start.41 = (bf16[400,256]{1,0:T(8,128)(2,1)S(1)}, bf16[400,256]{1,0:T(8,128)(2,1)S(1)}, u32[]{:S(2)}, u32[]{:S(2)}) collective-permute-start(bf16[400,256]{1,0:T(8,128)(2,1)S(1)} %get-tuple-element.111), channel_id=1, source_target_pairs={{0,3},{1,2},{2,1},{3,0},{4,7},{5,6},{6,5},{7,4},{8,11},{9,10},{10,... | collective-permute-start | bytes 614408 | tf_op jit(solution)/shard_map/ppermute | solution.py:28
  82.6 1.8 %collective-permute-done.40.refs_4_.refs_3_ = bf16[400,256]{1,0:T(8,128)(2,1)S(1)} collective-permute-done((bf16[400,256]{1,0:T(8,128)(2,1)S(1)}, bf16[400,256]{1,0:T(8,128)(2,1)S(1)}, u32[]{:S(2)}, u32[]{:S(2)}) %collective-permute-start.40) | collective-permute-done | bytes 204832 | tf_op jit(solution)/shard_map/ppermute | solution.py:28
  85.1 1.8 %collective-permute-start.45 = (bf16[384,256]{1,0:T(8,128)(2,1)S(1)}, bf16[384,256]{1,0:T(8,128)(2,1)S(1)}, u32[]{:S(2)}, u32[]{:S(2)}) collective-permute-start(bf16[384,256]{1,0:T(8,128)(2,1)S(1)} %hub_j.1), channel_id=1, source_target_pairs={{0,1},{1,0},{2,3},{3,2},{4,5},{5,4},{6,7},{7,6},{8,9},{9,8},{10,11... | collective-permute-start | bytes 589832 | tf_op jit(solution)/shard_map/ppermute | solution.py:28
  86.9 3.4 %collective-permute-done.38.refs_2_ = bf16[2,192,256]{2,1,0:T(8,128)(2,1)S(1)} collective-permute-done((bf16[2,192,256]{2,1,0:T(8,128)(2,1)S(1)}, bf16[2,192,256]{2,1,0:T(8,128)(2,1)S(1)}, u32[]{:S(2)}, u32[]{:S(2)}) %collective-permute-start.38) | collective-permute-done | bytes 196640 | tf_op jit(solution)/shard_map/ppermute | solution.py:24
  90.5 1.7 %collective-permute-done.45.refs_7_ = bf16[384,256]{1,0:T(8,128)(2,1)S(1)} collective-permute-done((bf16[384,256]{1,0:T(8,128)(2,1)S(1)}, bf16[384,256]{1,0:T(8,128)(2,1)S(1)}, u32[]{:S(2)}, u32[]{:S(2)}) %collective-permute-start.45) | collective-permute-done | bytes 196640 | tf_op jit(solution)/shard_map/ppermute | solution.py:28
  (90 shorter events, 24.6 us)
Async XLA Ops:
  1.6 13.2 %collective-permute-start.1 = (bf16[384,256]{1,0:T(8,128)(2,1)S(1)}, bf16[384,256]{1,0:T(8,128)(2,1)S(1)}, u32[]{:S(2)}, u32[]{:S(2)}) collective-permute-start(bf16[384,256]{1,0:T(8,128)(2,1)S(1)} %get-tuple-element.61), channel_id=1, source_target_pairs={{0,2},{1,3},{2,0},{3,1},{4,6},{5,7},{6,4},{7,5},{8,10},{9,11},{10,... | collective-permute-start | bytes 589832 | tf_op jit(solution)/shard_map/ppermute | solution.py:28
  5.7 9.1 %collective-permute-start.2 = (bf16[2,192,256]{2,1,0:T(8,128)(2,1)S(1)}, bf16[2,192,256]{2,1,0:T(8,128)(2,1)S(1)}, u32[]{:S(2)}, u32[]{:S(2)}) collective-permute-start(bf16[2,192,256]{2,1,0:T(8,128)(2,1)S(1)} %bitcast.6), channel_id=1, source_target_pairs={{0,8},{4,20},{8,0},{12,28},{16,24},{20,4},{24,16},{28,12},{1,9},{5... | collective-permute-start | bytes 589832 | tf_op jit(solution)/shard_map/ppermute | solution.py:24
  7.2 7.6 %collective-permute-start = (bf16[2,192,256]{2,1,0:T(8,128)(2,1)S(1)}, bf16[2,192,256]{2,1,0:T(8,128)(2,1)S(1)}, u32[]{:S(2)}, u32[]{:S(2)}) collective-permute-start(bf16[2,192,256]{2,1,0:T(8,128)(2,1)S(1)} %bitcast.7), channel_id=1, source_target_pairs={{0,16},{4,12},{8,24},{12,4},{16,0},{20,28},{24,8},{28,20},{1,17},{... | collective-permute-start | bytes 589832 | tf_op jit(solution)/shard_map/ppermute | solution.py:24
  14.9 11.2 %collective-permute-start.3 = (bf16[3,192,256]{2,1,0:T(8,128)(2,1)S(1)}, bf16[3,192,256]{2,1,0:T(8,128)(2,1)S(1)}, u32[]{:S(2)}, u32[]{:S(2)}) collective-permute-start(bf16[3,192,256]{2,1,0:T(8,128)(2,1)S(1)} %get-tuple-element.65), channel_id=1, source_target_pairs={{0,16},{4,12},{8,24},{12,4},{16,0},{20,28},{24,8},{28,20},{1,17},{... | collective-permute-start | bytes 884744 | tf_op jit(solution)/shard_map/ppermute | solution.py:24
  16.5 9.6 %collective-permute-start.5 = (bf16[3,192,256]{2,1,0:T(8,128)(2,1)S(1)}, bf16[3,192,256]{2,1,0:T(8,128)(2,1)S(1)}, u32[]{:S(2)}, u32[]{:S(2)}) collective-permute-start(bf16[3,192,256]{2,1,0:T(8,128)(2,1)S(1)} %get-tuple-element.63.refs_2_), channel_id=1, source_target_pairs={{0,8},{4,20},{8,0},{12,28},{16,24},{20,4},{24,16},{28,12},{1,9},{5... | collective-permute-start | bytes 884744 | tf_op jit(solution)/shard_map/ppermute | solution.py:24
  18.0 8.1 %collective-permute-start.4 = (bf16[384,256]{1,0:T(8,128)(2,1)S(1)}, bf16[384,256]{1,0:T(8,128)(2,1)S(1)}, u32[]{:S(2)}, u32[]{:S(2)}) collective-permute-start(bf16[384,256]{1,0:T(8,128)(2,1)S(1)} %get-tuple-element.66), channel_id=1, source_target_pairs={{0,3},{1,2},{2,1},{3,0},{4,7},{5,6},{6,5},{7,4},{8,11},{9,10},{10,... | collective-permute-start | bytes 589832 | tf_op jit(solution)/shard_map/ppermute | solution.py:28
  26.3 9.7 %collective-permute-start.9 = (bf16[3,192,256]{2,1,0:T(8,128)(2,1)S(1)}, bf16[3,192,256]{2,1,0:T(8,128)(2,1)S(1)}, u32[]{:S(2)}, u32[]{:S(2)}) collective-permute-start(bf16[3,192,256]{2,1,0:T(8,128)(2,1)S(1)} %get-tuple-element.73), channel_id=1, source_target_pairs={{0,16},{4,12},{8,24},{12,4},{16,0},{20,28},{24,8},{28,20},{1,17},{... | collective-permute-start | bytes 884744 | tf_op jit(solution)/shard_map/ppermute | solution.py:24
  26.9 9.1 %collective-permute-start.11 = (bf16[3,192,256]{2,1,0:T(8,128)(2,1)S(1)}, bf16[3,192,256]{2,1,0:T(8,128)(2,1)S(1)}, u32[]{:S(2)}, u32[]{:S(2)}) collective-permute-start(bf16[3,192,256]{2,1,0:T(8,128)(2,1)S(1)} %get-tuple-element.75), channel_id=1, source_target_pairs={{0,8},{4,20},{8,0},{12,28},{16,24},{20,4},{24,16},{28,12},{1,9},{5... | collective-permute-start | bytes 884744 | tf_op jit(solution)/shard_map/ppermute | solution.py:24
  27.4 8.1 %collective-permute-start.10 = (bf16[384,256]{1,0:T(8,128)(2,1)S(1)}, bf16[384,256]{1,0:T(8,128)(2,1)S(1)}, u32[]{:S(2)}, u32[]{:S(2)}) collective-permute-start(bf16[384,256]{1,0:T(8,128)(2,1)S(1)} %get-tuple-element.74), channel_id=1, source_target_pairs={{0,1},{1,0},{2,3},{3,2},{4,5},{5,4},{6,7},{7,6},{8,9},{9,8},{10,11... | collective-permute-start | bytes 589832 | tf_op jit(solution)/shard_map/ppermute | solution.py:28
  36.1 9.7 %collective-permute-start.12 = (bf16[3,192,256]{2,1,0:T(8,128)(2,1)S(1)}, bf16[3,192,256]{2,1,0:T(8,128)(2,1)S(1)}, u32[]{:S(2)}, u32[]{:S(2)}) collective-permute-start(bf16[3,192,256]{2,1,0:T(8,128)(2,1)S(1)} %get-tuple-element.76), channel_id=1, source_target_pairs={{0,16},{4,12},{8,24},{12,4},{16,0},{20,28},{24,8},{28,20},{1,17},{... | collective-permute-start | bytes 884744 | tf_op jit(solution)/shard_map/ppermute | solution.py:24
  37.3 8.5 %collective-permute-start.16 = (bf16[3,192,256]{2,1,0:T(8,128)(2,1)S(1)}, bf16[3,192,256]{2,1,0:T(8,128)(2,1)S(1)}, u32[]{:S(2)}, u32[]{:S(2)}) collective-permute-start(bf16[3,192,256]{2,1,0:T(8,128)(2,1)S(1)} %get-tuple-element.81), channel_id=1, source_target_pairs={{0,8},{4,20},{8,0},{12,28},{16,24},{20,4},{24,16},{28,12},{1,9},{5... | collective-permute-start | bytes 884744 | tf_op jit(solution)/shard_map/ppermute | solution.py:24
  46.3 9.6 %collective-permute-start.17 = (bf16[3,192,256]{2,1,0:T(8,128)(2,1)S(1)}, bf16[3,192,256]{2,1,0:T(8,128)(2,1)S(1)}, u32[]{:S(2)}, u32[]{:S(2)}) collective-permute-start(bf16[3,192,256]{2,1,0:T(8,128)(2,1)S(1)} %get-tuple-element.82), channel_id=1, source_target_pairs={{0,16},{4,12},{8,24},{12,4},{16,0},{20,28},{24,8},{28,20},{1,17},{... | collective-permute-start | bytes 884744 | tf_op jit(solution)/shard_map/ppermute | solution.py:24
  47.4 8.5 %collective-permute-start.19 = (bf16[3,192,256]{2,1,0:T(8,128)(2,1)S(1)}, bf16[3,192,256]{2,1,0:T(8,128)(2,1)S(1)}, u32[]{:S(2)}, u32[]{:S(2)}) collective-permute-start(bf16[3,192,256]{2,1,0:T(8,128)(2,1)S(1)} %get-tuple-element.84), channel_id=1, source_target_pairs={{0,8},{4,20},{8,0},{12,28},{16,24},{20,4},{24,16},{28,12},{1,9},{5... | collective-permute-start | bytes 884744 | tf_op jit(solution)/shard_map/ppermute | solution.py:24
  56.4 8.9 %collective-permute-start.28 = (bf16[3,192,256]{2,1,0:T(8,128)(2,1)S(1)}, bf16[3,192,256]{2,1,0:T(8,128)(2,1)S(1)}, u32[]{:S(2)}, u32[]{:S(2)}) collective-permute-start(bf16[3,192,256]{2,1,0:T(8,128)(2,1)S(1)} %get-tuple-element.95), channel_id=1, source_target_pairs={{0,16},{4,12},{8,24},{12,4},{16,0},{20,28},{24,8},{28,20},{1,17},{... | collective-permute-start | bytes 884744 | tf_op jit(solution)/shard_map/ppermute | solution.py:24
  57.9 6.9 %collective-permute-start.27 = (bf16[384,256]{1,0:T(8,128)(2,1)S(1)}, bf16[384,256]{1,0:T(8,128)(2,1)S(1)}, u32[]{:S(2)}, u32[]{:S(2)}) collective-permute-start(bf16[384,256]{1,0:T(8,128)(2,1)S(1)} %get-tuple-element.94), channel_id=1, source_target_pairs={{0,4},{4,0},{8,12},{12,8},{16,20},{20,16},{24,28},{28,24},{1,5},{5... | collective-permute-start | bytes 589832 | tf_op jit(solution)/shard_map/ppermute | solution.py:20
  57.9 7.8 %collective-permute-start.30 = (bf16[3,192,256]{2,1,0:T(8,128)(2,1)S(1)}, bf16[3,192,256]{2,1,0:T(8,128)(2,1)S(1)}, u32[]{:S(2)}, u32[]{:S(2)}) collective-permute-start(bf16[3,192,256]{2,1,0:T(8,128)(2,1)S(1)} %get-tuple-element.97), channel_id=1, source_target_pairs={{0,8},{4,20},{8,0},{12,28},{16,24},{20,4},{24,16},{28,12},{1,9},{5... | collective-permute-start | bytes 884744 | tf_op jit(solution)/shard_map/ppermute | solution.py:24
  66.1 8.6 %collective-permute-start.21 = (bf16[384,256]{1,0:T(8,128)(2,1)S(1)}, bf16[384,256]{1,0:T(8,128)(2,1)S(1)}, u32[]{:S(2)}, u32[]{:S(2)}) collective-permute-start(bf16[384,256]{1,0:T(8,128)(2,1)S(1)} %get-tuple-element.87), channel_id=1, source_target_pairs={{0,4},{4,0},{8,12},{12,8},{16,20},{20,16},{24,28},{28,24},{1,5},{5... | collective-permute-start | bytes 589832 | tf_op jit(solution)/shard_map/ppermute | solution.py:20
  66.5 9.5 %collective-permute-start.32 = (bf16[2,192,256]{2,1,0:T(8,128)(2,1)S(1)}, bf16[2,192,256]{2,1,0:T(8,128)(2,1)S(1)}, u32[]{:S(2)}, u32[]{:S(2)}) collective-permute-start(bf16[2,192,256]{2,1,0:T(8,128)(2,1)S(1)} %get-tuple-element.99), channel_id=1, source_target_pairs={{0,8},{4,20},{8,0},{12,28},{16,24},{20,4},{24,16},{28,12},{1,9},{5... | collective-permute-start | bytes 589832 | tf_op jit(solution)/shard_map/ppermute | solution.py:24
  69.8 14.6 %collective-permute-start.40 = (bf16[400,256]{1,0:T(8,128)(2,1)S(1)}, bf16[400,256]{1,0:T(8,128)(2,1)S(1)}, u32[]{:S(2)}, u32[]{:S(2)}) collective-permute-start(bf16[400,256]{1,0:T(8,128)(2,1)S(1)} %get-tuple-element.109), channel_id=1, source_target_pairs={{0,2},{1,3},{2,0},{3,1},{4,6},{5,7},{6,4},{7,5},{8,10},{9,11},{10,... | collective-permute-start | bytes 614408 | tf_op jit(solution)/shard_map/ppermute | solution.py:28
  74.5 8.0 %collective-permute-start.42 = (bf16[384,256]{1,0:T(8,128)(2,1)S(1)}, bf16[384,256]{1,0:T(8,128)(2,1)S(1)}, u32[]{:S(2)}, u32[]{:S(2)}) collective-permute-start(bf16[384,256]{1,0:T(8,128)(2,1)S(1)} %get-tuple-element.113), channel_id=1, source_target_pairs={{0,4},{4,0},{8,12},{12,8},{16,20},{20,16},{24,28},{28,24},{1,5},{5... | collective-permute-start | bytes 589832 | tf_op jit(solution)/shard_map/ppermute | solution.py:20
  74.7 9.7 %collective-permute-start.44 = (bf16[2,192,256]{2,1,0:T(8,128)(2,1)S(1)}, bf16[2,192,256]{2,1,0:T(8,128)(2,1)S(1)}, u32[]{:S(2)}, u32[]{:S(2)}) collective-permute-start(bf16[2,192,256]{2,1,0:T(8,128)(2,1)S(1)} %get-tuple-element.114), channel_id=1, source_target_pairs={{0,16},{4,12},{8,24},{12,4},{16,0},{20,28},{24,8},{28,20},{1,17},{... | collective-permute-start | bytes 589832 | tf_op jit(solution)/shard_map/ppermute | solution.py:24
  76.0 9.0 %collective-permute-start.43 = (bf16[2,192,256]{2,1,0:T(8,128)(2,1)S(1)}, bf16[2,192,256]{2,1,0:T(8,128)(2,1)S(1)}, u32[]{:S(2)}, u32[]{:S(2)}) collective-permute-start(bf16[2,192,256]{2,1,0:T(8,128)(2,1)S(1)} %get-tuple-element.105.refs_9_), channel_id=1, source_target_pairs={{0,8},{4,20},{8,0},{12,28},{16,24},{20,4},{24,16},{28,12},{1,9},{5... | collective-permute-start | bytes 589832 | tf_op jit(solution)/shard_map/ppermute | solution.py:24
  80.3 10.2 %collective-permute-start.41 = (bf16[400,256]{1,0:T(8,128)(2,1)S(1)}, bf16[400,256]{1,0:T(8,128)(2,1)S(1)}, u32[]{:S(2)}, u32[]{:S(2)}) collective-permute-start(bf16[400,256]{1,0:T(8,128)(2,1)S(1)} %get-tuple-element.111), channel_id=1, source_target_pairs={{0,3},{1,2},{2,1},{3,0},{4,7},{5,6},{6,5},{7,4},{8,11},{9,10},{10,... | collective-permute-start | bytes 614408 | tf_op jit(solution)/shard_map/ppermute | solution.py:28
  85.1 7.2 %collective-permute-start.45 = (bf16[384,256]{1,0:T(8,128)(2,1)S(1)}, bf16[384,256]{1,0:T(8,128)(2,1)S(1)}, u32[]{:S(2)}, u32[]{:S(2)}) collective-permute-start(bf16[384,256]{1,0:T(8,128)(2,1)S(1)} %hub_j.1), channel_id=1, source_target_pairs={{0,1},{1,0},{2,3},{3,2},{4,5},{5,4},{6,7},{7,6},{8,9},{9,8},{10,11... | collective-permute-start | bytes 589832 | tf_op jit(solution)/shard_map/ppermute | solution.py:28
  (24 other events, 110.9 us)

commit v4 on v3

--- a/solution.py
+++ b/solution.py
@@ -131,7 +131,10 @@
             gate = g if gate is None else gate + g
             up = u if up is None else up + u
         hidden[:, columns] = (gate / (1.0 + jnp.exp(-gate)) * up).astype(BF16)
-    slots = [(ref, me ^ (2 * j + 1)) for j, ref in enumerate(give_refs)]
+    gives = [give_refs[0]]
+    for ref in give_refs[1:]:
+        gives += [ref] if len(ref.shape) == 2 else [ref.at[j] for j in range(ref.shape[0])]
+    slots = [(ref, me ^ (2 * j + 1)) for ref, j in zip(gives, (3, 0, 1, 2))]
     slots += [(keep_ref.at[j], me ^ (2 * j)) for j in range(chips)]
     for ref, target in slots:
         columns = pl.ds(pl.multiple_of(target * width, width), width)
@@ -175,6 +178,12 @@
 
     shapes = [shape for shape, *_ in outputs]
     return call(body, name, shapes, arrays, deps)
+
+
+def hold_kernel(in_ref, out_ref):
+    capacity = in_ref.shape[0]
+    out_ref[:capacity] = in_ref[...]
+    out_ref[capacity:] = in_ref[: out_ref.shape[0] - capacity]
 
 
 def load_kernel(gate_ref, up_ref, down_ref, new_gate_ref, new_up_ref, new_down_ref, sems):
@@ -198,7 +207,7 @@
     keep, got, mix, back = {}, {}, None, {}
 
     def both(c, j, rows, extra=()):
-        return [(keep[c], (j, rows)), (got[c][j], rows), *extra]
+        return [(keep[c], (j, rows)), (got[c][j][0], (*got[c][j][1], rows)), *extra]
 
     def send(steps):
         to_x, to_y, lands = [], [], []
@@ -252,7 +261,7 @@
             rows = [
                 (place, [*both(c, 0, place), last_x[c][i], last_y[c][i]]) for i, place in enumerate((top, bot))
             ]
-            pad = PAD if c in (1, 2) else 0
+            pad = (0, 2 * PAD, PAD, 0)[c]
             if pad:
                 rows.append((slice(capacity, capacity + pad), [(keep[c], (0, slice(0, pad)))]))
             outputs.append(((capacity + pad, width), rows))
@@ -266,11 +275,14 @@
             keep[ready], *give = call(
                 expert_kernel,
                 "expert",
-                [(4, capacity, width)] + [(capacity, width)] * 4,
+                [(4, capacity, width), (capacity, width)] + ([(capacity, width)] * 3 if ready in (2, 3) else [(3, capacity, width)]),
                 [rest[0], over_core(rest[0]), *matrices],
                 scratch=[pltpu.VMEM((capacity, units), BF16)],
             )
-            got[ready] = [over_core(array) for array in give]
+            last, *others = [(over_core(array), ()) for array in give]
+            if len(others) == 1:
+                others = [(others[0][0], (j,)) for j in range(3)]
+            got[ready] = [*others, last]
             rest = rest[1:]
         for c, result in zip(results, rest):
             back[c] = over_expert(result, ORDER[c]) if ORDER[c] else result
@@ -287,9 +299,11 @@
         specs=[ANY] * 3,
         scratch=[pltpu.SemaphoreType.DMA((3,))],
     )
-    made, _ = phase("hub_b", [("relay", 0), ("piece", 1)], deps=(matrices[0],))
+    held = call(hold_kernel, "hold", [(capacity + PAD, width)], [outgoing[ORDER[2]]], (matrices[0],))[0]
+    pieces[2] = over_expert(held, ORDER[2])
+    made, _ = phase("hub_b", [("piece", 1)], [("relay", 0)])
     mix = [mixing(routes, scores, count, capacity, (made,))[j] for j in ORDER]
-    phase("hub_c", [("relay", 1), ("piece", 2)], ready=0, deps=(mix[0],))
+    phase("hub_c", [("relay", 1), ("piece", 2)], ready=0, deps=(mix[0], pieces[3]))
     phase("hub_d", [("relay", 2), ("piece", 3)], ready=1, deps=(keep[0],))
     phase("hub_e", [("relay", 3), ("diagonal", 1), ("diagonal", 0)], ready=2)
     phase("hub_f", [("diagonal", 2), ("near", 1)], ready=3)
@@ -298,8 +312,9 @@
     phase("hub_i", [("near", 0)], results=(2,), deps=(made,))
     phase("hub_j", results=(3,), deps=(back[1],))
     phase("hub_k", results=(0,))
-    pairs = [array for c in range(count) for array in (mix[c], back[c])]
-    return call(combine_kernel, "combine", [(routes.shape[0], width)], pairs)[0]
+    shape = (routes.shape[0], width)
+    acc = call(combine_kernel, "combine", [shape], [mix[0], back[0], mix[1], back[1]], dtype=F32)[0]
+    return call(combine_kernel, "combine", [shape], [mix[2], back[2], mix[3], back[3], acc])[0]
 
 
 def experts_by_axes(outgoing, weights):

time: 93.8 us -> 93 us (level)
  waiting for transfers between devices: 21 us -> 19.6 us
    ppermute x6, waiting for transfers between devices: 8.78 us -> 3.1 us  [over_expert(): lax.ppermute(value, 'expert', [(i, i ^ mask) for i in range(lax.axis_size...]
    ppermute x20 -> x22, waiting for transfers between devices: 12.1 us -> 16.2 us  [over_links(): lax.ppermute(value, 'dp', [(i, i ^ (odd if i & 1 else even)) for i in ran...]
    ppermute x20 -> x22, starting transfers between devices: 21.4 us -> 25.1 us  [over_links(): lax.ppermute(value, 'dp', [(i, i ^ (odd if i & 1 else even)) for i in ran...]
    ppermute x6, starting transfers between devices: 16.8 us -> 13.7 us  [over_expert(): lax.ppermute(value, 'expert', [(i, i ^ mask) for i in range(lax.axis_size...]
    pallas_call x18 -> x20, Pallas kernels: 30.2 us -> 30.5 us  [call(): pl.pallas_call(ordered(body, len(operands), len(deps)), out_shape=[jax.Sh...]
    ppermute x20 -> x16, starting transfers between devices: 3.87 us -> 3.72 us  [over_core(): lax.ppermute(value, 'dp', [(i, i ^ CORE) for i in range(lax.axis_size('dp...]
  transfers between devices with their start and end apart: 46 -> 44, of which waited for: 12 -> 14; matrix products, arithmetic and copies ran while one was open for 0% -> 0% of each run, Pallas kernels for 28% -> 29%
where the time goes in v4:
time: 93 us; the launch traced here: 92.9 us
  starting transfers between devices  42.5 us (46%)
  Pallas kernels  30.5 us (33%)
  waiting for transfers between devices  19.6 us (21%)
    pallas_call x20, Pallas kernels, call(): pl.pallas_call(ordered(body, len(operands), len(deps)), out_shape=[jax.Sh...  30.5 us
    ppermute x22, starting transfers between devices, over_links(): lax.ppermute(value, 'dp', [(i, i ^ (odd if i & 1 else even)) for i in ran...  25.1 us
    ppermute x22, waiting for transfers between devices, over_links(): lax.ppermute(value, 'dp', [(i, i ^ (odd if i & 1 else even)) for i in ran...  16.2 us
    ppermute x6, starting transfers between devices, over_expert(): lax.ppermute(value, 'expert', [(i, i ^ mask) for i in range(lax.axis_size...  13.7 us
    ppermute x16, starting transfers between devices, over_core(): lax.ppermute(value, 'dp', [(i, i ^ CORE) for i in range(lax.axis_size('dp...  3.72 us
    ppermute x6, waiting for transfers between devices, over_expert(): lax.ppermute(value, 'expert', [(i, i ^ mask) for i in range(lax.axis_size...  3.1 us
  transfers between devices with their start and end apart: 44, of which 14 were waited for; matrix products, arithmetic and copies ran while one was open for 0% of the time, Pallas kernels for 29%

profile of v4, /device:TPU:0, one launch (start us, length us, event | category | flops | bytes accessed | tf_op | source)
XLA Modules:
  0.0 92.9 jit_solution(12410395129800753694)
XLA Ops:
  0.0 1.6 %dispatch.1 = (bf16[384,256]{1,0:T(8,128)(2,1)S(1)}, bf16[384,256]{1,0:T(8,128)(2,1)S(1)}, bf16[384,256]{1,0:T(8,128)(2,1)S(1)}, bf16[384,256]{1,0:T(8,128)(2,1)S(1)}) custom-call(s32[2,512]{1,0:T(2,128)} %bitcast.8, bf16[512,256]{1,0:T(8,128)(2,1)} %refs_1_.1), custom_call_target="tpu_custom_call" | custom-call | tf_op jit(solution)/shard_map/dispatch/pallas_call | solution.py:39
  1.6 4.1 %collective-permute-start = (bf16[384,256]{1,0:T(8,128)(2,1)S(1)}, bf16[384,256]{1,0:T(8,128)(2,1)S(1)}, u32[]{:S(2)}, u32[]{:S(2)}) collective-permute-start(bf16[384,256]{1,0:T(8,128)(2,1)S(1)} %get-tuple-element.58), channel_id=1, source_target_pairs={{0,2},{1,3},{2,0},{3,1},{4,6},{5,7},{6,4},{7,5},{8,10},{9,11},{10,... | collective-permute-start | bytes 589832 | tf_op jit(solution)/shard_map/ppermute | solution.py:28
  5.7 1.5 %collective-permute-start.2 = (bf16[2,192,256]{2,1,0:T(8,128)(2,1)S(1)}, bf16[2,192,256]{2,1,0:T(8,128)(2,1)S(1)}, u32[]{:S(2)}, u32[]{:S(2)}) collective-permute-start(bf16[2,192,256]{2,1,0:T(8,128)(2,1)S(1)} %bitcast.6), channel_id=1, source_target_pairs={{0,8},{4,20},{8,0},{12,28},{16,24},{20,4},{24,16},{28,12},{1,9},{5... | collective-permute-start | bytes 589832 | tf_op jit(solution)/shard_map/ppermute | solution.py:24
  7.2 1.5 %collective-permute-start.1 = (bf16[2,192,256]{2,1,0:T(8,128)(2,1)S(1)}, bf16[2,192,256]{2,1,0:T(8,128)(2,1)S(1)}, u32[]{:S(2)}, u32[]{:S(2)}) collective-permute-start(bf16[2,192,256]{2,1,0:T(8,128)(2,1)S(1)} %bitcast.7), channel_id=1, source_target_pairs={{0,16},{4,12},{8,24},{12,4},{16,0},{20,28},{24,8},{28,20},{1,17},{... | collective-permute-start | bytes 589832 | tf_op jit(solution)/shard_map/ppermute | solution.py:24
  8.7 1.6 %collective-permute-start.8 = (bf16[384,256]{1,0:T(8,128)(2,1)S(1)}, bf16[384,256]{1,0:T(8,128)(2,1)S(1)}, u32[]{:S(2)}, u32[]{:S(2)}) collective-permute-start(bf16[384,256]{1,0:T(8,128)(2,1)S(1)} %get-tuple-element.68), channel_id=1, source_target_pairs={{0,1},{1,0},{2,3},{3,2},{4,5},{5,4},{6,7},{7,6},{8,9},{9,8},{10,11... | collective-permute-start | bytes 589832 | tf_op jit(solution)/shard_map/ppermute | solution.py:28
  10.3 4.7 %load.1 = (bf16[2048,1024]{1,0:T(8,128)(2,1)S(1)}, bf16[2048,1024]{1,0:T(8,128)(2,1)S(1)}, bf16[1024,2048]{1,0:T(8,128)(2,1)S(1)}) custom-call(bf16[2048,1024]{1,0:T(8,128)(2,1)} %bitcast.11, bf16[2048,1024]{1,0:T(8,128)(2,1)} %bitcast.12, bf16[1024,2048]{1,0:T(8,128)(2,1)} %bitcast.13, bf16[384,256]{1,0:T(8,128)(2,1)S(1)} %get-tuple-element.59.refs_3_), custom_call_target="tpu_custom_call" | custom-call | tf_op jit(solution)/shard_map/load/pallas_call | solution.py:39
  16.6 1.9 %collective-permute-start.5 = (bf16[2,192,256]{2,1,0:T(8,128)(2,1)S(1)}, bf16[2,192,256]{2,1,0:T(8,128)(2,1)S(1)}, u32[]{:S(2)}, u32[]{:S(2)}) collective-permute-start(bf16[2,192,256]{2,1,0:T(8,128)(2,1)S(1)} %get-tuple-element.60.refs_2_), channel_id=1, source_target_pairs={{0,8},{4,20},{8,0},{12,28},{16,24},{20,4},{24,16},{28,12},{1,9},{5... | collective-permute-start | bytes 589832 | tf_op jit(solution)/shard_map/ppermute | solution.py:24
  20.3 2.4 %collective-permute-done.4.refs_1_.refs_6_ = bf16[400,256]{1,0:T(8,128)(2,1)S(1)} collective-permute-done((bf16[400,256]{1,0:T(8,128)(2,1)S(1)}, bf16[400,256]{1,0:T(8,128)(2,1)S(1)}, u32[]{:S(2)}, u32[]{:S(2)}) %collective-permute-start.4) | collective-permute-done | bytes 204832 | tf_op jit(solution)/shard_map/ppermute | solution.py:28
  24.3 1.6 %collective-permute-start.11 = (bf16[3,192,256]{2,1,0:T(8,128)(2,1)S(1)}, bf16[3,192,256]{2,1,0:T(8,128)(2,1)S(1)}, u32[]{:S(2)}, u32[]{:S(2)}) collective-permute-start(bf16[3,192,256]{2,1,0:T(8,128)(2,1)S(1)} %get-tuple-element.74), channel_id=1, source_target_pairs={{0,16},{4,12},{8,24},{12,4},{16,0},{20,28},{24,8},{28,20},{1,17},{... | collective-permute-start | bytes 884744 | tf_op jit(solution)/shard_map/ppermute | solution.py:24
  26.5 5.1 %expert.4 = (bf16[4,384,256]{2,1,0:T(8,128)(2,1)S(1)}, bf16[384,256]{1,0:T(8,128)(2,1)S(1)}, bf16[3,384,256]{2,1,0:T(8,128)(2,1)S(1)}) custom-call(bf16[4,384,256]{2,1,0:T(8,128)(2,1)S(1)} %get-tuple-element.69.refs_0_, bf16[4,384,256]{2,1,0:T(8,128)(2,1)S(1)} %collective-permute-done.9.refs_1_, bf16[2048,1024]{1,0:T(8,128)(2,1)S(1)} %get-tuple-element.64.refs_1_.refs_2_, ...), custom_call_target="tpu_custom_call" | custom-call | tf_op jit(solution)/shard_map/expert/pallas_call | solution.py:39
  31.6 2.3 %collective-permute-done.11.refs_0_.refs_8_ = bf16[3,192,256]{2,1,0:T(8,128)(2,1)S(1)} collective-permute-done((bf16[3,192,256]{2,1,0:T(8,128)(2,1)S(1)}, bf16[3,192,256]{2,1,0:T(8,128)(2,1)S(1)}, u32[]{:S(2)}, u32[]{:S(2)}) %collective-permute-start.11) | collective-permute-done | bytes 294944 | tf_op jit(solution)/shard_map/ppermute | solution.py:24
  34.2 1.5 %collective-permute-start.13 = (bf16[3,192,256]{2,1,0:T(8,128)(2,1)S(1)}, bf16[3,192,256]{2,1,0:T(8,128)(2,1)S(1)}, u32[]{:S(2)}, u32[]{:S(2)}) collective-permute-start(bf16[3,192,256]{2,1,0:T(8,128)(2,1)S(1)} %get-tuple-element.76), channel_id=1, source_target_pairs={{0,16},{4,12},{8,24},{12,4},{16,0},{20,28},{24,8},{28,20},{1,17},{... | collective-permute-start | bytes 884744 | tf_op jit(solution)/shard_map/ppermute | solution.py:24
  36.4 5.1 %expert.5 = (bf16[4,384,256]{2,1,0:T(8,128)(2,1)S(1)}, bf16[384,256]{1,0:T(8,128)(2,1)S(1)}, bf16[3,384,256]{2,1,0:T(8,128)(2,1)S(1)}) custom-call(bf16[4,384,256]{2,1,0:T(8,128)(2,1)S(1)} %get-tuple-element.77.refs_0_, bf16[4,384,256]{2,1,0:T(8,128)(2,1)S(1)} %collective-permute-done.14.refs_1_, bf16[2048,1024]{1,0:T(8,128)(2,1)S(1)} %get-tuple-element.64.refs_1_.refs_2_, ...), custom_call_target="tpu_custom_call" | custom-call | tf_op jit(solution)/shard_map/expert/pallas_call | solution.py:39
  41.9 1.6 %collective-permute-done.13.refs_0_.refs_8_ = bf16[3,192,256]{2,1,0:T(8,128)(2,1)S(1)} collective-permute-done((bf16[3,192,256]{2,1,0:T(8,128)(2,1)S(1)}, bf16[3,192,256]{2,1,0:T(8,128)(2,1)S(1)}, u32[]{:S(2)}, u32[]{:S(2)}) %collective-permute-start.13) | collective-permute-done | bytes 294944 | tf_op jit(solution)/shard_map/ppermute | solution.py:24
  44.4 1.5 %collective-permute-start.18 = (bf16[3,192,256]{2,1,0:T(8,128)(2,1)S(1)}, bf16[3,192,256]{2,1,0:T(8,128)(2,1)S(1)}, u32[]{:S(2)}, u32[]{:S(2)}) collective-permute-start(bf16[3,192,256]{2,1,0:T(8,128)(2,1)S(1)} %get-tuple-element.82), channel_id=1, source_target_pairs={{0,16},{4,12},{8,24},{12,4},{16,0},{20,28},{24,8},{28,20},{1,17},{... | collective-permute-start | bytes 884744 | tf_op jit(solution)/shard_map/ppermute | solution.py:24
  46.4 5.2 %expert.6 = (bf16[4,384,256]{2,1,0:T(8,128)(2,1)S(1)}, bf16[384,256]{1,0:T(8,128)(2,1)S(1)}, bf16[384,256]{1,0:T(8,128)(2,1)S(1)}, bf16[384,256]{1,0:T(8,128)(2,1)S(1)}, bf16[384,256]{1,0:T(8,128)(2,1)S(1)}) custom-call(bf16[4,384,256]{2,1,0:T(8,128)(2,1)S(1)} %get-tuple-element.84.refs_0_, bf16[4,384,256]{2,1,0:T(8,128)(2,1)S(1)} %collective-permute-done.20.refs_1_, ...), custom_call_target="tpu_custom_call" | custom-call | tf_op jit(solution)/shard_map/expert/pallas_call | solution.py:39
  51.8 2.0 %collective-permute-done.18.refs_4_.refs_2_ = bf16[3,192,256]{2,1,0:T(8,128)(2,1)S(1)} collective-permute-done((bf16[3,192,256]{2,1,0:T(8,128)(2,1)S(1)}, bf16[3,192,256]{2,1,0:T(8,128)(2,1)S(1)}, u32[]{:S(2)}, u32[]{:S(2)}) %collective-permute-start.18) | collective-permute-done | bytes 294944 | tf_op jit(solution)/shard_map/ppermute | solution.py:24
  56.5 1.5 %collective-permute-start.29 = (bf16[3,192,256]{2,1,0:T(8,128)(2,1)S(1)}, bf16[3,192,256]{2,1,0:T(8,128)(2,1)S(1)}, u32[]{:S(2)}, u32[]{:S(2)}) collective-permute-start(bf16[3,192,256]{2,1,0:T(8,128)(2,1)S(1)} %get-tuple-element.95), channel_id=1, source_target_pairs={{0,8},{4,20},{8,0},{12,28},{16,24},{20,4},{24,16},{28,12},{1,9},{5... | collective-permute-start | bytes 884744 | tf_op jit(solution)/shard_map/ppermute | solution.py:24
  58.0 5.1 %expert.7 = (bf16[4,384,256]{2,1,0:T(8,128)(2,1)S(1)}, bf16[384,256]{1,0:T(8,128)(2,1)S(1)}, bf16[384,256]{1,0:T(8,128)(2,1)S(1)}, bf16[384,256]{1,0:T(8,128)(2,1)S(1)}, bf16[384,256]{1,0:T(8,128)(2,1)S(1)}) custom-call(bf16[4,384,256]{2,1,0:T(8,128)(2,1)S(1)} %get-tuple-element.89.refs_0_, bf16[4,384,256]{2,1,0:T(8,128)(2,1)S(1)} %collective-permute-done.24.refs_1_, ...), custom_call_target="tpu_custom_call" | custom-call | tf_op jit(solution)/shard_map/expert/pallas_call | solution.py:39
  64.9 1.5 %collective-permute-start.30 = (bf16[2,192,256]{2,1,0:T(8,128)(2,1)S(1)}, bf16[2,192,256]{2,1,0:T(8,128)(2,1)S(1)}, u32[]{:S(2)}, u32[]{:S(2)}) collective-permute-start(bf16[2,192,256]{2,1,0:T(8,128)(2,1)S(1)} %get-tuple-element.96), channel_id=1, source_target_pairs={{0,8},{4,20},{8,0},{12,28},{16,24},{20,4},{24,16},{28,12},{1,9},{5... | collective-permute-start | bytes 589832 | tf_op jit(solution)/shard_map/ppermute | solution.py:24
  68.4 2.3 %collective-permute-start.40 = (bf16[416,256]{1,0:T(8,128)(2,1)S(1)}, bf16[416,256]{1,0:T(8,128)(2,1)S(1)}, u32[]{:S(2)}, u32[]{:S(2)}) collective-permute-start(bf16[416,256]{1,0:T(8,128)(2,1)S(1)} %get-tuple-element.107), channel_id=1, source_target_pairs={{0,2},{1,3},{2,0},{3,1},{4,6},{5,7},{6,4},{7,5},{8,10},{9,11},{10,... | collective-permute-start | bytes 638984 | tf_op jit(solution)/shard_map/ppermute | solution.py:28
  75.0 3.1 %collective-permute-done.31.refs_7_ = bf16[2,192,256]{2,1,0:T(8,128)(2,1)S(1)} collective-permute-done((bf16[2,192,256]{2,1,0:T(8,128)(2,1)S(1)}, bf16[2,192,256]{2,1,0:T(8,128)(2,1)S(1)}, u32[]{:S(2)}, u32[]{:S(2)}) %collective-permute-start.31) | collective-permute-done | bytes 196640 | tf_op jit(solution)/shard_map/ppermute | solution.py:24
  78.3 5.3 %collective-permute-start.36 = (bf16[400,256]{1,0:T(8,128)(2,1)S(1)}, bf16[400,256]{1,0:T(8,128)(2,1)S(1)}, u32[]{:S(2)}, u32[]{:S(2)}) collective-permute-start(bf16[400,256]{1,0:T(8,128)(2,1)S(1)} %get-tuple-element.103), channel_id=1, source_target_pairs={{0,3},{1,2},{2,1},{3,0},{4,7},{5,6},{6,5},{7,4},{8,11},{9,10},{10,... | collective-permute-start | bytes 614408 | tf_op jit(solution)/shard_map/ppermute | solution.py:28
  86.1 3.2 %collective-permute-done.42.refs_2_ = bf16[2,192,256]{2,1,0:T(8,128)(2,1)S(1)} collective-permute-done((bf16[2,192,256]{2,1,0:T(8,128)(2,1)S(1)}, bf16[2,192,256]{2,1,0:T(8,128)(2,1)S(1)}, u32[]{:S(2)}, u32[]{:S(2)}) %collective-permute-start.42) | collective-permute-done | bytes 196640 | tf_op jit(solution)/shard_map/ppermute | solution.py:24
  (88 shorter events, 25.5 us)
Async XLA Ops:
  1.6 13.7 %collective-permute-start = (bf16[384,256]{1,0:T(8,128)(2,1)S(1)}, bf16[384,256]{1,0:T(8,128)(2,1)S(1)}, u32[]{:S(2)}, u32[]{:S(2)}) collective-permute-start(bf16[384,256]{1,0:T(8,128)(2,1)S(1)} %get-tuple-element.58), channel_id=1, source_target_pairs={{0,2},{1,3},{2,0},{3,1},{4,6},{5,7},{6,4},{7,5},{8,10},{9,11},{10,... | collective-permute-start | bytes 589832 | tf_op jit(solution)/shard_map/ppermute | solution.py:28
  5.7 9.6 %collective-permute-start.2 = (bf16[2,192,256]{2,1,0:T(8,128)(2,1)S(1)}, bf16[2,192,256]{2,1,0:T(8,128)(2,1)S(1)}, u32[]{:S(2)}, u32[]{:S(2)}) collective-permute-start(bf16[2,192,256]{2,1,0:T(8,128)(2,1)S(1)} %bitcast.6), channel_id=1, source_target_pairs={{0,8},{4,20},{8,0},{12,28},{16,24},{20,4},{24,16},{28,12},{1,9},{5... | collective-permute-start | bytes 589832 | tf_op jit(solution)/shard_map/ppermute | solution.py:24
  7.2 8.1 %collective-permute-start.1 = (bf16[2,192,256]{2,1,0:T(8,128)(2,1)S(1)}, bf16[2,192,256]{2,1,0:T(8,128)(2,1)S(1)}, u32[]{:S(2)}, u32[]{:S(2)}) collective-permute-start(bf16[2,192,256]{2,1,0:T(8,128)(2,1)S(1)} %bitcast.7), channel_id=1, source_target_pairs={{0,16},{4,12},{8,24},{12,4},{16,0},{20,28},{24,8},{28,20},{1,17},{... | collective-permute-start | bytes 589832 | tf_op jit(solution)/shard_map/ppermute | solution.py:24
  8.7 9.9 %collective-permute-start.8 = (bf16[384,256]{1,0:T(8,128)(2,1)S(1)}, bf16[384,256]{1,0:T(8,128)(2,1)S(1)}, u32[]{:S(2)}, u32[]{:S(2)}) collective-permute-start(bf16[384,256]{1,0:T(8,128)(2,1)S(1)} %get-tuple-element.68), channel_id=1, source_target_pairs={{0,1},{1,0},{2,3},{3,2},{4,5},{5,4},{6,7},{7,6},{8,9},{9,8},{10,11... | collective-permute-start | bytes 589832 | tf_op jit(solution)/shard_map/ppermute | solution.py:28
  15.0 7.7 %collective-permute-start.4 = (bf16[400,256]{1,0:T(8,128)(2,1)S(1)}, bf16[400,256]{1,0:T(8,128)(2,1)S(1)}, u32[]{:S(2)}, u32[]{:S(2)}) collective-permute-start(bf16[400,256]{1,0:T(8,128)(2,1)S(1)} %hold.1), channel_id=1, source_target_pairs={{0,3},{1,2},{2,1},{3,0},{4,7},{5,6},{6,5},{7,4},{8,11},{9,10},{10,... | collective-permute-start | bytes 614408 | tf_op jit(solution)/shard_map/ppermute | solution.py:28
  15.4 8.7 %collective-permute-start.3 = (bf16[2,192,256]{2,1,0:T(8,128)(2,1)S(1)}, bf16[2,192,256]{2,1,0:T(8,128)(2,1)S(1)}, u32[]{:S(2)}, u32[]{:S(2)}) collective-permute-start(bf16[2,192,256]{2,1,0:T(8,128)(2,1)S(1)} %get-tuple-element.62), channel_id=1, source_target_pairs={{0,16},{4,12},{8,24},{12,4},{16,0},{20,28},{24,8},{28,20},{1,17},{... | collective-permute-start | bytes 589832 | tf_op jit(solution)/shard_map/ppermute | solution.py:24
  24.3 9.6 %collective-permute-start.11 = (bf16[3,192,256]{2,1,0:T(8,128)(2,1)S(1)}, bf16[3,192,256]{2,1,0:T(8,128)(2,1)S(1)}, u32[]{:S(2)}, u32[]{:S(2)}) collective-permute-start(bf16[3,192,256]{2,1,0:T(8,128)(2,1)S(1)} %get-tuple-element.74), channel_id=1, source_target_pairs={{0,16},{4,12},{8,24},{12,4},{16,0},{20,28},{24,8},{28,20},{1,17},{... | collective-permute-start | bytes 884744 | tf_op jit(solution)/shard_map/ppermute | solution.py:24
  25.8 8.1 %collective-permute-start.12 = (bf16[3,192,256]{2,1,0:T(8,128)(2,1)S(1)}, bf16[3,192,256]{2,1,0:T(8,128)(2,1)S(1)}, u32[]{:S(2)}, u32[]{:S(2)}) collective-permute-start(bf16[3,192,256]{2,1,0:T(8,128)(2,1)S(1)} %get-tuple-element.75), channel_id=1, source_target_pairs={{0,8},{4,20},{8,0},{12,28},{16,24},{20,4},{24,16},{28,12},{1,9},{5... | collective-permute-start | bytes 884744 | tf_op jit(solution)/shard_map/ppermute | solution.py:24
  34.2 9.3 %collective-permute-start.13 = (bf16[3,192,256]{2,1,0:T(8,128)(2,1)S(1)}, bf16[3,192,256]{2,1,0:T(8,128)(2,1)S(1)}, u32[]{:S(2)}, u32[]{:S(2)}) collective-permute-start(bf16[3,192,256]{2,1,0:T(8,128)(2,1)S(1)} %get-tuple-element.76), channel_id=1, source_target_pairs={{0,16},{4,12},{8,24},{12,4},{16,0},{20,28},{24,8},{28,20},{1,17},{... | collective-permute-start | bytes 884744 | tf_op jit(solution)/shard_map/ppermute | solution.py:24
  35.7 7.8 %collective-permute-start.17 = (bf16[3,192,256]{2,1,0:T(8,128)(2,1)S(1)}, bf16[3,192,256]{2,1,0:T(8,128)(2,1)S(1)}, u32[]{:S(2)}, u32[]{:S(2)}) collective-permute-start(bf16[3,192,256]{2,1,0:T(8,128)(2,1)S(1)} %get-tuple-element.81), channel_id=1, source_target_pairs={{0,8},{4,20},{8,0},{12,28},{16,24},{20,4},{24,16},{28,12},{1,9},{5... | collective-permute-start | bytes 884744 | tf_op jit(solution)/shard_map/ppermute | solution.py:24
  44.3 9.5 %collective-permute-start.23 = (bf16[3,384,256]{2,1,0:T(8,128)(2,1)S(1)}, bf16[3,384,256]{2,1,0:T(8,128)(2,1)S(1)}, u32[]{:S(2)}, u32[]{:S(2)}) collective-permute-start(bf16[3,384,256]{2,1,0:T(8,128)(2,1)S(1)} %get-tuple-element.88), channel_id=1, source_target_pairs={{0,4},{4,0},{8,12},{12,8},{16,20},{20,16},{24,28},{28,24},{1,5},{5... | collective-permute-start | bytes 1769480 | tf_op jit(solution)/shard_map/ppermute | solution.py:20
  44.4 9.4 %collective-permute-start.18 = (bf16[3,192,256]{2,1,0:T(8,128)(2,1)S(1)}, bf16[3,192,256]{2,1,0:T(8,128)(2,1)S(1)}, u32[]{:S(2)}, u32[]{:S(2)}) collective-permute-start(bf16[3,192,256]{2,1,0:T(8,128)(2,1)S(1)} %get-tuple-element.82), channel_id=1, source_target_pairs={{0,16},{4,12},{8,24},{12,4},{16,0},{20,28},{24,8},{28,20},{1,17},{... | collective-permute-start | bytes 884744 | tf_op jit(solution)/shard_map/ppermute | solution.py:24
  46.0 7.8 %collective-permute-start.19 = (bf16[3,192,256]{2,1,0:T(8,128)(2,1)S(1)}, bf16[3,192,256]{2,1,0:T(8,128)(2,1)S(1)}, u32[]{:S(2)}, u32[]{:S(2)}) collective-permute-start(bf16[3,192,256]{2,1,0:T(8,128)(2,1)S(1)} %get-tuple-element.83), channel_id=1, source_target_pairs={{0,8},{4,20},{8,0},{12,28},{16,24},{20,4},{24,16},{28,12},{1,9},{5... | collective-permute-start | bytes 884744 | tf_op jit(solution)/shard_map/ppermute | solution.py:24
  54.4 12.0 %collective-permute-start.10 = (bf16[3,384,256]{2,1,0:T(8,128)(2,1)S(1)}, bf16[3,384,256]{2,1,0:T(8,128)(2,1)S(1)}, u32[]{:S(2)}, u32[]{:S(2)}) collective-permute-start(bf16[3,384,256]{2,1,0:T(8,128)(2,1)S(1)} %get-tuple-element.73), channel_id=1, source_target_pairs={{0,4},{4,0},{8,12},{12,8},{16,20},{20,16},{24,28},{28,24},{1,5},{5... | collective-permute-start | bytes 1769480 | tf_op jit(solution)/shard_map/ppermute | solution.py:20
  54.6 8.5 %collective-permute-start.26 = (bf16[384,256]{1,0:T(8,128)(2,1)S(1)}, bf16[384,256]{1,0:T(8,128)(2,1)S(1)}, u32[]{:S(2)}, u32[]{:S(2)}) collective-permute-start(bf16[384,256]{1,0:T(8,128)(2,1)S(1)} %get-tuple-element.92), channel_id=1, source_target_pairs={{0,4},{4,0},{8,12},{12,8},{16,20},{20,16},{24,28},{28,24},{1,5},{5... | collective-permute-start | bytes 589832 | tf_op jit(solution)/shard_map/ppermute | solution.py:20
  54.9 8.9 %collective-permute-start.27 = (bf16[3,192,256]{2,1,0:T(8,128)(2,1)S(1)}, bf16[3,192,256]{2,1,0:T(8,128)(2,1)S(1)}, u32[]{:S(2)}, u32[]{:S(2)}) collective-permute-start(bf16[3,192,256]{2,1,0:T(8,128)(2,1)S(1)} %get-tuple-element.93), channel_id=1, source_target_pairs={{0,16},{4,12},{8,24},{12,4},{16,0},{20,28},{24,8},{28,20},{1,17},{... | collective-permute-start | bytes 884744 | tf_op jit(solution)/shard_map/ppermute | solution.py:24
  56.5 7.5 %collective-permute-start.29 = (bf16[3,192,256]{2,1,0:T(8,128)(2,1)S(1)}, bf16[3,192,256]{2,1,0:T(8,128)(2,1)S(1)}, u32[]{:S(2)}, u32[]{:S(2)}) collective-permute-start(bf16[3,192,256]{2,1,0:T(8,128)(2,1)S(1)} %get-tuple-element.95), channel_id=1, source_target_pairs={{0,8},{4,20},{8,0},{12,28},{16,24},{20,4},{24,16},{28,12},{1,9},{5... | collective-permute-start | bytes 884744 | tf_op jit(solution)/shard_map/ppermute | solution.py:24
  64.0 8.9 %collective-permute-start.21 = (bf16[384,256]{1,0:T(8,128)(2,1)S(1)}, bf16[384,256]{1,0:T(8,128)(2,1)S(1)}, u32[]{:S(2)}, u32[]{:S(2)}) collective-permute-start(bf16[384,256]{1,0:T(8,128)(2,1)S(1)} %get-tuple-element.86), channel_id=1, source_target_pairs={{0,4},{4,0},{8,12},{12,8},{16,20},{20,16},{24,28},{28,24},{1,5},{5... | collective-permute-start | bytes 589832 | tf_op jit(solution)/shard_map/ppermute | solution.py:20
  64.9 9.2 %collective-permute-start.30 = (bf16[2,192,256]{2,1,0:T(8,128)(2,1)S(1)}, bf16[2,192,256]{2,1,0:T(8,128)(2,1)S(1)}, u32[]{:S(2)}, u32[]{:S(2)}) collective-permute-start(bf16[2,192,256]{2,1,0:T(8,128)(2,1)S(1)} %get-tuple-element.96), channel_id=1, source_target_pairs={{0,8},{4,20},{8,0},{12,28},{16,24},{20,4},{24,16},{28,12},{1,9},{5... | collective-permute-start | bytes 589832 | tf_op jit(solution)/shard_map/ppermute | solution.py:24
  68.4 16.4 %collective-permute-start.40 = (bf16[416,256]{1,0:T(8,128)(2,1)S(1)}, bf16[416,256]{1,0:T(8,128)(2,1)S(1)}, u32[]{:S(2)}, u32[]{:S(2)}) collective-permute-start(bf16[416,256]{1,0:T(8,128)(2,1)S(1)} %get-tuple-element.107), channel_id=1, source_target_pairs={{0,2},{1,3},{2,0},{3,1},{4,6},{5,7},{6,4},{7,5},{8,10},{9,11},{10,... | collective-permute-start | bytes 638984 | tf_op jit(solution)/shard_map/ppermute | solution.py:28
  72.8 10.8 %collective-permute-start.37 = (bf16[384,256]{1,0:T(8,128)(2,1)S(1)}, bf16[384,256]{1,0:T(8,128)(2,1)S(1)}, u32[]{:S(2)}, u32[]{:S(2)}) collective-permute-start(bf16[384,256]{1,0:T(8,128)(2,1)S(1)} %get-tuple-element.105), channel_id=1, source_target_pairs={{0,4},{4,0},{8,12},{12,8},{16,20},{20,16},{24,28},{28,24},{1,5},{5... | collective-permute-start | bytes 589832 | tf_op jit(solution)/shard_map/ppermute | solution.py:20
  72.9 13.0 %collective-permute-start.39 = (bf16[2,192,256]{2,1,0:T(8,128)(2,1)S(1)}, bf16[2,192,256]{2,1,0:T(8,128)(2,1)S(1)}, u32[]{:S(2)}, u32[]{:S(2)}) collective-permute-start(bf16[2,192,256]{2,1,0:T(8,128)(2,1)S(1)} %get-tuple-element.106), channel_id=1, source_target_pairs={{0,16},{4,12},{8,24},{12,4},{16,0},{20,28},{24,8},{28,20},{1,17},{... | collective-permute-start | bytes 589832 | tf_op jit(solution)/shard_map/ppermute | solution.py:24
  74.1 11.7 %collective-permute-start.38 = (bf16[2,192,256]{2,1,0:T(8,128)(2,1)S(1)}, bf16[2,192,256]{2,1,0:T(8,128)(2,1)S(1)}, u32[]{:S(2)}, u32[]{:S(2)}) collective-permute-start(bf16[2,192,256]{2,1,0:T(8,128)(2,1)S(1)} %get-tuple-element.102.refs_8_), channel_id=1, source_target_pairs={{0,8},{4,20},{8,0},{12,28},{16,24},{20,4},{24,16},{28,12},{1,9},{5... | collective-permute-start | bytes 589832 | tf_op jit(solution)/shard_map/ppermute | solution.py:24
  78.3 12.7 %collective-permute-start.36 = (bf16[400,256]{1,0:T(8,128)(2,1)S(1)}, bf16[400,256]{1,0:T(8,128)(2,1)S(1)}, u32[]{:S(2)}, u32[]{:S(2)}) collective-permute-start(bf16[400,256]{1,0:T(8,128)(2,1)S(1)} %get-tuple-element.103), channel_id=1, source_target_pairs={{0,3},{1,2},{2,1},{3,0},{4,7},{5,6},{6,5},{7,4},{8,11},{9,10},{10,... | collective-permute-start | bytes 614408 | tf_op jit(solution)/shard_map/ppermute | solution.py:28
  (22 other events, 98.0 us)

commit v5 on v4

--- a/solution.py
+++ b/solution.py
@@ -13,7 +13,7 @@
 VMEM = pl.BlockSpec(memory_space=pltpu.VMEM)
 CORE, X, Y, DIAGONAL = 1, 2, 4, 6
 PAD = 16
-ORDER = (0, 2, 3, 1)
+ORDER = (0, 3, 2, 1)
 
 
 def over_core(value):
@@ -24,8 +24,9 @@
     return lax.ppermute(value, "dp", [(i, i ^ (odd if i & 1 else even)) for i in range(lax.axis_size("dp"))])
 
 
-def over_expert(value, mask):
-    return lax.ppermute(value, "expert", [(i, i ^ mask) for i in range(lax.axis_size("expert"))])
+def over_expert(value, shift):
+    count = lax.axis_size("expert")
+    return lax.ppermute(value, "expert", [(i, (i + shift) % count) for i in range(count)])
 
 
 def ordered(body, operand_count, dep_count):
@@ -76,7 +77,7 @@
     loads[1].wait()
     tokens = tokens_ref[...]
     for j in range(len(out_refs)):
-        mine = jnp.max(jnp.where(ids == me ^ j, slots, -1), axis=0, keepdims=True)
+        mine = jnp.max(jnp.where(ids == lax.rem(me + j, len(out_refs)), slots, -1), axis=0, keepdims=True)
         placement = (slot_ids == mine).astype(F32).astype(BF16)
         out_refs[j][...] = jnp.dot(placement, tokens, preferred_element_type=F32).astype(BF16)
 
@@ -89,7 +90,7 @@
     weights = scores / jnp.sum(scores, axis=0, keepdims=True)
     slot_ids = lax.broadcasted_iota(jnp.int32, (capacity, row_count), 0)
     for j in range(len(out_refs)):
-        expert = me ^ j
+        expert = lax.rem(me + j, len(out_refs))
         mine = jnp.max(jnp.where(ids == expert, slots, -1), axis=0, keepdims=True)
         weight = jnp.where(routes_ref[0:1, :] == expert, weights[0:1, :], weights[1:2, :])
         out_refs[j][...] = jnp.where(slot_ids == mine, weight, 0.0).T.astype(BF16)
@@ -186,13 +187,26 @@
     out_ref[capacity:] = in_ref[: out_ref.shape[0] - capacity]
 
 
-def load_kernel(gate_ref, up_ref, down_ref, new_gate_ref, new_up_ref, new_down_ref, sems):
-    pairs = ((gate_ref, new_gate_ref), (up_ref, new_up_ref), (down_ref, new_down_ref))
-    copies = [pltpu.make_async_copy(old, new, sems.at[i]) for i, (old, new) in enumerate(pairs)]
+def load_kernel(*refs):
+    *refs, sems = refs
+    count = len(refs) // 2
+    copies = [pltpu.make_async_copy(refs[i], refs[count + i], sems.at[i]) for i in range(count)]
     for copy in copies:
         copy.start()
     for copy in copies:
         copy.wait()
+
+
+def load(weights, deps):
+    return call(
+        load_kernel,
+        "load",
+        [w.shape for w in weights],
+        [pltpu.with_memory_space_constraint(w, pltpu.HBM) for w in weights],
+        deps,
+        specs=[ANY] * len(weights),
+        scratch=[pltpu.SemaphoreType.DMA((len(weights),))],
+    )
 
 
 def experts_by_chips(outgoing, weights, routes, scores):
@@ -261,7 +275,7 @@
             rows = [
                 (place, [*both(c, 0, place), last_x[c][i], last_y[c][i]]) for i, place in enumerate((top, bot))
             ]
-            pad = (0, 2 * PAD, PAD, 0)[c]
+            pad = (0, PAD, PAD, 0)[c]
             if pad:
                 rows.append((slice(capacity, capacity + pad), [(keep[c], (0, slice(0, pad)))]))
             outputs.append(((capacity + pad, width), rows))
@@ -285,25 +299,18 @@
             got[ready] = [*others, last]
             rest = rest[1:]
         for c, result in zip(results, rest):
-            back[c] = over_expert(result, ORDER[c]) if ORDER[c] else result
+            back[c] = over_expert(result, -ORDER[c]) if ORDER[c] else result
         return made[0], came
 
     own = pieces[0].reshape(2, half, width)
     land([("piece", 0, 0, 0, 2)], over_links(own, X, Y), over_links(own, Y, X))
-    matrices = call(
-        load_kernel,
-        "load",
-        [w.shape for w in weights],
-        [pltpu.with_memory_space_constraint(w, pltpu.HBM) for w in weights],
-        (outgoing[0],),
-        specs=[ANY] * 3,
-        scratch=[pltpu.SemaphoreType.DMA((3,))],
-    )
-    held = call(hold_kernel, "hold", [(capacity + PAD, width)], [outgoing[ORDER[2]]], (matrices[0],))[0]
+    matrices = load(weights[:2], (outgoing[0],))
+    held = call(hold_kernel, "hold", [(capacity + PAD, width)], [outgoing[ORDER[2]]])[0]
     pieces[2] = over_expert(held, ORDER[2])
-    made, _ = phase("hub_b", [("piece", 1)], [("relay", 0)])
+    made, _ = phase("hub_b", [("piece", 1)], [("relay", 0)], deps=(matrices[0],))
+    matrices += load(weights[2:], (made,))
     mix = [mixing(routes, scores, count, capacity, (made,))[j] for j in ORDER]
-    phase("hub_c", [("relay", 1), ("piece", 2)], ready=0, deps=(mix[0], pieces[3]))
+    phase("hub_c", [("relay", 1), ("piece", 2)], ready=0, deps=(mix[0], matrices[2]))
     phase("hub_d", [("relay", 2), ("piece", 3)], ready=1, deps=(keep[0],))
     phase("hub_e", [("relay", 3), ("diagonal", 1), ("diagonal", 0)], ready=2)
     phase("hub_f", [("diagonal", 2), ("near", 1)], ready=3)
@@ -321,8 +328,8 @@
     expert_count = lax.axis_size("expert")
     capacity, width = outgoing[0].shape
     me = lax.axis_index("expert")
-    order = jnp.arange(expert_count) ^ me
-    rows = jnp.stack(outgoing)[order]
+    steps = jnp.arange(expert_count)
+    rows = jnp.stack(outgoing)[(steps - me) % expert_count]
     rows = lax.all_to_all(rows, "expert", split_axis=0, concat_axis=0, tiled=True)
     rows = lax.all_gather(rows.reshape(-1, width), "dp", axis=1, tiled=True)
     gate = jnp.dot(rows, weights[0], preferred_element_type=F32)
@@ -332,7 +339,7 @@
     total = lax.psum_scatter(part, "dp", scatter_dimension=1, tiled=True)
     back = lax.all_to_all(
         total.reshape(expert_count, capacity, width), "expert", split_axis=0, concat_axis=0, tiled=True
-    )[order]
+    )[(steps + me) % expert_count]
     return [back[j] for j in range(expert_count)]
 
 

time: 93 us -> 92.6 us (level)
  starting transfers between devices: 42.5 us -> 35.1 us
  waiting for transfers between devices: 19.6 us -> 25.4 us
  Pallas kernels: 30.5 us -> 31.6 us
    ppermute x6, starting transfers between devices: 13.7 us -> 6.02 us  [over_expert(): lax.ppermute(value, 'expert', [(i, (i + shift) % count) for i in range(co...]
    ppermute x6, waiting for transfers between devices: 3.1 us -> 6.36 us  [over_expert(): lax.ppermute(value, 'expert', [(i, (i + shift) % count) for i in range(co...]
    ppermute x22, waiting for transfers between devices: 16.2 us -> 17.7 us  [over_links(): lax.ppermute(value, 'dp', [(i, i ^ (odd if i & 1 else even)) for i in ran...]
    pallas_call x20 -> x21, Pallas kernels: 30.5 us -> 31.6 us  [call(): pl.pallas_call(ordered(body, len(operands), len(deps)), out_shape=[jax.Sh...]
    ppermute x16, waiting for transfers between devices: 0.34 us -> 1.34 us  [over_core(): lax.ppermute(value, 'dp', [(i, i ^ CORE) for i in range(lax.axis_size('dp...]
  transfers between devices with their start and end apart: 44 -> 44, of which waited for: 14 -> 18; matrix products, arithmetic and copies ran while one was open for 0% -> 0% of each run, Pallas kernels for 29% -> 30%
where the time goes in v5:
time: 92.6 us; the launch traced here: 92.4 us
  starting transfers between devices  35.1 us (38%)
  Pallas kernels  31.6 us (34%)
  waiting for transfers between devices  25.4 us (27%)
    pallas_call x21, Pallas kernels, call(): pl.pallas_call(ordered(body, len(operands), len(deps)), out_shape=[jax.Sh...  31.6 us
    ppermute x22, starting transfers between devices, over_links(): lax.ppermute(value, 'dp', [(i, i ^ (odd if i & 1 else even)) for i in ran...  25.9 us
    ppermute x22, waiting for transfers between devices, over_links(): lax.ppermute(value, 'dp', [(i, i ^ (odd if i & 1 else even)) for i in ran...  17.7 us
    ppermute x6, waiting for transfers between devices, over_expert(): lax.ppermute(value, 'expert', [(i, (i + shift) % count) for i in range(co...  6.36 us
    ppermute x6, starting transfers between devices, over_expert(): lax.ppermute(value, 'expert', [(i, (i + shift) % count) for i in range(co...  6.02 us
    ppermute x16, starting transfers between devices, over_core(): lax.ppermute(value, 'dp', [(i, i ^ CORE) for i in range(lax.axis_size('dp...  3.21 us
  transfers between devices with their start and end apart: 44, of which 18 were waited for; matrix products, arithmetic and copies ran while one was open for 0% of the time, Pallas kernels for 30%

profile of v5, /device:TPU:0, one launch (start us, length us, event | category | flops | bytes accessed | tf_op | source)
XLA Modules:
  0.0 92.4 jit_solution(14734245074452595666)
XLA Ops:
  0.0 1.6 %dispatch.1 = (bf16[384,256]{1,0:T(8,128)(2,1)S(1)}, bf16[384,256]{1,0:T(8,128)(2,1)S(1)}, bf16[384,256]{1,0:T(8,128)(2,1)S(1)}, bf16[384,256]{1,0:T(8,128)(2,1)S(1)}) custom-call(s32[2,512]{1,0:T(2,128)} %bitcast.8, bf16[512,256]{1,0:T(8,128)(2,1)} %refs_1_.1), custom_call_target="tpu_custom_call" | custom-call | tf_op jit(solution)/shard_map/dispatch/pallas_call | solution.py:40
  1.6 5.1 %collective-permute-start = (bf16[384,256]{1,0:T(8,128)(2,1)S(1)}, bf16[384,256]{1,0:T(8,128)(2,1)S(1)}, u32[]{:S(2)}, u32[]{:S(2)}) collective-permute-start(bf16[384,256]{1,0:T(8,128)(2,1)S(1)} %get-tuple-element.57), channel_id=1, source_target_pairs={{0,3},{1,0},{2,1},{3,2},{4,7},{5,4},{6,5},{7,6},{8,11},{9,8},{10,9... | collective-permute-start | bytes 589832 | tf_op jit(solution)/shard_map/ppermute | solution.py:29
  6.7 1.5 %collective-permute-start.2 = (bf16[2,192,256]{2,1,0:T(8,128)(2,1)S(1)}, bf16[2,192,256]{2,1,0:T(8,128)(2,1)S(1)}, u32[]{:S(2)}, u32[]{:S(2)}) collective-permute-start(bf16[2,192,256]{2,1,0:T(8,128)(2,1)S(1)} %bitcast.6), channel_id=1, source_target_pairs={{0,8},{4,20},{8,0},{12,28},{16,24},{20,4},{24,16},{28,12},{1,9},{5... | collective-permute-start | bytes 589832 | tf_op jit(solution)/shard_map/ppermute | solution.py:24
  8.2 1.5 %collective-permute-start.1 = (bf16[2,192,256]{2,1,0:T(8,128)(2,1)S(1)}, bf16[2,192,256]{2,1,0:T(8,128)(2,1)S(1)}, u32[]{:S(2)}, u32[]{:S(2)}) collective-permute-start(bf16[2,192,256]{2,1,0:T(8,128)(2,1)S(1)} %bitcast.7), channel_id=1, source_target_pairs={{0,16},{4,12},{8,24},{12,4},{16,0},{20,28},{24,8},{28,20},{1,17},{... | collective-permute-start | bytes 589832 | tf_op jit(solution)/shard_map/ppermute | solution.py:24
  9.8 3.5 %load.2 = (bf16[2048,1024]{1,0:T(8,128)(2,1)S(1)}, bf16[2048,1024]{1,0:T(8,128)(2,1)S(1)}) custom-call(bf16[2048,1024]{1,0:T(8,128)(2,1)} %bitcast.11, bf16[2048,1024]{1,0:T(8,128)(2,1)} %bitcast.12, bf16[384,256]{1,0:T(8,128)(2,1)S(1)} %get-tuple-element.58.refs_2_.refs_3_), custom_call_target="tpu_custom_call" | custom-call | tf_op jit(solution)/shard_map/load/pallas_call | solution.py:40
  19.2 2.2 %load.3.refs_9_.refs_4_ = bf16[1024,2048]{1,0:T(8,128)(2,1)S(1)} custom-call(bf16[1024,2048]{1,0:T(8,128)(2,1)} %bitcast.13, bf16[2,192,256]{2,1,0:T(8,128)(2,1)S(1)} %get-tuple-element.60.refs_2_.refs_1_), custom_call_target="tpu_custom_call" | custom-call | tf_op jit(solution)/shard_map/load/pallas_call | solution.py:40
  21.5 1.8 %collective-permute-done.6.refs_6_ = bf16[1,192,256]{2,1,0:T(8,128)(2,1)S(1)} collective-permute-done((bf16[1,192,256]{2,1,0:T(8,128)(2,1)S(1)}, bf16[1,192,256]{2,1,0:T(8,128)(2,1)S(1)}, u32[]{:S(2)}, u32[]{:S(2)}) %collective-permute-start.6) | collective-permute-done | bytes 98336 | tf_op jit(solution)/shard_map/ppermute | solution.py:24
  26.6 5.2 %expert.4 = (bf16[4,384,256]{2,1,0:T(8,128)(2,1)S(1)}, bf16[384,256]{1,0:T(8,128)(2,1)S(1)}, bf16[3,384,256]{2,1,0:T(8,128)(2,1)S(1)}) custom-call(bf16[4,384,256]{2,1,0:T(8,128)(2,1)S(1)} %get-tuple-element.67.refs_0_, bf16[4,384,256]{2,1,0:T(8,128)(2,1)S(1)} %collective-permute-done.8.refs_1_, bf16[2048,1024]{1,0:T(8,128)(2,1)S(1)} %get-tuple-element.59.refs_3_.refs_2_, ...), custom_call_target="tpu_custom_call" | custom-call | tf_op jit(solution)/shard_map/expert/pallas_call | solution.py:40
  31.8 2.2 %collective-permute-done.11.refs_1_.refs_6_ = bf16[384,256]{1,0:T(8,128)(2,1)S(1)} collective-permute-done((bf16[384,256]{1,0:T(8,128)(2,1)S(1)}, bf16[384,256]{1,0:T(8,128)(2,1)S(1)}, u32[]{:S(2)}, u32[]{:S(2)}) %collective-permute-start.11) | collective-permute-done | bytes 196640 | tf_op jit(solution)/shard_map/ppermute | solution.py:29
  34.6 1.4 %collective-permute-start.13 = (bf16[3,192,256]{2,1,0:T(8,128)(2,1)S(1)}, bf16[3,192,256]{2,1,0:T(8,128)(2,1)S(1)}, u32[]{:S(2)}, u32[]{:S(2)}) collective-permute-start(bf16[3,192,256]{2,1,0:T(8,128)(2,1)S(1)} %get-tuple-element.74), channel_id=1, source_target_pairs={{0,16},{4,12},{8,24},{12,4},{16,0},{20,28},{24,8},{28,20},{1,17},{... | collective-permute-start | bytes 884744 | tf_op jit(solution)/shard_map/ppermute | solution.py:24
  37.2 5.1 %expert.5 = (bf16[4,384,256]{2,1,0:T(8,128)(2,1)S(1)}, bf16[384,256]{1,0:T(8,128)(2,1)S(1)}, bf16[3,384,256]{2,1,0:T(8,128)(2,1)S(1)}) custom-call(bf16[4,384,256]{2,1,0:T(8,128)(2,1)S(1)} %get-tuple-element.75.refs_0_, bf16[4,384,256]{2,1,0:T(8,128)(2,1)S(1)} %collective-permute-done.14.refs_1_, bf16[2048,1024]{1,0:T(8,128)(2,1)S(1)} %get-tuple-element.59.refs_3_.refs_2_, ...), custom_call_target="tpu_custom_call" | custom-call | tf_op jit(solution)/shard_map/expert/pallas_call | solution.py:40
  45.1 1.4 %collective-permute-start.18 = (bf16[3,192,256]{2,1,0:T(8,128)(2,1)S(1)}, bf16[3,192,256]{2,1,0:T(8,128)(2,1)S(1)}, u32[]{:S(2)}, u32[]{:S(2)}) collective-permute-start(bf16[3,192,256]{2,1,0:T(8,128)(2,1)S(1)} %get-tuple-element.80), channel_id=1, source_target_pairs={{0,16},{4,12},{8,24},{12,4},{16,0},{20,28},{24,8},{28,20},{1,17},{... | collective-permute-start | bytes 884744 | tf_op jit(solution)/shard_map/ppermute | solution.py:24
  46.5 1.4 %collective-permute-start.19 = (bf16[3,192,256]{2,1,0:T(8,128)(2,1)S(1)}, bf16[3,192,256]{2,1,0:T(8,128)(2,1)S(1)}, u32[]{:S(2)}, u32[]{:S(2)}) collective-permute-start(bf16[3,192,256]{2,1,0:T(8,128)(2,1)S(1)} %get-tuple-element.81), channel_id=1, source_target_pairs={{0,8},{4,20},{8,0},{12,28},{16,24},{20,4},{24,16},{28,12},{1,9},{5... | collective-permute-start | bytes 884744 | tf_op jit(solution)/shard_map/ppermute | solution.py:24
  47.9 5.2 %expert.6 = (bf16[4,384,256]{2,1,0:T(8,128)(2,1)S(1)}, bf16[384,256]{1,0:T(8,128)(2,1)S(1)}, bf16[384,256]{1,0:T(8,128)(2,1)S(1)}, bf16[384,256]{1,0:T(8,128)(2,1)S(1)}, bf16[384,256]{1,0:T(8,128)(2,1)S(1)}) custom-call(bf16[4,384,256]{2,1,0:T(8,128)(2,1)S(1)} %get-tuple-element.82.refs_0_, bf16[4,384,256]{2,1,0:T(8,128)(2,1)S(1)} %collective-permute-done.20.refs_1_, ...), custom_call_target="tpu_custom_call" | custom-call | tf_op jit(solution)/shard_map/expert/pallas_call | solution.py:40
  53.2 1.5 %collective-permute-done.18.refs_4_.refs_2_ = bf16[3,192,256]{2,1,0:T(8,128)(2,1)S(1)} collective-permute-done((bf16[3,192,256]{2,1,0:T(8,128)(2,1)S(1)}, bf16[3,192,256]{2,1,0:T(8,128)(2,1)S(1)}, u32[]{:S(2)}, u32[]{:S(2)}) %collective-permute-start.18) | collective-permute-done | bytes 294944 | tf_op jit(solution)/shard_map/ppermute | solution.py:24
  55.6 1.4 %collective-permute-start.27 = (bf16[3,192,256]{2,1,0:T(8,128)(2,1)S(1)}, bf16[3,192,256]{2,1,0:T(8,128)(2,1)S(1)}, u32[]{:S(2)}, u32[]{:S(2)}) collective-permute-start(bf16[3,192,256]{2,1,0:T(8,128)(2,1)S(1)} %get-tuple-element.91), channel_id=1, source_target_pairs={{0,16},{4,12},{8,24},{12,4},{16,0},{20,28},{24,8},{28,20},{1,17},{... | collective-permute-start | bytes 884744 | tf_op jit(solution)/shard_map/ppermute | solution.py:24
  58.5 5.1 %expert.7 = (bf16[4,384,256]{2,1,0:T(8,128)(2,1)S(1)}, bf16[384,256]{1,0:T(8,128)(2,1)S(1)}, bf16[384,256]{1,0:T(8,128)(2,1)S(1)}, bf16[384,256]{1,0:T(8,128)(2,1)S(1)}, bf16[384,256]{1,0:T(8,128)(2,1)S(1)}) custom-call(bf16[4,384,256]{2,1,0:T(8,128)(2,1)S(1)} %get-tuple-element.87.refs_0_, bf16[4,384,256]{2,1,0:T(8,128)(2,1)S(1)} %collective-permute-done.24.refs_1_, ...), custom_call_target="tpu_custom_call" | custom-call | tf_op jit(solution)/shard_map/expert/pallas_call | solution.py:40
  66.8 1.4 %collective-permute-start.33 = (bf16[1,192,256]{2,1,0:T(8,128)(2,1)S(1)}, bf16[1,192,256]{2,1,0:T(8,128)(2,1)S(1)}, u32[]{:S(2)}, u32[]{:S(2)}) collective-permute-start(bf16[1,192,256]{2,1,0:T(8,128)(2,1)S(1)} %get-tuple-element.97), channel_id=1, source_target_pairs={{0,16},{4,12},{8,24},{12,4},{16,0},{20,28},{24,8},{28,20},{1,17},{... | collective-permute-start | bytes 294920 | tf_op jit(solution)/shard_map/ppermute | solution.py:24
  69.2 3.4 %collective-permute-done.33.refs_2_ = bf16[1,192,256]{2,1,0:T(8,128)(2,1)S(1)} collective-permute-done((bf16[1,192,256]{2,1,0:T(8,128)(2,1)S(1)}, bf16[1,192,256]{2,1,0:T(8,128)(2,1)S(1)}, u32[]{:S(2)}, u32[]{:S(2)}) %collective-permute-start.33) | collective-permute-done | bytes 98336 | tf_op jit(solution)/shard_map/ppermute | solution.py:24
  72.5 1.4 %collective-permute-start.31 = (bf16[2,192,256]{2,1,0:T(8,128)(2,1)S(1)}, bf16[2,192,256]{2,1,0:T(8,128)(2,1)S(1)}, u32[]{:S(2)}, u32[]{:S(2)}) collective-permute-start(bf16[2,192,256]{2,1,0:T(8,128)(2,1)S(1)} %get-tuple-element.95), channel_id=1, source_target_pairs={{0,16},{4,12},{8,24},{12,4},{16,0},{20,28},{24,8},{28,20},{1,17},{... | collective-permute-start | bytes 589832 | tf_op jit(solution)/shard_map/ppermute | solution.py:24
  75.7 2.7 %collective-permute-done.31.refs_7_ = bf16[2,192,256]{2,1,0:T(8,128)(2,1)S(1)} collective-permute-done((bf16[2,192,256]{2,1,0:T(8,128)(2,1)S(1)}, bf16[2,192,256]{2,1,0:T(8,128)(2,1)S(1)}, u32[]{:S(2)}, u32[]{:S(2)}) %collective-permute-start.31) | collective-permute-done | bytes 196640 | tf_op jit(solution)/shard_map/ppermute | solution.py:24
  79.5 2.3 %collective-permute-start.43 = (bf16[2,192,256]{2,1,0:T(8,128)(2,1)S(1)}, bf16[2,192,256]{2,1,0:T(8,128)(2,1)S(1)}, u32[]{:S(2)}, u32[]{:S(2)}) collective-permute-start(bf16[2,192,256]{2,1,0:T(8,128)(2,1)S(1)} %get-tuple-element.107), channel_id=1, source_target_pairs={{0,16},{4,12},{8,24},{12,4},{16,0},{20,28},{24,8},{28,20},{1,17},{... | collective-permute-start | bytes 589832 | tf_op jit(solution)/shard_map/ppermute | solution.py:24
  83.5 2.2 %collective-permute-done.42.refs_2_ = bf16[2,192,256]{2,1,0:T(8,128)(2,1)S(1)} collective-permute-done((bf16[2,192,256]{2,1,0:T(8,128)(2,1)S(1)}, bf16[2,192,256]{2,1,0:T(8,128)(2,1)S(1)}, u32[]{:S(2)}, u32[]{:S(2)}) %collective-permute-start.42) | collective-permute-done | bytes 196640 | tf_op jit(solution)/shard_map/ppermute | solution.py:24
  88.0 3.3 %collective-permute-done.41.refs_3_ = bf16[384,256]{1,0:T(8,128)(2,1)S(1)} collective-permute-done((bf16[384,256]{1,0:T(8,128)(2,1)S(1)}, bf16[384,256]{1,0:T(8,128)(2,1)S(1)}, u32[]{:S(2)}, u32[]{:S(2)}) %collective-permute-start.41) | collective-permute-done | bytes 196640 | tf_op jit(solution)/shard_map/ppermute | solution.py:29
  (89 shorter events, 28.2 us)
Async XLA Ops:
  1.6 11.7 %collective-permute-start = (bf16[384,256]{1,0:T(8,128)(2,1)S(1)}, bf16[384,256]{1,0:T(8,128)(2,1)S(1)}, u32[]{:S(2)}, u32[]{:S(2)}) collective-permute-start(bf16[384,256]{1,0:T(8,128)(2,1)S(1)} %get-tuple-element.57), channel_id=1, source_target_pairs={{0,3},{1,0},{2,1},{3,2},{4,7},{5,4},{6,5},{7,6},{8,11},{9,8},{10,9... | collective-permute-start | bytes 589832 | tf_op jit(solution)/shard_map/ppermute | solution.py:29
  6.7 7.6 %collective-permute-start.2 = (bf16[2,192,256]{2,1,0:T(8,128)(2,1)S(1)}, bf16[2,192,256]{2,1,0:T(8,128)(2,1)S(1)}, u32[]{:S(2)}, u32[]{:S(2)}) collective-permute-start(bf16[2,192,256]{2,1,0:T(8,128)(2,1)S(1)} %bitcast.6), channel_id=1, source_target_pairs={{0,8},{4,20},{8,0},{12,28},{16,24},{20,4},{24,16},{28,12},{1,9},{5... | collective-permute-start | bytes 589832 | tf_op jit(solution)/shard_map/ppermute | solution.py:24
  9.7 11.7 %collective-permute-start.4 = (bf16[400,256]{1,0:T(8,128)(2,1)S(1)}, bf16[400,256]{1,0:T(8,128)(2,1)S(1)}, u32[]{:S(2)}, u32[]{:S(2)}) collective-permute-start(bf16[400,256]{1,0:T(8,128)(2,1)S(1)} %hold.1), channel_id=1, source_target_pairs={{0,2},{1,3},{2,0},{3,1},{4,6},{5,7},{6,4},{7,5},{8,10},{9,11},{10,... | collective-permute-start | bytes 614408 | tf_op jit(solution)/shard_map/ppermute | solution.py:29
  14.4 9.8 %collective-permute-start.3 = (bf16[2,192,256]{2,1,0:T(8,128)(2,1)S(1)}, bf16[2,192,256]{2,1,0:T(8,128)(2,1)S(1)}, u32[]{:S(2)}, u32[]{:S(2)}) collective-permute-start(bf16[2,192,256]{2,1,0:T(8,128)(2,1)S(1)} %get-tuple-element.62), channel_id=1, source_target_pairs={{0,16},{4,12},{8,24},{12,4},{16,0},{20,28},{24,8},{28,20},{1,17},{... | collective-permute-start | bytes 589832 | tf_op jit(solution)/shard_map/ppermute | solution.py:24
  15.5 8.7 %collective-permute-start.5 = (bf16[2,192,256]{2,1,0:T(8,128)(2,1)S(1)}, bf16[2,192,256]{2,1,0:T(8,128)(2,1)S(1)}, u32[]{:S(2)}, u32[]{:S(2)}) collective-permute-start(bf16[2,192,256]{2,1,0:T(8,128)(2,1)S(1)} %get-tuple-element.60.refs_2_.refs_1_), channel_id=1, source_target_pairs={{0,8},{4,20},{8,0},{12,28},{16,24},{20,4},{24,16},{28,12},{1,9},{5... | collective-permute-start | bytes 589832 | tf_op jit(solution)/shard_map/ppermute | solution.py:24
  24.5 9.9 %collective-permute-start.10 = (bf16[3,192,256]{2,1,0:T(8,128)(2,1)S(1)}, bf16[3,192,256]{2,1,0:T(8,128)(2,1)S(1)}, u32[]{:S(2)}, u32[]{:S(2)}) collective-permute-start(bf16[3,192,256]{2,1,0:T(8,128)(2,1)S(1)} %get-tuple-element.71), channel_id=1, source_target_pairs={{0,16},{4,12},{8,24},{12,4},{16,0},{20,28},{24,8},{28,20},{1,17},{... | collective-permute-start | bytes 884744 | tf_op jit(solution)/shard_map/ppermute | solution.py:24
  25.0 9.3 %collective-permute-start.12 = (bf16[3,192,256]{2,1,0:T(8,128)(2,1)S(1)}, bf16[3,192,256]{2,1,0:T(8,128)(2,1)S(1)}, u32[]{:S(2)}, u32[]{:S(2)}) collective-permute-start(bf16[3,192,256]{2,1,0:T(8,128)(2,1)S(1)} %get-tuple-element.73), channel_id=1, source_target_pairs={{0,8},{4,20},{8,0},{12,28},{16,24},{20,4},{24,16},{28,12},{1,9},{5... | collective-permute-start | bytes 884744 | tf_op jit(solution)/shard_map/ppermute | solution.py:24
  25.5 8.5 %collective-permute-start.11 = (bf16[384,256]{1,0:T(8,128)(2,1)S(1)}, bf16[384,256]{1,0:T(8,128)(2,1)S(1)}, u32[]{:S(2)}, u32[]{:S(2)}) collective-permute-start(bf16[384,256]{1,0:T(8,128)(2,1)S(1)} %get-tuple-element.72), channel_id=1, source_target_pairs={{0,1},{1,2},{2,3},{3,0},{4,5},{5,6},{6,7},{7,4},{8,9},{9,10},{10,1... | collective-permute-start | bytes 589832 | tf_op jit(solution)/shard_map/ppermute | solution.py:29
  34.6 9.6 %collective-permute-start.13 = (bf16[3,192,256]{2,1,0:T(8,128)(2,1)S(1)}, bf16[3,192,256]{2,1,0:T(8,128)(2,1)S(1)}, u32[]{:S(2)}, u32[]{:S(2)}) collective-permute-start(bf16[3,192,256]{2,1,0:T(8,128)(2,1)S(1)} %get-tuple-element.74), channel_id=1, source_target_pairs={{0,16},{4,12},{8,24},{12,4},{16,0},{20,28},{24,8},{28,20},{1,17},{... | collective-permute-start | bytes 884744 | tf_op jit(solution)/shard_map/ppermute | solution.py:24
  36.0 8.2 %collective-permute-start.17 = (bf16[3,192,256]{2,1,0:T(8,128)(2,1)S(1)}, bf16[3,192,256]{2,1,0:T(8,128)(2,1)S(1)}, u32[]{:S(2)}, u32[]{:S(2)}) collective-permute-start(bf16[3,192,256]{2,1,0:T(8,128)(2,1)S(1)} %get-tuple-element.79), channel_id=1, source_target_pairs={{0,8},{4,20},{8,0},{12,28},{16,24},{20,4},{24,16},{28,12},{1,9},{5... | collective-permute-start | bytes 884744 | tf_op jit(solution)/shard_map/ppermute | solution.py:24
  44.7 10.0 %collective-permute-start.23 = (bf16[3,384,256]{2,1,0:T(8,128)(2,1)S(1)}, bf16[3,384,256]{2,1,0:T(8,128)(2,1)S(1)}, u32[]{:S(2)}, u32[]{:S(2)}) collective-permute-start(bf16[3,384,256]{2,1,0:T(8,128)(2,1)S(1)} %get-tuple-element.86), channel_id=1, source_target_pairs={{0,4},{4,0},{8,12},{12,8},{16,20},{20,16},{24,28},{28,24},{1,5},{5... | collective-permute-start | bytes 1769480 | tf_op jit(solution)/shard_map/ppermute | solution.py:20
  45.1 9.6 %collective-permute-start.18 = (bf16[3,192,256]{2,1,0:T(8,128)(2,1)S(1)}, bf16[3,192,256]{2,1,0:T(8,128)(2,1)S(1)}, u32[]{:S(2)}, u32[]{:S(2)}) collective-permute-start(bf16[3,192,256]{2,1,0:T(8,128)(2,1)S(1)} %get-tuple-element.80), channel_id=1, source_target_pairs={{0,16},{4,12},{8,24},{12,4},{16,0},{20,28},{24,8},{28,20},{1,17},{... | collective-permute-start | bytes 884744 | tf_op jit(solution)/shard_map/ppermute | solution.py:24
  46.5 8.2 %collective-permute-start.19 = (bf16[3,192,256]{2,1,0:T(8,128)(2,1)S(1)}, bf16[3,192,256]{2,1,0:T(8,128)(2,1)S(1)}, u32[]{:S(2)}, u32[]{:S(2)}) collective-permute-start(bf16[3,192,256]{2,1,0:T(8,128)(2,1)S(1)} %get-tuple-element.81), channel_id=1, source_target_pairs={{0,8},{4,20},{8,0},{12,28},{16,24},{20,4},{24,16},{28,12},{1,9},{5... | collective-permute-start | bytes 884744 | tf_op jit(solution)/shard_map/ppermute | solution.py:24
  55.1 11.7 %collective-permute-start.9 = (bf16[3,384,256]{2,1,0:T(8,128)(2,1)S(1)}, bf16[3,384,256]{2,1,0:T(8,128)(2,1)S(1)}, u32[]{:S(2)}, u32[]{:S(2)}) collective-permute-start(bf16[3,384,256]{2,1,0:T(8,128)(2,1)S(1)} %get-tuple-element.70), channel_id=1, source_target_pairs={{0,4},{4,0},{8,12},{12,8},{16,20},{20,16},{24,28},{28,24},{1,5},{5... | collective-permute-start | bytes 1769480 | tf_op jit(solution)/shard_map/ppermute | solution.py:20
  55.5 8.0 %collective-permute-start.26 = (bf16[384,256]{1,0:T(8,128)(2,1)S(1)}, bf16[384,256]{1,0:T(8,128)(2,1)S(1)}, u32[]{:S(2)}, u32[]{:S(2)}) collective-permute-start(bf16[384,256]{1,0:T(8,128)(2,1)S(1)} %get-tuple-element.90), channel_id=1, source_target_pairs={{0,4},{4,0},{8,12},{12,8},{16,20},{20,16},{24,28},{28,24},{1,5},{5... | collective-permute-start | bytes 589832 | tf_op jit(solution)/shard_map/ppermute | solution.py:20
  55.6 8.9 %collective-permute-start.27 = (bf16[3,192,256]{2,1,0:T(8,128)(2,1)S(1)}, bf16[3,192,256]{2,1,0:T(8,128)(2,1)S(1)}, u32[]{:S(2)}, u32[]{:S(2)}) collective-permute-start(bf16[3,192,256]{2,1,0:T(8,128)(2,1)S(1)} %get-tuple-element.91), channel_id=1, source_target_pairs={{0,16},{4,12},{8,24},{12,4},{16,0},{20,28},{24,8},{28,20},{1,17},{... | collective-permute-start | bytes 884744 | tf_op jit(solution)/shard_map/ppermute | solution.py:24
  57.3 7.6 %collective-permute-start.29 = (bf16[3,192,256]{2,1,0:T(8,128)(2,1)S(1)}, bf16[3,192,256]{2,1,0:T(8,128)(2,1)S(1)}, u32[]{:S(2)}, u32[]{:S(2)}) collective-permute-start(bf16[3,192,256]{2,1,0:T(8,128)(2,1)S(1)} %get-tuple-element.93), channel_id=1, source_target_pairs={{0,8},{4,20},{8,0},{12,28},{16,24},{20,4},{24,16},{28,12},{1,9},{5... | collective-permute-start | bytes 884744 | tf_op jit(solution)/shard_map/ppermute | solution.py:24
  65.0 9.1 %collective-permute-start.21 = (bf16[384,256]{1,0:T(8,128)(2,1)S(1)}, bf16[384,256]{1,0:T(8,128)(2,1)S(1)}, u32[]{:S(2)}, u32[]{:S(2)}) collective-permute-start(bf16[384,256]{1,0:T(8,128)(2,1)S(1)} %get-tuple-element.84), channel_id=1, source_target_pairs={{0,4},{4,0},{8,12},{12,8},{16,20},{20,16},{24,28},{28,24},{1,5},{5... | collective-permute-start | bytes 589832 | tf_op jit(solution)/shard_map/ppermute | solution.py:20
  65.6 9.2 %collective-permute-start.30 = (bf16[2,192,256]{2,1,0:T(8,128)(2,1)S(1)}, bf16[2,192,256]{2,1,0:T(8,128)(2,1)S(1)}, u32[]{:S(2)}, u32[]{:S(2)}) collective-permute-start(bf16[2,192,256]{2,1,0:T(8,128)(2,1)S(1)} %get-tuple-element.94), channel_id=1, source_target_pairs={{0,8},{4,20},{8,0},{12,28},{16,24},{20,4},{24,16},{28,12},{1,9},{5... | collective-permute-start | bytes 589832 | tf_op jit(solution)/shard_map/ppermute | solution.py:24
  69.2 10.4 %collective-permute-start.40 = (bf16[400,256]{1,0:T(8,128)(2,1)S(1)}, bf16[400,256]{1,0:T(8,128)(2,1)S(1)}, u32[]{:S(2)}, u32[]{:S(2)}) collective-permute-start(bf16[400,256]{1,0:T(8,128)(2,1)S(1)} %get-tuple-element.105), channel_id=1, source_target_pairs={{0,1},{1,2},{2,3},{3,0},{4,5},{5,6},{6,7},{7,4},{8,9},{9,10},{10,1... | collective-permute-start | bytes 614408 | tf_op jit(solution)/shard_map/ppermute | solution.py:29
  74.1 8.5 %collective-permute-start.39 = (bf16[2,192,256]{2,1,0:T(8,128)(2,1)S(1)}, bf16[2,192,256]{2,1,0:T(8,128)(2,1)S(1)}, u32[]{:S(2)}, u32[]{:S(2)}) collective-permute-start(bf16[2,192,256]{2,1,0:T(8,128)(2,1)S(1)} %get-tuple-element.104), channel_id=1, source_target_pairs={{0,16},{4,12},{8,24},{12,4},{16,0},{20,28},{24,8},{28,20},{1,17},{... | collective-permute-start | bytes 589832 | tf_op jit(solution)/shard_map/ppermute | solution.py:24
  74.8 7.9 %collective-permute-start.38 = (bf16[2,192,256]{2,1,0:T(8,128)(2,1)S(1)}, bf16[2,192,256]{2,1,0:T(8,128)(2,1)S(1)}, u32[]{:S(2)}, u32[]{:S(2)}) collective-permute-start(bf16[2,192,256]{2,1,0:T(8,128)(2,1)S(1)} %get-tuple-element.100.refs_8_), channel_id=1, source_target_pairs={{0,8},{4,20},{8,0},{12,28},{16,24},{20,4},{24,16},{28,12},{1,9},{5... | collective-permute-start | bytes 589832 | tf_op jit(solution)/shard_map/ppermute | solution.py:24
  78.7 9.4 %collective-permute-start.36 = (bf16[400,256]{1,0:T(8,128)(2,1)S(1)}, bf16[400,256]{1,0:T(8,128)(2,1)S(1)}, u32[]{:S(2)}, u32[]{:S(2)}) collective-permute-start(bf16[400,256]{1,0:T(8,128)(2,1)S(1)} %get-tuple-element.101), channel_id=1, source_target_pairs={{0,2},{1,3},{2,0},{3,1},{4,6},{5,7},{6,4},{7,5},{8,10},{9,11},{10,... | collective-permute-start | bytes 614408 | tf_op jit(solution)/shard_map/ppermute | solution.py:29
  82.8 8.5 %collective-permute-start.41 = (bf16[384,256]{1,0:T(8,128)(2,1)S(1)}, bf16[384,256]{1,0:T(8,128)(2,1)S(1)}, u32[]{:S(2)}, u32[]{:S(2)}) collective-permute-start(bf16[384,256]{1,0:T(8,128)(2,1)S(1)} %hub_j.1), channel_id=1, source_target_pairs={{0,3},{1,0},{2,1},{3,2},{4,7},{5,4},{6,5},{7,6},{8,11},{9,8},{10,9... | collective-permute-start | bytes 589832 | tf_op jit(solution)/shard_map/ppermute | solution.py:29
  (22 other events, 103.9 us)

commit v6 on v5

--- a/solution.py
+++ b/solution.py
@@ -304,19 +304,19 @@
 
     own = pieces[0].reshape(2, half, width)
     land([("piece", 0, 0, 0, 2)], over_links(own, X, Y), over_links(own, Y, X))
-    matrices = load(weights[:2], (outgoing[0],))
+    matrices = load(weights[:1], (outgoing[0],))
     held = call(hold_kernel, "hold", [(capacity + PAD, width)], [outgoing[ORDER[2]]])[0]
     pieces[2] = over_expert(held, ORDER[2])
     made, _ = phase("hub_b", [("piece", 1)], [("relay", 0)], deps=(matrices[0],))
-    matrices += load(weights[2:], (made,))
-    mix = [mixing(routes, scores, count, capacity, (made,))[j] for j in ORDER]
-    phase("hub_c", [("relay", 1), ("piece", 2)], ready=0, deps=(mix[0], matrices[2]))
+    matrices += load(weights[1:], (made,))
+    phase("hub_c", [("relay", 1), ("piece", 2)], ready=0, deps=(matrices[2],))
     phase("hub_d", [("relay", 2), ("piece", 3)], ready=1, deps=(keep[0],))
     phase("hub_e", [("relay", 3), ("diagonal", 1), ("diagonal", 0)], ready=2)
     phase("hub_f", [("diagonal", 2), ("near", 1)], ready=3)
     phase("hub_g", [("diagonal", 3)], [("near", 2)], results=(1,))
     made, _ = phase("hub_h", [("near", 3)])
-    phase("hub_i", [("near", 0)], results=(2,), deps=(made,))
+    mix = [mixing(routes, scores, count, capacity, (made,))[j] for j in ORDER]
+    phase("hub_i", [("near", 0)], results=(2,), deps=(mix[0],))
     phase("hub_j", results=(3,), deps=(back[1],))
     phase("hub_k", results=(0,))
     shape = (routes.shape[0], width)

time: 92.6 us -> 92.5 us (level)
  transfers between devices with their start and end apart: 44 -> 44, of which waited for: 18 -> 19; matrix products, arithmetic and copies ran while one was open for 0% -> 0% of each run, Pallas kernels for 30% -> 30%
where the time goes in v6:
time: 92.5 us; the launch traced here: 92.3 us
  starting transfers between devices  34.9 us (38%)
  Pallas kernels  31.5 us (34%)
  waiting for transfers between devices  25.6 us (28%)
    pallas_call x21, Pallas kernels, call(): pl.pallas_call(ordered(body, len(operands), len(deps)), out_shape=[jax.Sh...  31.5 us
    ppermute x22, starting transfers between devices, over_links(): lax.ppermute(value, 'dp', [(i, i ^ (odd if i & 1 else even)) for i in ran...  25.8 us
    ppermute x22, waiting for transfers between devices, over_links(): lax.ppermute(value, 'dp', [(i, i ^ (odd if i & 1 else even)) for i in ran...  17.8 us
    ppermute x6, waiting for transfers between devices, over_expert(): lax.ppermute(value, 'expert', [(i, (i + shift) % count) for i in range(co...  6.43 us
    ppermute x6, starting transfers between devices, over_expert(): lax.ppermute(value, 'expert', [(i, (i + shift) % count) for i in range(co...  5.91 us
    ppermute x16, starting transfers between devices, over_core(): lax.ppermute(value, 'dp', [(i, i ^ CORE) for i in range(lax.axis_size('dp...  3.2 us
  transfers between devices with their start and end apart: 44, of which 19 were waited for; matrix products, arithmetic and copies ran while one was open for 0% of the time, Pallas kernels for 30%

profile of v6, /device:TPU:0, one launch (start us, length us, event | category | flops | bytes accessed | tf_op | source)
XLA Modules:
  0.0 92.3 jit_solution(3705787198701953969)
XLA Ops:
  0.0 1.6 %dispatch.1 = (bf16[384,256]{1,0:T(8,128)(2,1)S(1)}, bf16[384,256]{1,0:T(8,128)(2,1)S(1)}, bf16[384,256]{1,0:T(8,128)(2,1)S(1)}, bf16[384,256]{1,0:T(8,128)(2,1)S(1)}) custom-call(s32[2,512]{1,0:T(2,128)} %bitcast.8, bf16[512,256]{1,0:T(8,128)(2,1)} %refs_1_.1), custom_call_target="tpu_custom_call" | custom-call | tf_op jit(solution)/shard_map/dispatch/pallas_call | solution.py:40
  1.6 5.1 %collective-permute-start = (bf16[384,256]{1,0:T(8,128)(2,1)S(1)}, bf16[384,256]{1,0:T(8,128)(2,1)S(1)}, u32[]{:S(2)}, u32[]{:S(2)}) collective-permute-start(bf16[384,256]{1,0:T(8,128)(2,1)S(1)} %get-tuple-element.57), channel_id=1, source_target_pairs={{0,3},{1,0},{2,1},{3,2},{4,7},{5,4},{6,5},{7,6},{8,11},{9,8},{10,9... | collective-permute-start | bytes 589832 | tf_op jit(solution)/shard_map/ppermute | solution.py:29
  6.7 1.5 %collective-permute-start.2 = (bf16[2,192,256]{2,1,0:T(8,128)(2,1)S(1)}, bf16[2,192,256]{2,1,0:T(8,128)(2,1)S(1)}, u32[]{:S(2)}, u32[]{:S(2)}) collective-permute-start(bf16[2,192,256]{2,1,0:T(8,128)(2,1)S(1)} %bitcast.6), channel_id=1, source_target_pairs={{0,8},{4,20},{8,0},{12,28},{16,24},{20,4},{24,16},{28,12},{1,9},{5... | collective-permute-start | bytes 589832 | tf_op jit(solution)/shard_map/ppermute | solution.py:24
  8.2 1.5 %collective-permute-start.1 = (bf16[2,192,256]{2,1,0:T(8,128)(2,1)S(1)}, bf16[2,192,256]{2,1,0:T(8,128)(2,1)S(1)}, u32[]{:S(2)}, u32[]{:S(2)}) collective-permute-start(bf16[2,192,256]{2,1,0:T(8,128)(2,1)S(1)} %bitcast.7), channel_id=1, source_target_pairs={{0,16},{4,12},{8,24},{12,4},{16,0},{20,28},{24,8},{28,20},{1,17},{... | collective-permute-start | bytes 589832 | tf_op jit(solution)/shard_map/ppermute | solution.py:24
  9.8 2.2 %load.2.refs_3_.refs_2_ = bf16[2048,1024]{1,0:T(8,128)(2,1)S(1)} custom-call(bf16[2048,1024]{1,0:T(8,128)(2,1)} %bitcast.11, bf16[384,256]{1,0:T(8,128)(2,1)S(1)} %get-tuple-element.58.refs_1_.refs_3_), custom_call_target="tpu_custom_call" | custom-call | tf_op jit(solution)/shard_map/load/pallas_call | solution.py:40
  12.1 2.2 %collective-permute-done.2.refs_2_.refs_4_ = bf16[2,192,256]{2,1,0:T(8,128)(2,1)S(1)} collective-permute-done((bf16[2,192,256]{2,1,0:T(8,128)(2,1)S(1)}, bf16[2,192,256]{2,1,0:T(8,128)(2,1)S(1)}, u32[]{:S(2)}, u32[]{:S(2)}) %collective-permute-start.2) | collective-permute-done | bytes 196640 | tf_op jit(solution)/shard_map/ppermute | solution.py:24
  18.5 3.5 %load.3 = (bf16[2048,1024]{1,0:T(8,128)(2,1)S(1)}, bf16[1024,2048]{1,0:T(8,128)(2,1)S(1)}) custom-call(bf16[2048,1024]{1,0:T(8,128)(2,1)} %bitcast.12, bf16[1024,2048]{1,0:T(8,128)(2,1)} %bitcast.13, bf16[2,192,256]{2,1,0:T(8,128)(2,1)S(1)} %get-tuple-element.61.refs_2_), custom_call_target="tpu_custom_call" | custom-call | tf_op jit(solution)/shard_map/load/pallas_call | solution.py:40
  26.6 5.1 %expert.4 = (bf16[4,384,256]{2,1,0:T(8,128)(2,1)S(1)}, bf16[384,256]{1,0:T(8,128)(2,1)S(1)}, bf16[3,384,256]{2,1,0:T(8,128)(2,1)S(1)}) custom-call(bf16[4,384,256]{2,1,0:T(8,128)(2,1)S(1)} %get-tuple-element.68.refs_0_, bf16[4,384,256]{2,1,0:T(8,128)(2,1)S(1)} %collective-permute-done.11.refs_1_, bf16[2048,1024]{1,0:T(8,128)(2,1)S(1)} %load.2.refs_3_.refs_2_, ...), custom_call_target="tpu_custom_call" | custom-call | tf_op jit(solution)/shard_map/expert/pallas_call | solution.py:40
  31.7 2.3 %collective-permute-done.9.refs_1_.refs_6_ = bf16[384,256]{1,0:T(8,128)(2,1)S(1)} collective-permute-done((bf16[384,256]{1,0:T(8,128)(2,1)S(1)}, bf16[384,256]{1,0:T(8,128)(2,1)S(1)}, u32[]{:S(2)}, u32[]{:S(2)}) %collective-permute-start.9) | collective-permute-done | bytes 196640 | tf_op jit(solution)/shard_map/ppermute | solution.py:29
  34.6 1.4 %collective-permute-start.12 = (bf16[3,192,256]{2,1,0:T(8,128)(2,1)S(1)}, bf16[3,192,256]{2,1,0:T(8,128)(2,1)S(1)}, u32[]{:S(2)}, u32[]{:S(2)}) collective-permute-start(bf16[3,192,256]{2,1,0:T(8,128)(2,1)S(1)} %get-tuple-element.71), channel_id=1, source_target_pairs={{0,16},{4,12},{8,24},{12,4},{16,0},{20,28},{24,8},{28,20},{1,17},{... | collective-permute-start | bytes 884744 | tf_op jit(solution)/shard_map/ppermute | solution.py:24
  37.2 5.1 %expert.5 = (bf16[4,384,256]{2,1,0:T(8,128)(2,1)S(1)}, bf16[384,256]{1,0:T(8,128)(2,1)S(1)}, bf16[3,384,256]{2,1,0:T(8,128)(2,1)S(1)}) custom-call(bf16[4,384,256]{2,1,0:T(8,128)(2,1)S(1)} %get-tuple-element.72.refs_0_, bf16[4,384,256]{2,1,0:T(8,128)(2,1)S(1)} %collective-permute-done.13.refs_1_, bf16[2048,1024]{1,0:T(8,128)(2,1)S(1)} %load.2.refs_3_.refs_2_, ...), custom_call_target="tpu_custom_call" | custom-call | tf_op jit(solution)/shard_map/expert/pallas_call | solution.py:40
  45.1 1.4 %collective-permute-start.20 = (bf16[3,192,256]{2,1,0:T(8,128)(2,1)S(1)}, bf16[3,192,256]{2,1,0:T(8,128)(2,1)S(1)}, u32[]{:S(2)}, u32[]{:S(2)}) collective-permute-start(bf16[3,192,256]{2,1,0:T(8,128)(2,1)S(1)} %get-tuple-element.81), channel_id=1, source_target_pairs={{0,16},{4,12},{8,24},{12,4},{16,0},{20,28},{24,8},{28,20},{1,17},{... | collective-permute-start | bytes 884744 | tf_op jit(solution)/shard_map/ppermute | solution.py:24
  46.5 1.4 %collective-permute-start.21 = (bf16[3,192,256]{2,1,0:T(8,128)(2,1)S(1)}, bf16[3,192,256]{2,1,0:T(8,128)(2,1)S(1)}, u32[]{:S(2)}, u32[]{:S(2)}) collective-permute-start(bf16[3,192,256]{2,1,0:T(8,128)(2,1)S(1)} %get-tuple-element.82), channel_id=1, source_target_pairs={{0,8},{4,20},{8,0},{12,28},{16,24},{20,4},{24,16},{28,12},{1,9},{5... | collective-permute-start | bytes 884744 | tf_op jit(solution)/shard_map/ppermute | solution.py:24
  47.9 5.2 %expert.6 = (bf16[4,384,256]{2,1,0:T(8,128)(2,1)S(1)}, bf16[384,256]{1,0:T(8,128)(2,1)S(1)}, bf16[384,256]{1,0:T(8,128)(2,1)S(1)}, bf16[384,256]{1,0:T(8,128)(2,1)S(1)}, bf16[384,256]{1,0:T(8,128)(2,1)S(1)}) custom-call(bf16[4,384,256]{2,1,0:T(8,128)(2,1)S(1)} %get-tuple-element.77.refs_0_, bf16[4,384,256]{2,1,0:T(8,128)(2,1)S(1)} %collective-permute-done.17.refs_1_, ...), custom_call_target="tpu_custom_call" | custom-call | tf_op jit(solution)/shard_map/expert/pallas_call | solution.py:40
  53.2 1.5 %collective-permute-done.20.refs_4_.refs_2_ = bf16[3,192,256]{2,1,0:T(8,128)(2,1)S(1)} collective-permute-done((bf16[3,192,256]{2,1,0:T(8,128)(2,1)S(1)}, bf16[3,192,256]{2,1,0:T(8,128)(2,1)S(1)}, u32[]{:S(2)}, u32[]{:S(2)}) %collective-permute-start.20) | collective-permute-done | bytes 294944 | tf_op jit(solution)/shard_map/ppermute | solution.py:24
  55.6 1.4 %collective-permute-start.26 = (bf16[3,192,256]{2,1,0:T(8,128)(2,1)S(1)}, bf16[3,192,256]{2,1,0:T(8,128)(2,1)S(1)}, u32[]{:S(2)}, u32[]{:S(2)}) collective-permute-start(bf16[3,192,256]{2,1,0:T(8,128)(2,1)S(1)} %get-tuple-element.88), channel_id=1, source_target_pairs={{0,16},{4,12},{8,24},{12,4},{16,0},{20,28},{24,8},{28,20},{1,17},{... | collective-permute-start | bytes 884744 | tf_op jit(solution)/shard_map/ppermute | solution.py:24
  58.5 5.1 %expert.7 = (bf16[4,384,256]{2,1,0:T(8,128)(2,1)S(1)}, bf16[384,256]{1,0:T(8,128)(2,1)S(1)}, bf16[384,256]{1,0:T(8,128)(2,1)S(1)}, bf16[384,256]{1,0:T(8,128)(2,1)S(1)}, bf16[384,256]{1,0:T(8,128)(2,1)S(1)}) custom-call(bf16[4,384,256]{2,1,0:T(8,128)(2,1)S(1)} %get-tuple-element.83.refs_0_, bf16[4,384,256]{2,1,0:T(8,128)(2,1)S(1)} %collective-permute-done.22.refs_1_, ...), custom_call_target="tpu_custom_call" | custom-call | tf_op jit(solution)/shard_map/expert/pallas_call | solution.py:40
  66.8 1.4 %collective-permute-start.29 = (bf16[1,192,256]{2,1,0:T(8,128)(2,1)S(1)}, bf16[1,192,256]{2,1,0:T(8,128)(2,1)S(1)}, u32[]{:S(2)}, u32[]{:S(2)}) collective-permute-start(bf16[1,192,256]{2,1,0:T(8,128)(2,1)S(1)} %get-tuple-element.91), channel_id=1, source_target_pairs={{0,16},{4,12},{8,24},{12,4},{16,0},{20,28},{24,8},{28,20},{1,17},{... | collective-permute-start | bytes 294920 | tf_op jit(solution)/shard_map/ppermute | solution.py:24
  69.2 3.4 %collective-permute-done.29.refs_2_ = bf16[1,192,256]{2,1,0:T(8,128)(2,1)S(1)} collective-permute-done((bf16[1,192,256]{2,1,0:T(8,128)(2,1)S(1)}, bf16[1,192,256]{2,1,0:T(8,128)(2,1)S(1)}, u32[]{:S(2)}, u32[]{:S(2)}) %collective-permute-start.29) | collective-permute-done | bytes 98336 | tf_op jit(solution)/shard_map/ppermute | solution.py:24
  72.5 1.4 %collective-permute-start.35 = (bf16[2,192,256]{2,1,0:T(8,128)(2,1)S(1)}, bf16[2,192,256]{2,1,0:T(8,128)(2,1)S(1)}, u32[]{:S(2)}, u32[]{:S(2)}) collective-permute-start(bf16[2,192,256]{2,1,0:T(8,128)(2,1)S(1)} %get-tuple-element.99), channel_id=1, source_target_pairs={{0,16},{4,12},{8,24},{12,4},{16,0},{20,28},{24,8},{28,20},{1,17},{... | collective-permute-start | bytes 589832 | tf_op jit(solution)/shard_map/ppermute | solution.py:24
  76.5 2.0 %collective-permute-done.35.refs_7_ = bf16[2,192,256]{2,1,0:T(8,128)(2,1)S(1)} collective-permute-done((bf16[2,192,256]{2,1,0:T(8,128)(2,1)S(1)}, bf16[2,192,256]{2,1,0:T(8,128)(2,1)S(1)}, u32[]{:S(2)}, u32[]{:S(2)}) %collective-permute-start.35) | collective-permute-done | bytes 196640 | tf_op jit(solution)/shard_map/ppermute | solution.py:24
  79.5 2.3 %collective-permute-start.43 = (bf16[2,192,256]{2,1,0:T(8,128)(2,1)S(1)}, bf16[2,192,256]{2,1,0:T(8,128)(2,1)S(1)}, u32[]{:S(2)}, u32[]{:S(2)}) collective-permute-start(bf16[2,192,256]{2,1,0:T(8,128)(2,1)S(1)} %get-tuple-element.107), channel_id=1, source_target_pairs={{0,16},{4,12},{8,24},{12,4},{16,0},{20,28},{24,8},{28,20},{1,17},{... | collective-permute-start | bytes 589832 | tf_op jit(solution)/shard_map/ppermute | solution.py:24
  83.4 2.3 %collective-permute-done.42.refs_2_ = bf16[2,192,256]{2,1,0:T(8,128)(2,1)S(1)} collective-permute-done((bf16[2,192,256]{2,1,0:T(8,128)(2,1)S(1)}, bf16[2,192,256]{2,1,0:T(8,128)(2,1)S(1)}, u32[]{:S(2)}, u32[]{:S(2)}) %collective-permute-start.42) | collective-permute-done | bytes 196640 | tf_op jit(solution)/shard_map/ppermute | solution.py:24
  87.7 3.5 %collective-permute-done.41.refs_3_ = bf16[384,256]{1,0:T(8,128)(2,1)S(1)} collective-permute-done((bf16[384,256]{1,0:T(8,128)(2,1)S(1)}, bf16[384,256]{1,0:T(8,128)(2,1)S(1)}, u32[]{:S(2)}, u32[]{:S(2)}) %collective-permute-start.41) | collective-permute-done | bytes 196640 | tf_op jit(solution)/shard_map/ppermute | solution.py:29
  (89 shorter events, 28.2 us)
Async XLA Ops:
  1.6 10.5 %collective-permute-start = (bf16[384,256]{1,0:T(8,128)(2,1)S(1)}, bf16[384,256]{1,0:T(8,128)(2,1)S(1)}, u32[]{:S(2)}, u32[]{:S(2)}) collective-permute-start(bf16[384,256]{1,0:T(8,128)(2,1)S(1)} %get-tuple-element.57), channel_id=1, source_target_pairs={{0,3},{1,0},{2,1},{3,2},{4,7},{5,4},{6,5},{7,6},{8,11},{9,8},{10,9... | collective-permute-start | bytes 589832 | tf_op jit(solution)/shard_map/ppermute | solution.py:29
  6.7 7.6 %collective-permute-start.2 = (bf16[2,192,256]{2,1,0:T(8,128)(2,1)S(1)}, bf16[2,192,256]{2,1,0:T(8,128)(2,1)S(1)}, u32[]{:S(2)}, u32[]{:S(2)}) collective-permute-start(bf16[2,192,256]{2,1,0:T(8,128)(2,1)S(1)} %bitcast.6), channel_id=1, source_target_pairs={{0,8},{4,20},{8,0},{12,28},{16,24},{20,4},{24,16},{28,12},{1,9},{5... | collective-permute-start | bytes 589832 | tf_op jit(solution)/shard_map/ppermute | solution.py:24
  9.7 12.3 %collective-permute-start.4 = (bf16[400,256]{1,0:T(8,128)(2,1)S(1)}, bf16[400,256]{1,0:T(8,128)(2,1)S(1)}, u32[]{:S(2)}, u32[]{:S(2)}) collective-permute-start(bf16[400,256]{1,0:T(8,128)(2,1)S(1)} %hold.1), channel_id=1, source_target_pairs={{0,2},{1,3},{2,0},{3,1},{4,6},{5,7},{6,4},{7,5},{8,10},{9,11},{10,... | collective-permute-start | bytes 614408 | tf_op jit(solution)/shard_map/ppermute | solution.py:29
  14.4 9.8 %collective-permute-start.3 = (bf16[2,192,256]{2,1,0:T(8,128)(2,1)S(1)}, bf16[2,192,256]{2,1,0:T(8,128)(2,1)S(1)}, u32[]{:S(2)}, u32[]{:S(2)}) collective-permute-start(bf16[2,192,256]{2,1,0:T(8,128)(2,1)S(1)} %get-tuple-element.59), channel_id=1, source_target_pairs={{0,16},{4,12},{8,24},{12,4},{16,0},{20,28},{24,8},{28,20},{1,17},{... | collective-permute-start | bytes 589832 | tf_op jit(solution)/shard_map/ppermute | solution.py:24
  15.5 8.7 %collective-permute-start.5 = (bf16[2,192,256]{2,1,0:T(8,128)(2,1)S(1)}, bf16[2,192,256]{2,1,0:T(8,128)(2,1)S(1)}, u32[]{:S(2)}, u32[]{:S(2)}) collective-permute-start(bf16[2,192,256]{2,1,0:T(8,128)(2,1)S(1)} %get-tuple-element.61.refs_2_), channel_id=1, source_target_pairs={{0,8},{4,20},{8,0},{12,28},{16,24},{20,4},{24,16},{28,12},{1,9},{5... | collective-permute-start | bytes 589832 | tf_op jit(solution)/shard_map/ppermute | solution.py:24
  24.5 9.9 %collective-permute-start.8 = (bf16[3,192,256]{2,1,0:T(8,128)(2,1)S(1)}, bf16[3,192,256]{2,1,0:T(8,128)(2,1)S(1)}, u32[]{:S(2)}, u32[]{:S(2)}) collective-permute-start(bf16[3,192,256]{2,1,0:T(8,128)(2,1)S(1)} %get-tuple-element.65), channel_id=1, source_target_pairs={{0,16},{4,12},{8,24},{12,4},{16,0},{20,28},{24,8},{28,20},{1,17},{... | collective-permute-start | bytes 884744 | tf_op jit(solution)/shard_map/ppermute | solution.py:24
  25.0 9.3 %collective-permute-start.10 = (bf16[3,192,256]{2,1,0:T(8,128)(2,1)S(1)}, bf16[3,192,256]{2,1,0:T(8,128)(2,1)S(1)}, u32[]{:S(2)}, u32[]{:S(2)}) collective-permute-start(bf16[3,192,256]{2,1,0:T(8,128)(2,1)S(1)} %get-tuple-element.67), channel_id=1, source_target_pairs={{0,8},{4,20},{8,0},{12,28},{16,24},{20,4},{24,16},{28,12},{1,9},{5... | collective-permute-start | bytes 884744 | tf_op jit(solution)/shard_map/ppermute | solution.py:24
  25.5 8.5 %collective-permute-start.9 = (bf16[384,256]{1,0:T(8,128)(2,1)S(1)}, bf16[384,256]{1,0:T(8,128)(2,1)S(1)}, u32[]{:S(2)}, u32[]{:S(2)}) collective-permute-start(bf16[384,256]{1,0:T(8,128)(2,1)S(1)} %get-tuple-element.66), channel_id=1, source_target_pairs={{0,1},{1,2},{2,3},{3,0},{4,5},{5,6},{6,7},{7,4},{8,9},{9,10},{10,1... | collective-permute-start | bytes 589832 | tf_op jit(solution)/shard_map/ppermute | solution.py:29
  34.6 9.6 %collective-permute-start.12 = (bf16[3,192,256]{2,1,0:T(8,128)(2,1)S(1)}, bf16[3,192,256]{2,1,0:T(8,128)(2,1)S(1)}, u32[]{:S(2)}, u32[]{:S(2)}) collective-permute-start(bf16[3,192,256]{2,1,0:T(8,128)(2,1)S(1)} %get-tuple-element.71), channel_id=1, source_target_pairs={{0,16},{4,12},{8,24},{12,4},{16,0},{20,28},{24,8},{28,20},{1,17},{... | collective-permute-start | bytes 884744 | tf_op jit(solution)/shard_map/ppermute | solution.py:24
  36.0 8.2 %collective-permute-start.16 = (bf16[3,192,256]{2,1,0:T(8,128)(2,1)S(1)}, bf16[3,192,256]{2,1,0:T(8,128)(2,1)S(1)}, u32[]{:S(2)}, u32[]{:S(2)}) collective-permute-start(bf16[3,192,256]{2,1,0:T(8,128)(2,1)S(1)} %get-tuple-element.76), channel_id=1, source_target_pairs={{0,8},{4,20},{8,0},{12,28},{16,24},{20,4},{24,16},{28,12},{1,9},{5... | collective-permute-start | bytes 884744 | tf_op jit(solution)/shard_map/ppermute | solution.py:24
  44.7 10.0 %collective-permute-start.19 = (bf16[3,384,256]{2,1,0:T(8,128)(2,1)S(1)}, bf16[3,384,256]{2,1,0:T(8,128)(2,1)S(1)}, u32[]{:S(2)}, u32[]{:S(2)}) collective-permute-start(bf16[3,384,256]{2,1,0:T(8,128)(2,1)S(1)} %get-tuple-element.80), channel_id=1, source_target_pairs={{0,4},{4,0},{8,12},{12,8},{16,20},{20,16},{24,28},{28,24},{1,5},{5... | collective-permute-start | bytes 1769480 | tf_op jit(solution)/shard_map/ppermute | solution.py:20
  45.1 9.6 %collective-permute-start.20 = (bf16[3,192,256]{2,1,0:T(8,128)(2,1)S(1)}, bf16[3,192,256]{2,1,0:T(8,128)(2,1)S(1)}, u32[]{:S(2)}, u32[]{:S(2)}) collective-permute-start(bf16[3,192,256]{2,1,0:T(8,128)(2,1)S(1)} %get-tuple-element.81), channel_id=1, source_target_pairs={{0,16},{4,12},{8,24},{12,4},{16,0},{20,28},{24,8},{28,20},{1,17},{... | collective-permute-start | bytes 884744 | tf_op jit(solution)/shard_map/ppermute | solution.py:24
  46.5 8.2 %collective-permute-start.21 = (bf16[3,192,256]{2,1,0:T(8,128)(2,1)S(1)}, bf16[3,192,256]{2,1,0:T(8,128)(2,1)S(1)}, u32[]{:S(2)}, u32[]{:S(2)}) collective-permute-start(bf16[3,192,256]{2,1,0:T(8,128)(2,1)S(1)} %get-tuple-element.82), channel_id=1, source_target_pairs={{0,8},{4,20},{8,0},{12,28},{16,24},{20,4},{24,16},{28,12},{1,9},{5... | collective-permute-start | bytes 884744 | tf_op jit(solution)/shard_map/ppermute | solution.py:24
  55.1 11.7 %collective-permute-start.32 = (bf16[3,384,256]{2,1,0:T(8,128)(2,1)S(1)}, bf16[3,384,256]{2,1,0:T(8,128)(2,1)S(1)}, u32[]{:S(2)}, u32[]{:S(2)}) collective-permute-start(bf16[3,384,256]{2,1,0:T(8,128)(2,1)S(1)} %get-tuple-element.96), channel_id=1, source_target_pairs={{0,4},{4,0},{8,12},{12,8},{16,20},{20,16},{24,28},{28,24},{1,5},{5... | collective-permute-start | bytes 1769480 | tf_op jit(solution)/shard_map/ppermute | solution.py:20
  55.5 8.0 %collective-permute-start.25 = (bf16[384,256]{1,0:T(8,128)(2,1)S(1)}, bf16[384,256]{1,0:T(8,128)(2,1)S(1)}, u32[]{:S(2)}, u32[]{:S(2)}) collective-permute-start(bf16[384,256]{1,0:T(8,128)(2,1)S(1)} %get-tuple-element.87), channel_id=1, source_target_pairs={{0,4},{4,0},{8,12},{12,8},{16,20},{20,16},{24,28},{28,24},{1,5},{5... | collective-permute-start | bytes 589832 | tf_op jit(solution)/shard_map/ppermute | solution.py:20
  55.6 8.9 %collective-permute-start.26 = (bf16[3,192,256]{2,1,0:T(8,128)(2,1)S(1)}, bf16[3,192,256]{2,1,0:T(8,128)(2,1)S(1)}, u32[]{:S(2)}, u32[]{:S(2)}) collective-permute-start(bf16[3,192,256]{2,1,0:T(8,128)(2,1)S(1)} %get-tuple-element.88), channel_id=1, source_target_pairs={{0,16},{4,12},{8,24},{12,4},{16,0},{20,28},{24,8},{28,20},{1,17},{... | collective-permute-start | bytes 884744 | tf_op jit(solution)/shard_map/ppermute | solution.py:24
  57.3 7.6 %collective-permute-start.28 = (bf16[3,192,256]{2,1,0:T(8,128)(2,1)S(1)}, bf16[3,192,256]{2,1,0:T(8,128)(2,1)S(1)}, u32[]{:S(2)}, u32[]{:S(2)}) collective-permute-start(bf16[3,192,256]{2,1,0:T(8,128)(2,1)S(1)} %get-tuple-element.90), channel_id=1, source_target_pairs={{0,8},{4,20},{8,0},{12,28},{16,24},{20,4},{24,16},{28,12},{1,9},{5... | collective-permute-start | bytes 884744 | tf_op jit(solution)/shard_map/ppermute | solution.py:24
  65.0 9.1 %collective-permute-start.33 = (bf16[384,256]{1,0:T(8,128)(2,1)S(1)}, bf16[384,256]{1,0:T(8,128)(2,1)S(1)}, u32[]{:S(2)}, u32[]{:S(2)}) collective-permute-start(bf16[384,256]{1,0:T(8,128)(2,1)S(1)} %get-tuple-element.97), channel_id=1, source_target_pairs={{0,4},{4,0},{8,12},{12,8},{16,20},{20,16},{24,28},{28,24},{1,5},{5... | collective-permute-start | bytes 589832 | tf_op jit(solution)/shard_map/ppermute | solution.py:20
  65.6 9.2 %collective-permute-start.34 = (bf16[2,192,256]{2,1,0:T(8,128)(2,1)S(1)}, bf16[2,192,256]{2,1,0:T(8,128)(2,1)S(1)}, u32[]{:S(2)}, u32[]{:S(2)}) collective-permute-start(bf16[2,192,256]{2,1,0:T(8,128)(2,1)S(1)} %get-tuple-element.98), channel_id=1, source_target_pairs={{0,8},{4,20},{8,0},{12,28},{16,24},{20,4},{24,16},{28,12},{1,9},{5... | collective-permute-start | bytes 589832 | tf_op jit(solution)/shard_map/ppermute | solution.py:24
  69.1 10.3 %collective-permute-start.40 = (bf16[400,256]{1,0:T(8,128)(2,1)S(1)}, bf16[400,256]{1,0:T(8,128)(2,1)S(1)}, u32[]{:S(2)}, u32[]{:S(2)}) collective-permute-start(bf16[400,256]{1,0:T(8,128)(2,1)S(1)} %get-tuple-element.105), channel_id=1, source_target_pairs={{0,1},{1,2},{2,3},{3,0},{4,5},{5,6},{6,7},{7,4},{8,9},{9,10},{10,1... | collective-permute-start | bytes 614408 | tf_op jit(solution)/shard_map/ppermute | solution.py:29
  74.1 8.5 %collective-permute-start.39 = (bf16[2,192,256]{2,1,0:T(8,128)(2,1)S(1)}, bf16[2,192,256]{2,1,0:T(8,128)(2,1)S(1)}, u32[]{:S(2)}, u32[]{:S(2)}) collective-permute-start(bf16[2,192,256]{2,1,0:T(8,128)(2,1)S(1)} %get-tuple-element.104), channel_id=1, source_target_pairs={{0,16},{4,12},{8,24},{12,4},{16,0},{20,28},{24,8},{28,20},{1,17},{... | collective-permute-start | bytes 589832 | tf_op jit(solution)/shard_map/ppermute | solution.py:24
  74.8 7.9 %collective-permute-start.38 = (bf16[2,192,256]{2,1,0:T(8,128)(2,1)S(1)}, bf16[2,192,256]{2,1,0:T(8,128)(2,1)S(1)}, u32[]{:S(2)}, u32[]{:S(2)}) collective-permute-start(bf16[2,192,256]{2,1,0:T(8,128)(2,1)S(1)} %get-tuple-element.94.refs_2_), channel_id=1, source_target_pairs={{0,8},{4,20},{8,0},{12,28},{16,24},{20,4},{24,16},{28,12},{1,9},{5... | collective-permute-start | bytes 589832 | tf_op jit(solution)/shard_map/ppermute | solution.py:24
  78.7 9.1 %collective-permute-start.36 = (bf16[400,256]{1,0:T(8,128)(2,1)S(1)}, bf16[400,256]{1,0:T(8,128)(2,1)S(1)}, u32[]{:S(2)}, u32[]{:S(2)}) collective-permute-start(bf16[400,256]{1,0:T(8,128)(2,1)S(1)} %get-tuple-element.101), channel_id=1, source_target_pairs={{0,2},{1,3},{2,0},{3,1},{4,6},{5,7},{6,4},{7,5},{8,10},{9,11},{10,... | collective-permute-start | bytes 614408 | tf_op jit(solution)/shard_map/ppermute | solution.py:29
  82.8 8.4 %collective-permute-start.41 = (bf16[384,256]{1,0:T(8,128)(2,1)S(1)}, bf16[384,256]{1,0:T(8,128)(2,1)S(1)}, u32[]{:S(2)}, u32[]{:S(2)}) collective-permute-start(bf16[384,256]{1,0:T(8,128)(2,1)S(1)} %hub_j.1), channel_id=1, source_target_pairs={{0,3},{1,0},{2,1},{3,2},{4,7},{5,4},{6,5},{7,6},{8,11},{9,8},{10,9... | collective-permute-start | bytes 589832 | tf_op jit(solution)/shard_map/ppermute | solution.py:29
  (22 other events, 117.8 us)
